TPU v7x, 32 devices: a whole 2x2x4 slice. The times are simulated.
32 devices in a mesh: groups: 2 (over y), feat: 4 (over z), rows: 2 (over x), sub: 2 (over core).
Axes of the slice: x: 2, y: 2, z: 4, core: 2. Of those that a mesh axis runs over, the one named last changes fastest.
Arguments:
- activations: bfloat16 [8192, 28672], P(('groups', 'rows', 'sub'), 'feat'), parts along dimension 0, may hold values from -6 to 6
- out_grads: bfloat16 [8192, 8192], P(('groups', 'rows', 'sub'), 'feat'), parts along dimension 0, may hold values from -6 to 6
- proj_in: bfloat16 [57344, 128], P(('groups', 'feat')), parts along dimension 0, may hold values from -0.03125 to 0.03125
- proj_out: bfloat16 [16384, 128], P(('groups', 'feat')), parts along dimension 0, may hold values from -0.0625 to 0.0625
- lengths: int32 [256], P('groups'), parts along dimension 0, may hold values from 1 to 64, 4096 in all
- corpus: bfloat16 [16384, 16384], P(('groups', 'rows', 'sub'), 'feat'), parts along dimension 0, may hold values from -200 to 200
- owner: int32 [8192], P(('rows', 'sub')), may hold values from 0 to 255, as said below
Outputs:
- influence: float32 [256, 16384], P(('groups', 'rows', 'sub'), 'feat'), parts along dimension 0
There are 2 independent parts, one for each index of `groups`. A program takes and returns all parts, laid end to end along the dimension named above; an argument that names none is the same for every part. Nothing has to cross between parts.
Inputs may be any that keep to these rules, and one draw needn't show every extreme that they name: `owner`: every draw holds at least two different labels, so each passage keeps some corpus rows.
All inputs are finite; a program needn't handle non-finite values.
Results may differ from a plain program's by a relative error of at most 0.007.
The roundings to bfloat16 on the way count: a program that leaves them out, or rounds other values in their place, can miss the bound.
Values may be sent and summed in bfloat16 or wider, within the bound.
No kernel may reach another device: no remote copies, remote signals or barrier semaphores. Data moves between devices by JAX's collectives and lax.ppermute only.
A program may use at most 128 MiB of HBM per device.

v0:
```python
import math

import jax
import jax.numpy as jnp
from jax import lax
from jax.sharding import PartitionSpec as P

K = 16384


def local(activations, out_grads, proj_in, proj_out, lengths, corpus, owner):
    tok_local = activations.shape[0]
    passages = lengths.shape[0]
    nfeat = lax.axis_size("feat")
    part_x = jnp.dot(activations, proj_in, preferred_element_type=jnp.float32)
    part_g = jnp.dot(out_grads, proj_out, preferred_element_type=jnp.float32)
    width_cols = part_g.shape[1] // nfeat
    summed_x = lax.psum(part_x, "feat")
    x_low = summed_x.astype(jnp.bfloat16)
    g_low = lax.psum_scatter(part_g, "feat", scatter_dimension=1, tiled=True).astype(jnp.bfloat16)
    ends = jnp.cumsum(lengths)
    starts = ends - lengths
    positions = lax.axis_index(("rows", "sub")) * tok_local + jnp.arange(tok_local, dtype=jnp.int32)
    member = (
        (positions[None, :] >= starts[:, None]) & (positions[None, :] < ends[:, None])
    ).astype(jnp.bfloat16)
    scaled_member = member[None, :, :] * jnp.transpose(g_low)[:, None, :]
    partial_grad = jnp.einsum(
        "apt,tb->pab", scaled_member, x_low, preferred_element_type=jnp.float32
    )
    partial_grad = partial_grad.reshape(passages, width_cols * x_low.shape[1])
    pgrad = lax.psum(partial_grad, ("rows", "sub"))
    pgrad_low = pgrad.astype(jnp.bfloat16)
    sumsq_part = jnp.sum(pgrad * pgrad, axis=1)
    raw_part = lax.dot_general(
        pgrad_low, corpus, (((1,), (1,)), ((), ())), preferred_element_type=jnp.float32
    )
    labels = jnp.arange(passages, dtype=jnp.int32)[:, None]
    raw, sumsq = lax.psum((raw_part, sumsq_part), "feat")
    scale = 2.5 / math.sqrt(K) * lax.rsqrt(sumsq / K + 1e-06)
    score = raw * scale[:, None]
    owned = owner[None, :] == labels
    local_top = jnp.max(jnp.where(owned, jnp.float32(-1e30), score), axis=1)
    top = lax.pmax(local_top, ("rows", "sub"))
    weight = jnp.where(owned, jnp.float32(0.0), jnp.exp(score - top[:, None]))
    total = lax.psum(jnp.sum(weight, axis=1), ("rows", "sub"))
    weight_low = weight.astype(jnp.bfloat16)
    span = passages // lax.axis_size(("rows", "sub"))
    summed = lax.psum_scatter(
        jnp.dot(weight_low, corpus, preferred_element_type=jnp.float32),
        ("rows", "sub"),
        scatter_dimension=0,
        tiled=True,
    )
    own_total = lax.dynamic_slice_in_dim(total, lax.axis_index(("rows", "sub")) * span, span, 0)
    return summed / own_total[:, None]


def solution(mesh):
    return jax.shard_map(
        local,
        mesh=mesh,
        in_specs=(
            P(("groups", "rows", "sub"), "feat"),
            P(("groups", "rows", "sub"), "feat"),
            P(("groups", "feat"), None),
            P(("groups", "feat"), None),
            P("groups"),
            P(("groups", "rows", "sub"), "feat"),
            P(("rows", "sub")),
        ),
        out_specs=P(("groups", "rows", "sub"), "feat"),
        check_vma=False,
    )
```

profile of v0, /device:TPU:0, one launch (start us, length us, event | category | flops | bytes accessed | tf_op | source)
XLA Modules:
  0.0 233.7 jit_solution(10716244795493063472)
XLA Ops:
  6.5 0.0 copy-start
  6.5 0.0 reduce-scatter.3.cloned.1.call-start
  6.5 4.7 %fusion.18 = f32[1024,128]{0,1:T(8,128)} fusion(bf16[1024,2048]{1,0:T(8,128)(2,1)} %param.8, bf16[2048,128]{1,0:T(8,128)(2,1)} %param.10), kind=kOutput, calls=%fused_computation.26 | convolution fusion | flops 536870912 | bytes 5242880 | tf_op jit(solution)/shard_map/dot_general | solution.py:16
  11.3 0.0 reduce-scatter.3.cloned.1.call-update
  11.3 0.0 copy-start.3
  11.3 0.0 all-reduce.4.cloned.1.call-start
  11.4 0.0 copy-done
  11.4 10.1 %fusion.17 = f32[1024,128]{0,1:T(8,128)S(1)} fusion(bf16[1024,7168]{1,0:T(8,128)(2,1)} %param.7, bf16[7168,128]{1,0:T(8,128)(2,1)S(1)} %copy-done), kind=kOutput, calls=%fused_computation.25 | convolution fusion | flops 1879048192 | bytes 17039360 | tf_op jit(solution)/shard_map/dot_general | solution.py:15
  21.5 0.0 copy-done.3
  21.5 0.1 copy.9
  21.7 0.2 reduce-window.8
  21.8 0.1 reduce
  22.0 0.1 and_convert_fusion
  22.1 34.1 %all-reduce.7 = bf16[1024,128]{0,1:T(8,128)(2,1)S(1)} all-reduce(f32[1024,128]{0,1:T(8,128)S(1)} %fusion.17), channel_id=1, replica_groups=mesh['groups'=2,'feat'=4,'rows'=2,'sub'=2] {'feat'}, use_global_device_ids=true, to_apply=%region_0.0 | all-reduce | flops 131072 | bytes 786432 | tf_op jit(solution)/shard_map/psum | solution.py:18
  56.2 0.0 reduce-scatter.3.cloned.1.call-done
  56.3 0.9 convert_bitcast_fusion
  57.2 4.1 %fusion = f32[128,32,128]{2,0,1:T(8,128)} fusion(bf16[32,1024]{1,0:T(8,128)(2,1)S(1)} %convert_bitcast_fusion, bf16[128,1024]{1,0:T(8,128)(2,1)S(1)} %and_convert_fusion, bf16[1024,128]{0,1:T(8,128)(2,1)S(1)} %all-reduce.7), kind=kOutput, calls=%fused_computation | convolution fusion | flops 1090519040 | bytes 2686976 | tf_op jit(solution)/shard_map/apt,tb->pab/dot_general | solution.py:28
  61.3 0.0 all-reduce.4.cloned.1.call-update
  61.3 0.0 copy-start.2
  61.3 0.0 all-reduce.6.cloned.1.call-start
  61.4 49.9 %all-reduce.4.cloned.1.call-done = f32[128,4096]{0,1:T(8,128)} async-done(((f32[128,4096]{0,1:T(8,128)}), f32[128,4096]{0,1:T(8,128)}) %all-reduce.4.cloned.1.call-update) | async-done | bytes 2097168 | tf_op jit(solution)/shard_map/psum | solution.py:32
  111.3 13.1 %fusion.4 = f32[128,2048]{1,0:T(8,128)} fusion(bf16[2048,4096]{1,0:T(8,128)(2,1)} %param.12, f32[128,4096]{0,1:T(8,128)} %all-reduce.4.cloned.1.call-done), kind=kOutput, calls=%fused_computation.7 | convolution fusion | flops 2148007936 | bytes 19922944 | tf_op jit(solution)/shard_map/dot_general | solution.py:35
  124.3 0.0 all-reduce.6.cloned.1.call-update
  124.3 0.0 reduce-scatter.5.cloned.1.call-start
  124.4 2.1 multiply_reduce_fusion
  126.5 12.0 %psum.38 = f32[128]{0:T(128)S(1)} all-reduce(f32[128]{0:T(128)S(1)} %multiply_reduce_fusion), channel_id=1, replica_groups=mesh['groups'=2,'feat'=4,'rows'=2,'sub'=2] {'feat'}, use_global_device_ids=true, to_apply=%region_6.7 | all-reduce | flops 128 | bytes 1024 | tf_op jit(solution)/shard_map/psum | solution.py:39
  138.6 37.9 %all-reduce.6.cloned.1.call-done = f32[128,2048]{1,0:T(8,128)} async-done(((f32[128,2048]{1,0:T(8,128)}), f32[128,2048]{1,0:T(8,128)}) %all-reduce.6.cloned.1.call-update) | async-done | bytes 1048592 | tf_op jit(solution)/shard_map/psum | solution.py:39
  176.5 0.0 copy-done.2
  176.5 1.5 select_reduce_fusion
  178.0 7.0 %pmax.7 = f32[128]{0:T(128)S(1)} all-reduce(f32[128]{0:T(128)S(1)} %select_reduce_fusion), channel_id=1, replica_groups=mesh['groups'=2,'feat'=4,'rows'=2,'sub'=2] {'rows','sub'}, use_global_device_ids=true, to_apply=%region_8.9 | all-reduce | flops 128 | bytes 1024 | tf_op jit(solution)/shard_map/pmax | solution.py:44
  185.1 0.0 copy-start.1
  185.1 10.0 %fusion.8 = f32[128,4096]{1,0:T(8,128)} fusion(bf16[2048,4096]{1,0:T(8,128)(2,1)} %param.12, f32[128,2048]{1,0:T(8,128)} %all-reduce.6.cloned.1.call-done, f32[128]{0:T(128)S(1)} %pmax.7, f32[128]{0:T(128)S(1)} %rsqrt_multiply_fusion, s32[2048]{0:T(1024)S(1)} %copy-done.2), kind=kOutput, calls=%fused_computation.12 | convolution fusion | flops 2148794368 | bytes 19932160 | tf_op jit(solution)/shard_map/dot_general | solution.py:50
  195.1 0.0 reduce-scatter.5.cloned.1.call-update
  195.1 0.0 copy-done.1
  195.1 0.4 fusion.6
  195.5 5.9 %psum.39 = f32[128]{0:T(128)S(1)} all-reduce(f32[128]{0:T(128)S(1)} %fusion.6), channel_id=1, replica_groups=mesh['groups'=2,'feat'=4,'rows'=2,'sub'=2] {'rows','sub'}, use_global_device_ids=true, to_apply=%region_11.12 | all-reduce | flops 128 | bytes 1024 | tf_op jit(solution)/shard_map/psum | solution.py:46
  201.4 0.1 dynamic_slice.3
  201.5 23.7 %reduce-scatter.5.cloned.1.call-done = f32[32,4096]{1,0:T(8,128)} async-done(((f32[128,4096]{1,0:T(8,128)}), f32[32,4096]{1,0:T(8,128)}) %reduce-scatter.5.cloned.1.call-update) | async-done | bytes 524304 | tf_op jit(solution)/shard_map/reduce_scatter | solution.py:49
  225.2 1.9 broadcast_divide_fusion
  (3 shorter events, 0.0 us)
Async XLA Ops:
  6.5 4.8 %copy-start = (bf16[7168,128]{1,0:T(8,128)(2,1)S(1)}, bf16[7168,128]{1,0:T(8,128)(2,1)}, u32[]{:S(2)}) copy-start(bf16[7168,128]{1,0:T(8,128)(2,1)} %param.9) | copy-start | bytes 5505028
  6.5 49.7 %reduce-scatter.3.cloned.1.call-start = ((), (), s32[]{:S(2)}) async-start(), calls=%async_computation.2 | async-start | bytes 655360 | tf_op jit(solution)/shard_map/reduce_scatter | solution.py:20
  11.3 10.2 %copy-start.3 = (s32[128]{0:T(128)S(1)}, s32[128]{0:T(128)}, u32[]{:S(2)}) copy-start(s32[128]{0:T(128)} %param.11) | copy-start | bytes 1540
  11.3 99.9 %all-reduce.4.cloned.1.call-start = ((), (), s32[]{:S(2)}) async-start(), calls=%async_computation.3 | async-start | bytes 4194304 | tf_op jit(solution)/shard_map/psum | solution.py:32
  61.3 115.2 %copy-start.2 = (s32[2048]{0:T(1024)S(1)}, s32[2048]{0:T(1024)}, u32[]{:S(2)}) copy-start(s32[2048]{0:T(1024)} %param.13) | copy-start | bytes 24580
  61.3 115.2 %all-reduce.6.cloned.1.call-start = ((), (), s32[]{:S(2)}) async-start(), calls=%async_computation.4 | async-start | bytes 2097152 | tf_op jit(solution)/shard_map/psum | solution.py:39
  124.3 100.9 %reduce-scatter.5.cloned.1.call-start = ((), (), s32[]{:S(2)}) async-start(), calls=%async_computation.5 | async-start | bytes 2621440 | tf_op jit(solution)/shard_map/reduce_scatter | solution.py:49
  185.1 10.0 %copy-start.1 = (f32[128,2048]{1,0:T(8,128)S(1)}, f32[128,2048]{1,0:T(8,128)}, u32[]{:S(2)}) copy-start(f32[128,2048]{1,0:T(8,128)} %all-reduce.6.cloned.1.call-done) | copy-start | bytes 3145732
Sparse Core Ops, SparseCore 0:
  11.4 26.0 reduce-scatter.2
  61.4 49.7 all-reduce.3
  124.5 52.0 all-reduce.5
  195.2 29.9 reduce-scatter.4
where the time goes:
time: 234 us
  waiting for transfers between devices  112 us (48%)
  blocking collectives  59.1 us (25%)
  matrix products  42.1 us (18%)
  between operations  13.2 us (6%)
  other arithmetic  7.37 us (3%)
    psum x1, waiting for transfers between devices, local(): pgrad = lax.psum(partial_grad, ('rows', 'sub'))  49.9 us
    psum x1, waiting for transfers between devices, local(): raw, sumsq = lax.psum((raw_part, sumsq_part), 'feat')  37.9 us
    psum x1, blocking collectives, local(): summed_x = lax.psum(part_x, 'feat')  34.1 us
    reduce_scatter x1, waiting for transfers between devices, local(): lax.psum_scatter(jnp.dot(weight_low, corpus, preferred_element_type=jnp.f...  23.7 us
    dot_general x1, matrix products, local(): lax.dot_general(pgrad_low, corpus, (((1,), (1,)), ((), ())), preferred_el...  13.1 us
    psum x1, blocking collectives, local(): raw, sumsq = lax.psum((raw_part, sumsq_part), 'feat')  12 us
    dot_general x1, matrix products, local(): part_x = jnp.dot(activations, proj_in, preferred_element_type=jnp.float32)  10.1 us
    dot_general x1, matrix products, local(): jnp.dot(weight_low, corpus, preferred_element_type=jnp.float32)  10 us
  transfers between devices with their start and end apart: 4, of which 3 were waited for; matrix products, arithmetic and copies ran while one was open for 6% of the time, Pallas kernels for 0%

commit v1 on v0

v1 whole, which is shorter than its diff:
```python
import functools
import math

import jax
import jax.numpy as jnp
from jax import lax
from jax.experimental import pallas as pl
from jax.experimental.pallas import tpu as pltpu
from jax.sharding import PartitionSpec as P

K = 16384
LONGEST = 64
LANES = 128
LOW = -1e30
F32, BF16 = jnp.float32, jnp.bfloat16
MIB = 1024 * 1024
CODES = 16
STEP = 369.0
FULL = 32767.0


def params(mib=16):
    return pltpu.CompilerParams(vmem_limit_bytes=mib * MIB)


def whole(shape):
    return pl.BlockSpec(shape, lambda *_: (0,) * len(shape))


VMEM = pl.BlockSpec(memory_space=pltpu.VMEM)
ANY = pl.BlockSpec(memory_space=pl.ANY)
HBM = pl.BlockSpec(memory_space=pltpu.HBM)


def level_of(value):
    return jnp.floor(jnp.log(jnp.maximum(value, 1e-30)) * STEP)


def value_of(level):
    return jnp.exp(level * (1.0 / STEP))


def to_short(value):
    return jnp.floor(value + 0.5).astype(jnp.int32).astype(jnp.int16)


def from_short(value):
    return value.astype(jnp.int32).astype(F32)


def scale_level(peak):
    return level_of(peak) + 2.0


def turned_dot(proj_t, tokens):
    return lax.dot_general(proj_t, tokens, (((1,), (1,)), ((), ())), preferred_element_type=F32)


def rows_of(total, count):
    return [pl.ds(n * (total // count), total // count) for n in range(count)]


def eye(size):
    return jnp.where(
        lax.broadcasted_iota(jnp.int32, (size, size), 0) == lax.broadcasted_iota(jnp.int32, (size, size), 1), 1.0, 0.0
    ).astype(BF16)


def turn_low(value):
    return turned_dot(eye(value.shape[1]), value).astype(BF16)


def x_body(nfeat, steps, ahead, me_ref, act_hbm, proj_hbm, own_ref, *rest):
    outs, (acts, proj, total, act_sems, proj_sems) = rest[:nfeat - 1], rest[nfeat - 1:]
    rank, quarter = own_ref.shape
    depth = proj_hbm.shape[0]
    chunks = rows_of(depth, steps)
    loads = [pltpu.make_async_copy(act_hbm.at[:, c], acts.at[n], act_sems.at[n]) for n, c in enumerate(chunks)]
    proj_loads = [pltpu.make_async_copy(proj_hbm.at[c, :], proj.at[n], proj_sems.at[n]) for n, c in enumerate(chunks)]
    for n in range(ahead):
        proj_loads[n].start()
        loads[n].start()
    for n in range(steps):
        proj_loads[n].wait()
        proj_t = turn_low(proj[n])
        loads[n].wait()
        if n + ahead < steps:
            proj_loads[n + ahead].start()
            loads[n + ahead].start()
        part = turned_dot(proj_t, acts[n])
        total[...] = part if n == 0 else total[...] + part
    for j in range(nfeat):
        to = lax.rem(me_ref[0] + j, nfeat)
        value = total[:, pl.ds(pl.multiple_of(to * quarter, quarter), quarter)]
        if j == 0:
            own_ref[...] = value
        else:
            level = scale_level(jnp.max(jnp.abs(value), axis=0, keepdims=True))
            outs[j - 1][:rank, :] = to_short(value * (FULL / value_of(level)))
            outs[j - 1][rank:, :] = jnp.broadcast_to(level, (CODES, quarter)).astype(jnp.int32).astype(jnp.int16)


def project_x(me, act, proj, nfeat):
    tok, depth = act.shape
    rank = proj.shape[1]
    quarter = tok // nfeat
    steps = 7
    chunk = depth // steps
    return pl.pallas_call(
        functools.partial(x_body, nfeat, steps, 3),
        grid_spec=pltpu.PrefetchScalarGridSpec(
            num_scalar_prefetch=1,
            grid=(),
            in_specs=[HBM, HBM],
            out_specs=[VMEM] * nfeat,
            scratch_shapes=[
                pltpu.VMEM((steps, tok, chunk), BF16),
                pltpu.VMEM((steps, chunk, rank), BF16),
                pltpu.VMEM((rank, tok), F32),
                pltpu.SemaphoreType.DMA((steps,)),
                pltpu.SemaphoreType.DMA((steps,)),
            ],
        ),
        out_shape=[jax.ShapeDtypeStruct((rank, quarter), F32)]
        + [jax.ShapeDtypeStruct((rank + CODES, quarter), jnp.int16)] * (nfeat - 1),
        compiler_params=params(52),
        cost_estimate=pl.CostEstimate(flops=2 * tok * depth * rank, bytes_accessed=2 * depth * (tok + rank), transcendentals=0),
        name="project_x",
    )(me, act, proj)


def g_body(nfeat, steps, me_ref, grad_hbm, proj_hbm, starts_ref, ends_ref, own_ref, *rest):
    outs, (grads, proj, turned, grad_sems, proj_sem) = rest[:nfeat - 1], rest[nfeat - 1:]
    width, tok = own_ref.shape
    rows = rows_of(tok, steps)
    proj_load = pltpu.make_async_copy(proj_hbm, proj, proj_sem)
    proj_load.start()
    loads = [pltpu.make_async_copy(grad_hbm.at[r, :], grads.at[r, :], grad_sems.at[n]) for n, r in enumerate(rows)]
    for load in loads:
        load.start()
    proj_load.wait()
    proj_t = turn_low(proj[...])
    for n in range(0, steps, 2):
        loads[n].wait()
        loads[n + 1].wait()
        at = slice(n * tok // steps, (n + 2) * tok // steps)
        turned[:, at] = turned_dot(proj_t, grads[at, :])
    chunks = tok // LANES
    for j in range(nfeat):
        to = lax.rem(me_ref[0] + j, nfeat)
        at = pl.ds(pl.multiple_of(to * width, width), width)
        if j == 0:
            own_ref[...] = turned[at, :]
        else:
            parts = [turned[at, n * LANES:(n + 1) * LANES] for n in range(chunks)]
            peak = functools.reduce(jnp.maximum, [jnp.abs(p) for p in parts])
            level = scale_level(jnp.max(peak, axis=0, keepdims=True))
            factor = FULL / value_of(level)
            for n in range(chunks):
                outs[j - 1][n * width:(n + 1) * width, :] = to_short(parts[n] * factor)
            outs[j - 1][chunks * width:, :] = jnp.broadcast_to(level, (CODES, LANES)).astype(jnp.int32).astype(jnp.int16)


def project_g(me, grads, proj, nfeat, *after):
    tok, depth = grads.shape
    rank = proj.shape[1]
    width = rank // nfeat
    steps = 4
    short = (tok // LANES * width + CODES, LANES)
    return pl.pallas_call(
        functools.partial(g_body, nfeat, steps),
        grid_spec=pltpu.PrefetchScalarGridSpec(
            num_scalar_prefetch=1,
            grid=(),
            in_specs=[HBM, HBM] + [ANY] * len(after),
            out_specs=[VMEM] * nfeat,
            scratch_shapes=[
                pltpu.VMEM((tok, depth), BF16),
                pltpu.VMEM((depth, rank), BF16),
                pltpu.VMEM((rank, tok), F32),
                pltpu.SemaphoreType.DMA((steps,)),
                pltpu.SemaphoreType.DMA,
            ],
        ),
        out_shape=[jax.ShapeDtypeStruct((width, tok), F32)] + [jax.ShapeDtypeStruct(short, jnp.int16)] * (nfeat - 1),
        compiler_params=params(53),
        cost_estimate=pl.CostEstimate(flops=2 * tok * depth * rank, bytes_accessed=2 * depth * (tok + rank), transcendentals=0),
        name="project_g",
    )(me, grads, proj, *after)


def join_x_body(nafter, *refs):
    own_ref, others, out_ref = refs[nafter], refs[nafter + 1:-1], refs[-1]
    rows = own_ref.shape[0]
    value = own_ref[...]
    for other in others:
        scale = value_of(from_short(other[rows:, :])[0:1, :]) * (1.0 / FULL)
        value = value + from_short(other[:rows, :]) * scale
    out_ref[...] = value.astype(BF16)


def join_g_body(nafter, *refs):
    own_ref, others, out_ref = refs[nafter], refs[nafter + 1:-1], refs[-1]
    width, tok = own_ref.shape
    chunks = tok // LANES
    scales = [value_of(from_short(other[chunks * width:, :])[0:1, :]) * (1.0 / FULL) for other in others]
    for c in range(chunks):
        value = own_ref[:, c * LANES:(c + 1) * LANES]
        for other, scale in zip(others, scales):
            value = value + from_short(other[c * width:(c + 1) * width, :]) * scale
        out_ref[:, c * LANES:(c + 1) * LANES] = value.astype(BF16)


def join(body, parts, after=()):
    return pl.pallas_call(
        functools.partial(body, len(after)),
        in_specs=[ANY] * len(after) + [VMEM] * len(parts),
        out_specs=VMEM,
        out_shape=jax.ShapeDtypeStruct(parts[0].shape, BF16),
        compiler_params=params(),
        name=body.__name__,
    )(*after, *parts)


def pack_body(x_refs, *rest):
    pieces, more, out_ref = rest[:x_refs], rest[x_refs:-1], rest[-1]
    size = pieces[0].shape[1]
    for n, piece in enumerate(pieces):
        out_ref[:, n * size:(n + 1) * size] = piece[...]
    for ref in more:
        rows = ref.shape[0]
        for n in range(ref.shape[1] // size):
            out_ref[n * rows:(n + 1) * rows, x_refs * size:] = ref[:, n * size:(n + 1) * size]


def pack(pieces, more=()):
    rows, size = pieces[0].shape
    count = len(pieces) + len(more)
    return pl.pallas_call(
        functools.partial(pack_body, len(pieces)),
        in_specs=[VMEM] * count,
        out_specs=VMEM,
        out_shape=jax.ShapeDtypeStruct((rows, count * size), BF16),
        compiler_params=params(),
        name="pack",
    )(*pieces, *more)


def token_body(width, me_ref, first_ref, last_ref, *rest):
    out_ref = rest[-1]
    rank = first_ref.shape[0]
    size = last_ref.shape[1] // 2
    pieces = [first_ref[:, n * size:(n + 1) * size] for n in range(3)] + [last_ref[:, :size]]
    for source, piece in zip(sources_of(me_ref[0]), pieces):
        out_ref[:rank, pl.ds(pl.multiple_of(source * size, size), size)] = piece
    for n in range(rank // width):
        out_ref[rank:, n * size:(n + 1) * size] = last_ref[n * width:(n + 1) * width, size:]


def token_block(me, first, last, width, after=()):
    rank, size = last.shape
    return pl.pallas_call(
        functools.partial(token_body, width),
        grid_spec=pltpu.PrefetchScalarGridSpec(
            num_scalar_prefetch=1, grid=(), in_specs=[VMEM] * 2 + [ANY] * len(after), out_specs=VMEM
        ),
        out_shape=jax.ShapeDtypeStruct((rank + width, rank // width * size // 2), BF16),
        compiler_params=params(),
        name="token_block",
    )(me, first, last, *after)


def turn(row):
    return jnp.transpose(jnp.broadcast_to(row, (LANES, row.shape[1])))[:, 0:1]


def turn_back(column):
    return jnp.transpose(jnp.broadcast_to(column, (column.shape[0], LANES)))[0:1, :]


def norm_of(sumsq):
    return sumsq / K + 1e-06


def spread(row, lanes):
    return jnp.concatenate([row] * (lanes // row.shape[1]), axis=1)


def code_rows(rows, lanes):
    at = lax.broadcasted_iota(jnp.int32, (CODES, lanes), 0)
    tile = jnp.zeros((CODES, lanes), F32)
    for n, row in enumerate(rows):
        tile = jnp.where(at == n, spread(row, lanes), tile)
    return tile


def loads_of(corpus_hbm, corpus_ref, sems, quarters, halves):
    size = corpus_ref.shape[1]
    loads = []
    for n, quarter in enumerate(quarters):
        rows = pl.ds(pl.multiple_of(quarter * size, size), size)
        for h, here in enumerate(rows_of(corpus_ref.shape[2], halves)):
            loads.append(pltpu.make_async_copy(corpus_hbm.at[rows, here], corpus_ref.at[n, :, here], sems.at[n * halves + h]))
    return loads


def write_scores(value, sumsq, out_ref):
    passages, quarter = value.shape
    coarse = level_of(sumsq)
    fine = jnp.floor((jnp.maximum(sumsq, 1e-30) / value_of(coarse) - 1.0) * (2.0**22))
    level = scale_level(jnp.max(jnp.abs(value), axis=0, keepdims=True))
    out_ref[:passages, :] = to_short(value * (FULL / value_of(level)))
    out_ref[passages:, :] = code_rows([level, coarse, fine], quarter).astype(jnp.int32).astype(jnp.int16)


def hold_body(me_ref, corpus_hbm, after_ref, held_ref, sem):
    size = held_ref.shape[0]
    load = pltpu.make_async_copy(corpus_hbm.at[pl.ds(pl.multiple_of(me_ref[0] * size, size), size), :], held_ref, sem)
    load.start()
    load.wait()


def hold(me, corpus, nfeat, after):
    rows, depth = corpus.shape
    return pl.pallas_call(
        hold_body,
        grid_spec=pltpu.PrefetchScalarGridSpec(
            num_scalar_prefetch=1,
            grid=(),
            in_specs=[HBM, ANY],
            out_specs=VMEM,
            scratch_shapes=[pltpu.SemaphoreType.DMA],
        ),
        out_shape=jax.ShapeDtypeStruct((rows // nfeat, depth), BF16),
        compiler_params=params(34),
        cost_estimate=pl.CostEstimate(flops=0, bytes_accessed=4 * rows // nfeat * depth, transcendentals=0),
        name="hold",
    )(me, corpus, after)


def first_body(nblk, passages, place_ref, starts_ref, ends_ref, *rest):
    blocks, corpus_hbm = rest[:nblk], rest[nblk]
    out_ref, sumsq_ref, low, held_ref, corpus_ref, tokens, grad, sems, held_sems = rest[nblk + 1:]
    me = place_ref[0]
    sources = sources_of(me)
    loads = loads_of(corpus_hbm, corpus_ref, sems, sources[3:], 1)
    later = loads_of(corpus_hbm, held_ref, held_sems, sources[1:3], 1)
    for load in loads + later:
        load.start()

    height, tok = blocks[0].shape
    rank = height - low.shape[1] // LANES
    width = height - rank
    for n in range(nblk):
        tokens[:, pl.ds(pl.multiple_of(place_ref[3 + n] * tok, tok), tok)] = blocks[n][...]
    group = LANES // width
    window = -(-group * LONGEST // LANES) * LANES + LANES

    def step(i, carry):
        first = i * group
        base = jnp.minimum((starts_ref[first] // LANES) * LANES, nblk * tok - window)
        here = pl.ds(pl.multiple_of(base, LANES), window)
        g_part = tokens[rank:, here]
        token = base + lax.broadcasted_iota(jnp.int32, (CODES, window), 1)
        stack = []
        for q in range(group):
            inside = (token >= starts_ref[first + q]) & (token < ends_ref[first + q])
            member = jnp.where(inside, 1.0, 0.0).astype(BF16)
            stack.append(g_part * jnp.concatenate([member] * (width // CODES), axis=0))
        grad[pl.ds(pl.multiple_of(i * LANES, LANES), LANES), :] = lax.dot_general(
            jnp.concatenate(stack, axis=0), tokens[:rank, here], (((1,), (1,)), ((), ())), preferred_element_type=F32
        )
        return carry

    lax.fori_loop(0, passages // group, step, 0, unroll=4)
    squares = jnp.zeros((passages, LANES), F32)
    for a in range(width):
        column = grad[pl.ds(a, passages, stride=width), :]
        squares = squares + column * column
        low[:, a * LANES:(a + 1) * LANES] = column.astype(BF16)
    sumsq = jnp.sum(jnp.transpose(squares), axis=0, keepdims=True)
    sumsq_ref[...] = jnp.broadcast_to(sumsq, sumsq_ref.shape)
    norm = turn(lax.rsqrt(norm_of(sumsq)))
    for load in loads:
        load.wait()
    write_scores(norm * turned_dot(low[...], corpus_ref[0]), sumsq, out_ref)
    for load in later:
        load.wait()


def first_scores(place, starts, ends, blocks, corpus, nfeat):
    passages = starts.shape[0]
    rows, depth = corpus.shape
    quarter = rows // nfeat
    height, tok = blocks[0].shape
    nblk = len(blocks)
    return pl.pallas_call(
        functools.partial(first_body, nblk, passages),
        grid_spec=pltpu.PrefetchScalarGridSpec(
            num_scalar_prefetch=3,
            grid=(),
            in_specs=[VMEM] * nblk + [HBM],
            out_specs=[VMEM] * 4,
            scratch_shapes=[
                pltpu.VMEM((1, quarter, depth), BF16),
                pltpu.VMEM((height, nblk * tok), BF16),
                pltpu.VMEM((passages * depth // LANES, LANES), F32),
                pltpu.SemaphoreType.DMA((1,)),
                pltpu.SemaphoreType.DMA((nfeat - 2,)),
            ],
        ),
        out_shape=[
            jax.ShapeDtypeStruct((passages + CODES, quarter), jnp.int16),
            jax.ShapeDtypeStruct((8, passages), F32),
            jax.ShapeDtypeStruct((passages, depth), BF16),
            jax.ShapeDtypeStruct((nfeat - 2, quarter, depth), BF16),
        ],
        compiler_params=params(30),
        cost_estimate=pl.CostEstimate(flops=2 * passages * depth * rows, bytes_accessed=rows * depth, transcendentals=0),
        name="first_scores",
    )(place, starts, ends, *blocks, corpus)


def near_body(low_ref, sumsq_ref, held_own_ref, held_ref, own_ref, across_ref, beside_ref):
    sumsq = sumsq_ref[0:1, :]
    norm = turn(lax.rsqrt(norm_of(sumsq)))
    write_scores(norm * turned_dot(low_ref[...], held_ref[0]), sumsq, beside_ref)
    across_ref[...] = norm * turned_dot(low_ref[...], held_ref[1])
    own_ref[...] = norm * turned_dot(low_ref[...], held_own_ref[...])


def near_scores(low, sumsq, held_own, held):
    passages, depth = low.shape
    quarter = held.shape[1]
    return pl.pallas_call(
        near_body,
        in_specs=[VMEM] * 4,
        out_specs=[VMEM] * 3,
        out_shape=[jax.ShapeDtypeStruct((passages, quarter), F32)] * 2
        + [jax.ShapeDtypeStruct((passages + CODES, quarter), jnp.int16)],
        compiler_params=params(8),
        cost_estimate=pl.CostEstimate(flops=6 * passages * depth * quarter, bytes_accessed=6 * quarter * depth, transcendentals=0),
        name="near_scores",
    )(low, sumsq, held_own, held)


def split3(value):
    high = value.astype(BF16)
    rest = value - high.astype(F32)
    middle = rest.astype(BF16)
    return [p.astype(F32) for p in (high, middle, (rest - middle.astype(F32)).astype(BF16))]


def pack_level(tile):
    lane = lax.broadcasted_iota(jnp.int32, tile.shape, 1)
    out = jnp.zeros(tile.shape, F32)
    for n, piece in enumerate(split3(tile)):
        out = jnp.where(lane == n, piece, out)
    return out.astype(BF16)


def unpack_level(tile):
    return jnp.broadcast_to(jnp.sum(tile.astype(F32), axis=1, keepdims=True), tile.shape)


def read_scores(ref):
    passages = ref.shape[0] - CODES
    code = from_short(ref[passages:, :])
    base = value_of(code[1:2, :passages])
    square = base + base * (code[2:3, :passages] * (1.0 / 2.0**22))
    return from_short(ref[:passages, :]) * (value_of(code[0:1, :]) * (1.0 / FULL)), square


def add_terms(terms):
    sumsq = functools.reduce(jnp.add, [square for _, square in terms])
    scale = lax.rsqrt(norm_of(sumsq))
    return functools.reduce(jnp.add, [value * turn(scale * jnp.sqrt(norm_of(square))) for value, square in terms]), sumsq


def add_body(score_ref, sumsq_ref, message_ref, out_ref):
    value, sumsq = add_terms([(score_ref[...], sumsq_ref[0:1, :]), read_scores(message_ref)])
    write_scores(value, sumsq, out_ref)


def add_scores(score, sumsq, message):
    return pl.pallas_call(
        add_body,
        in_specs=[VMEM] * 3,
        out_specs=VMEM,
        out_shape=jax.ShapeDtypeStruct(message.shape, message.dtype),
        compiler_params=params(8),
        name="add_scores",
    )(score, sumsq, message)


def half_of(value, half, owners):
    size = value.shape[0] // owners // 2
    return jnp.concatenate([value[(2 * n + half) * size:(2 * n + half + 1) * size] for n in range(owners)], axis=0)


def weight_body(owners, me_ref, owner_ref, own_ref, sumsq_ref, *rest):
    *messages, first_ref, second_ref = rest
    passages, rows = own_ref.shape
    value, _ = add_terms([(own_ref[...], sumsq_ref[0:1, :])] + [read_scores(message) for message in messages])
    score = value * (2.5 / math.sqrt(K))
    owner = owner_ref[:, pl.ds(pl.multiple_of(me_ref[0] * rows, rows), rows)]
    owned = owner == lax.broadcasted_iota(jnp.int32, (passages, rows), 0)
    score = jnp.where(owned, LOW, score)
    top = jnp.max(score, axis=1, keepdims=True)
    weight = jnp.where(owned, 0.0, jnp.exp(score - top))
    total = jnp.sum(weight, axis=1, keepdims=True)
    first_ref[:passages // 2, :] = half_of(weight, 0, owners).astype(BF16)
    first_ref[passages // 2:, :] = code_rows(split3(turn_back(top)) + split3(turn_back(total)), rows).astype(BF16)
    second_ref[...] = half_of(weight, 1, owners).astype(BF16)


def weights_of(me, owner, own, sumsq, messages, owners):
    passages, rows = own.shape
    return pl.pallas_call(
        functools.partial(weight_body, owners),
        grid_spec=pltpu.PrefetchScalarGridSpec(
            num_scalar_prefetch=1, grid=(), in_specs=[VMEM] * (3 + len(messages)), out_specs=[VMEM] * 2
        ),
        out_shape=[
            jax.ShapeDtypeStruct((passages // 2 + CODES, rows), BF16),
            jax.ShapeDtypeStruct((passages // 2, rows), BF16),
        ],
        compiler_params=params(8),
        cost_estimate=pl.CostEstimate(flops=8 * passages * rows, bytes_accessed=16 * passages * rows, transcendentals=passages * rows),
        name="weights",
    )(me, owner.reshape(1, -1), own, sumsq, *messages)


def running_stats(owners, codes, before):
    rows = 2 * (codes[0].shape[0] - CODES)
    codes = [code[code.shape[0] - CODES:, :rows].astype(F32) for code in codes]

    def columns(first):
        turned = [turn((c[first:first + 1] + c[first + 1:first + 2]) + c[first + 2:first + 3]) for c in codes]
        return [jnp.concatenate([half_of(column, half, owners) for half in range(2)], axis=0) for column in turned]

    tops, totals = columns(0), columns(3)
    if before is not None:
        tops.append(before[:, 0:1])
        totals.append(before[:, 1:2])
    top = functools.reduce(jnp.maximum, tops)
    factors = [jnp.exp(t - top) for t in tops]
    total = functools.reduce(jnp.add, [f * t for f, t in zip(factors, totals)])
    return top, total, factors


def add_sums(weights, quarters, factors, old, acc_ref):
    step = 512
    for n, (weight, quarter) in enumerate(zip(weights, quarters)):
        for at in range(0, acc_ref.shape[1], step):
            here = slice(at, at + step)
            value = factors[n] * jnp.dot(weight, quarter[:, here], preferred_element_type=F32)
            if n:
                value = acc_ref[:, here] + value
            elif old is not None:
                value = factors[-1] * old[:, here] + value
            acc_ref[:, here] = value


def stats_tile(top, total):
    lane = lax.broadcasted_iota(jnp.int32, (top.shape[0], LANES), 1)
    return jnp.where(lane == 0, top, total)


def sums_body(owners, sources, started, fetch, me_ref, *rest):
    count = 2 * sources
    parts, held_ref, rest = rest[:count], rest[count], rest[count + 1:]
    before, rest = rest[:2 * started], rest[2 * started:]
    if fetch:
        corpus_hbm, acc_ref, stats_ref, fetch_ref, sem = rest
        size = fetch_ref.shape[0]
        at = pl.multiple_of(sources_of(me_ref[0])[fetch] * size, size)
        load = pltpu.make_async_copy(corpus_hbm.at[pl.ds(at, size), :], fetch_ref, sem)
        load.start()
    else:
        acc_ref, stats_ref = rest[-2:]
    pieces = [parts[2 * n:2 * n + 2] for n in range(sources)]
    quarters = [held_ref] if sources == 1 else [held_ref.at[n] for n in range(sources)]
    top, total, factors = running_stats(owners, parts[::2], before[1] if before else None)
    weights = [jnp.concatenate([piece[0][:piece[1].shape[0], :], piece[1][...]], axis=0) for piece in pieces]
    add_sums(weights, quarters, factors, before[0] if before else None, acc_ref)
    stats_ref[...] = stats_tile(top, total)
    if fetch:
        load.wait()


def weighted_sums(me, owners, pieces, held, before, corpus=None, fetch=0, after=()):
    parts = [part for piece in pieces for part in piece]
    passages = 2 * parts[1].shape[0]
    quarter, depth = held.shape[-2:]
    fetched = [jax.ShapeDtypeStruct((quarter, depth), BF16)] if fetch else []
    return pl.pallas_call(
        functools.partial(sums_body, owners, len(pieces), len(before) // 2, fetch),
        grid_spec=pltpu.PrefetchScalarGridSpec(
            num_scalar_prefetch=1,
            grid=(),
            in_specs=[VMEM] * (len(parts) + 1 + len(before)) + [HBM] * len(fetched) + [ANY] * len(after),
            out_specs=[VMEM] * (2 + len(fetched)),
            scratch_shapes=[pltpu.SemaphoreType.DMA] * len(fetched),
        ),
        out_shape=[jax.ShapeDtypeStruct((passages, depth), F32), jax.ShapeDtypeStruct((passages, LANES), F32)] + fetched,
        compiler_params=params(30 if fetch else 8),
        cost_estimate=pl.CostEstimate(flops=2 * passages * quarter * len(pieces) * depth, bytes_accessed=2 * quarter * depth, transcendentals=0),
        name="weighted_sums",
    )(me, *parts, held, *before, *([corpus] if fetch else []), *after)


def last_sums_body(half, nrows, nsub, place_ref, piece_ref, held_ref, old_ref, stats_ref, *rest):
    send_ref, keep_ref = rest[:2] if half == 0 else rest[-3:-1]
    acc = rest[-1]
    span = send_ref.shape[1]
    passages, depth = acc.shape
    core = place_ref[1]
    if half == 0:
        top, total, factors = running_stats(nrows * nsub, [piece_ref], stats_ref)
        share = 1.0 / jnp.maximum(total, 1e-30)
        level = top + jnp.log(jnp.maximum(total, 1e-30))
        columns = [factors[0] * share, factors[1] * share, level]
        lane = lax.broadcasted_iota(jnp.int32, (passages, LANES), 1)
        later = [column[passages:] for column in columns]
        rest[2][...] = jnp.where(lane == 0, later[0], jnp.where(lane == 1, later[1], later[2]))
        columns = [column[:passages] for column in columns]
    else:
        columns = [stats_ref[:, n:n + 1] for n in range(3)]
    old = old_ref.at[pl.ds(half * passages, passages), :]
    add_sums([piece_ref[:passages, :]], [held_ref], columns[:2], old, acc)
    mine = [pl.multiple_of((x * nsub + core) * span, span) for x in range(nrows)]
    other = [pl.multiple_of((x * nsub + (nsub - 1 - core)) * span, span) for x in range(nrows)]
    for x in range(nrows):
        keep_ref[x, :, :depth] = acc[pl.ds(mine[x], span), :]
        send_ref[x, :, :depth] = acc[pl.ds(other[x], span), :].astype(BF16)
    acc[:, 0:LANES] = jnp.broadcast_to(columns[2], (passages, LANES))
    for x in range(nrows):
        keep_ref[x, :, depth:] = acc[pl.ds(mine[x], span), 0:LANES]
        send_ref[x, :, depth:] = pack_level(acc[pl.ds(other[x], span), 0:LANES])


def last_sums(place, half, piece, held, sums, stats, nrows, nsub):
    quarter, depth = held.shape
    passages = sums.shape[0] // 2
    shape = (nrows, passages // (nrows * nsub), depth + LANES)
    ratios = [jax.ShapeDtypeStruct((passages, LANES), F32)] * (1 - half)
    return pl.pallas_call(
        functools.partial(last_sums_body, half, nrows, nsub),
        grid_spec=pltpu.PrefetchScalarGridSpec(
            num_scalar_prefetch=1,
            grid=(),
            in_specs=[VMEM] * 4,
            out_specs=[VMEM] * (3 - half),
            scratch_shapes=[pltpu.VMEM((passages, depth), F32)],
        ),
        out_shape=[jax.ShapeDtypeStruct(shape, BF16), jax.ShapeDtypeStruct(shape, F32)] + ratios,
        compiler_params=params(),
        cost_estimate=pl.CostEstimate(flops=0, bytes_accessed=0, transcendentals=0),
        name="last_sums",
    )(place, piece, held, sums, stats)


def merge_shares(mine, other):
    top = jnp.maximum(mine, other)
    a, b = jnp.exp(mine - top), jnp.exp(other - top)
    share = 1.0 / (a + b)
    return a * share, b * share, top + jnp.log(a + b)


def merged(keep_ref, other_ref, a, b, tile):
    here = slice(tile * LANES, (tile + 1) * LANES)
    return keep_ref[:, here] * a + other_ref[:, here].astype(F32) * b


def merge_core_body(place_ref, keep_ref, other_ref, send_ref, next_ref):
    depth = send_ref.shape[1] - LANES
    mine = place_ref[2]
    blocks = [(keep_ref.at[at], other_ref.at[at]) for at in (1 - mine, mine)]
    shares = [merge_shares(keep[:, depth:], unpack_level(other[:, depth:])) for keep, other in blocks]
    for tile in range(depth // LANES):
        here = slice(tile * LANES, (tile + 1) * LANES)
        send_ref[:, here] = merged(*blocks[0], *shares[0][:2], tile).astype(BF16)
        next_ref[:, here] = merged(*blocks[1], *shares[1][:2], tile)
    send_ref[:, depth:] = pack_level(shares[0][2])
    next_ref[:, depth:] = shares[1][2]


def merge_core(place, keep, other):
    shape = keep.shape[1:]
    return pl.pallas_call(
        merge_core_body,
        grid_spec=pltpu.PrefetchScalarGridSpec(
            num_scalar_prefetch=1,
            grid=(),
            in_specs=[pl.BlockSpec(memory_space=pltpu.VMEM)] * 2,
            out_specs=[pl.BlockSpec(memory_space=pltpu.VMEM)] * 2,
        ),
        out_shape=[jax.ShapeDtypeStruct(shape, BF16), jax.ShapeDtypeStruct(shape, F32)],
        compiler_params=params(),
        name="merge_core",
    )(place, keep, other)


def merge_last_body(done, keep_ref, other_ref, *rest):
    out_ref = rest[-1]
    if done:
        out_ref[:done, :] = rest[0][...]
    depth = keep_ref.shape[1] - LANES
    a, b, _ = merge_shares(keep_ref[:, depth:], unpack_level(other_ref[:, depth:]))
    for tile in range(depth // LANES):
        out_ref[done:, tile * LANES:(tile + 1) * LANES] = merged(keep_ref, other_ref, a, b, tile)


def merge_last(keep, other, before):
    done = before[0].shape[0] if before else 0
    return pl.pallas_call(
        functools.partial(merge_last_body, done),
        in_specs=[VMEM] * (2 + len(before)),
        out_specs=VMEM,
        out_shape=jax.ShapeDtypeStruct((done + keep.shape[0], keep.shape[1] - LANES), F32),
        compiler_params=params(),
        name="merge_last",
    )(keep, other, *before)


def shift(value, axis, by):
    count = lax.axis_size(axis)
    return lax.ppermute(value, axis, [(i, (i + by) % count) for i in range(count)])


def scatter_parts(blocks):
    return [blocks[0]] + [shift(blocks[j], "feat", j) for j in range(1, len(blocks))]


def to_pair(value):
    return lax.ppermute(value, "feat", [(i, i ^ 1) for i in range(lax.axis_size("feat"))])


def sources_of(me):
    return [me, me ^ 1, me ^ 2, me ^ 3]


def relay_body(piece_ref, *rest):
    rest[-1][...] = piece_ref[...]


def relay(piece, *after):
    return pl.pallas_call(
        relay_body,
        in_specs=[VMEM] + [ANY] * len(after),
        out_specs=VMEM,
        out_shape=jax.ShapeDtypeStruct(piece.shape, piece.dtype),
        compiler_params=params(),
        name="relay",
    )(piece, *after)


def gather_tokens(me, g_own, g_others, piece, meanwhile):
    across, beside = shift(piece, "feat", 2), to_pair(piece)
    first = pack([piece, beside, across])
    g_low = join(join_g_body, [g_own] + g_others, (first,))
    last = pack([to_pair(across)], [g_low])
    done = meanwhile(last)
    width = g_low.shape[0]
    here = token_block(me, first, last, width)
    there = token_block(me, shift(first, "rows", 1), shift(last, "rows", 1), width, (done,))
    return [here, there, shift(here, "sub", 1), shift(there, "sub", 1)], [(0, 0), (1, 0), (0, 1), (1, 1)], done


def fast(activations, out_grads, proj_in, proj_out, lengths, corpus, owner):
    nfeat, nrows, nsub = (lax.axis_size(a) for a in ("feat", "rows", "sub"))
    feat, row, sub = (lax.axis_index(a).astype(jnp.int32) for a in ("feat", "rows", "sub"))
    me = feat.reshape(1)
    ends = jnp.cumsum(lengths)
    starts = ends - lengths
    x_parts = project_x(me, activations, proj_in, nfeat)
    g_parts = project_g(me, out_grads, proj_out, nfeat, starts, ends)
    x_piece = join(join_x_body, scatter_parts(x_parts), g_parts[:1])
    blocks, back, held_own = gather_tokens(
        me, g_parts[0], scatter_parts(g_parts)[1:], x_piece, lambda after: hold(me, corpus, nfeat, after)
    )
    order = [(row ^ d) * nsub + (sub ^ c) for d, c in back]
    place = jnp.stack([feat, sub, row] + order)
    message, sumsq, low, held = first_scores(place, starts, ends, blocks, corpus, nfeat)
    own, across, beside = near_scores(low, sumsq, held_own, held)
    across = add_scores(across, sumsq, to_pair(message))
    owners = nrows * nsub
    messages = [to_pair(beside), shift(across, "feat", 2)]
    pieces = weights_of(me, owner, own, sumsq, messages, owners)
    beside, across = [to_pair(p) for p in pieces], [shift(p, "feat", 2) for p in pieces]
    *sums, fetched = weighted_sums(me, owners, [pieces], held_own, (), corpus, 3)
    relayed = [relay(across[0], sums[1])]
    relayed.append(relay(across[1], relayed[0]))
    last = [to_pair(p) for p in relayed]
    sums = weighted_sums(me, owners, [beside, across], held, sums, after=relayed[1:])
    *first, ratios = last_sums(place, 0, last[0], fetched, *sums, nrows, nsub)
    halves = [first, last_sums(place, 1, last[1], fetched, sums[0], ratios, nrows, nsub)]
    ended = [merge_core(place, keep, shift(send, "sub", 1)) for send, keep in halves]
    out = ()
    for send, keep in ended:
        out = (merge_last(keep, shift(send, "rows", 1), out),)
    return out[0]


def general(activations, out_grads, proj_in, proj_out, lengths, corpus, owner):
    tok_local = activations.shape[0]
    passages = lengths.shape[0]
    nfeat = lax.axis_size("feat")
    part_x = jnp.dot(activations, proj_in, preferred_element_type=F32)
    part_g = jnp.dot(out_grads, proj_out, preferred_element_type=F32)
    width_cols = part_g.shape[1] // nfeat
    x_low = lax.psum(part_x, "feat").astype(BF16)
    g_low = lax.psum_scatter(part_g, "feat", scatter_dimension=1, tiled=True).astype(BF16)
    ends = jnp.cumsum(lengths)
    starts = ends - lengths
    positions = lax.axis_index(("rows", "sub")) * tok_local + jnp.arange(tok_local, dtype=jnp.int32)
    member = ((positions[None, :] >= starts[:, None]) & (positions[None, :] < ends[:, None])).astype(BF16)
    scaled_member = member[None, :, :] * jnp.transpose(g_low)[:, None, :]
    partial_grad = jnp.einsum("apt,tb->pab", scaled_member, x_low, preferred_element_type=F32)
    partial_grad = partial_grad.reshape(passages, width_cols * x_low.shape[1])
    pgrad = lax.psum(partial_grad, ("rows", "sub"))
    pgrad_low = pgrad.astype(BF16)
    sumsq_part = jnp.sum(pgrad * pgrad, axis=1)
    raw_part = lax.dot_general(pgrad_low, corpus, (((1,), (1,)), ((), ())), preferred_element_type=F32)
    labels = jnp.arange(passages, dtype=jnp.int32)[:, None]
    raw, sumsq = lax.psum((raw_part, sumsq_part), "feat")
    scale = 2.5 / math.sqrt(K) * lax.rsqrt(sumsq / K + 1e-06)
    score = raw * scale[:, None]
    owned = owner[None, :] == labels
    top = lax.pmax(jnp.max(jnp.where(owned, F32(LOW), score), axis=1), ("rows", "sub"))
    weight = jnp.where(owned, F32(0.0), jnp.exp(score - top[:, None]))
    total = lax.psum(jnp.sum(weight, axis=1), ("rows", "sub"))
    span = passages // lax.axis_size(("rows", "sub"))
    summed = lax.psum_scatter(
        jnp.dot(weight.astype(BF16), corpus, preferred_element_type=F32),
        ("rows", "sub"),
        scatter_dimension=0,
        tiled=True,
    )
    own_total = lax.dynamic_slice_in_dim(total, lax.axis_index(("rows", "sub")) * span, span, 0)
    return summed / own_total[:, None]


def solution(mesh):
    small = mesh.shape["feat"] == 4 and mesh.shape["rows"] == 2 and mesh.shape["sub"] == 2
    return jax.shard_map(
        fast if small else general,
        mesh=mesh,
        in_specs=(
            P(("groups", "rows", "sub"), "feat"),
            P(("groups", "rows", "sub"), "feat"),
            P(("groups", "feat"), None),
            P(("groups", "feat"), None),
            P("groups"),
            P(("groups", "rows", "sub"), "feat"),
            P(("rows", "sub")),
        ),
        out_specs=P(("groups", "rows", "sub"), "feat"),
        check_vma=False,
    )
```

time: 234 us -> 89.6 us (0.38)
  waiting for transfers between devices: 112 us -> 21.5 us
  blocking collectives: 59.1 us -> 0 us
  matrix products: 42.1 us -> 0 us
  Pallas kernels: 0 us -> 34.7 us
  starting transfers between devices: 0.13 us -> 30.4 us
  between operations: 13.2 us -> 0.24 us
  other arithmetic: 7.37 us -> 0.28 us
    psum x2 -> x0, waiting for transfers between devices: 87.8 us -> none  [the longest x1 49.9 us: local(): pgrad = lax.psum(partial_grad, ('rows', 'sub'))]
    psum x3 -> x0, blocking collectives: 52.1 us -> none  [the longest x1 34.1 us: local(): summed_x = lax.psum(part_x, 'feat')]
    dot_general x5 -> x0, matrix products: 42.1 us -> none  [the longest x1 13.1 us: local(): lax.dot_general(pgrad_low, corpus, (((1,), (1,)), ((), ())), preferred_el...]
    pallas_call x0 -> x23, Pallas kernels: none -> 34.7 us  [the longest x1 8.5 us: project_x(): pl.pallas_call(functools.partial(x_body, nfeat, steps, 3), grid_spec=pltp...]
    ppermute x0 -> x26, starting transfers between devices: none -> 30.4 us  [the longest x18 20.1 us: shift(): lax.ppermute(value, axis, [(i, (i + by) % count) for i in range(count)])]
    reduce_scatter x2 -> x0, waiting for transfers between devices: 23.7 us -> none  [the longest x1 23.7 us: local(): lax.psum_scatter(jnp.dot(weight_low, corpus, preferred_element_type=jnp.f...]
    ppermute x0 -> x26, waiting for transfers between devices: none -> 21.5 us  [the longest x18 14.8 us: shift(): lax.ppermute(value, axis, [(i, (i + by) % count) for i in range(count)])]
    pmax x1 -> x0, blocking collectives: 7.02 us -> none  [local(): top = lax.pmax(local_top, ('rows', 'sub'))]
  transfers between devices with their start and end apart: 4 -> 26, of which waited for: 3 -> 13; matrix products, arithmetic and copies ran while one was open for 6% -> 1% of each run, Pallas kernels for 0% -> 21%
where the time goes in v1:
time: 89.6 us; the launch traced here: 89.4 us
  Pallas kernels  34.7 us (39%)
  starting transfers between devices  30.4 us (34%)
  waiting for transfers between devices  21.5 us (24%)
  local copies, waits for them, and re-layouts  2.17 us (2%)
    ppermute x18, starting transfers between devices, shift(): lax.ppermute(value, axis, [(i, (i + by) % count) for i in range(count)])  20.1 us
    ppermute x18, waiting for transfers between devices, shift(): lax.ppermute(value, axis, [(i, (i + by) % count) for i in range(count)])  14.8 us
    ppermute x8, starting transfers between devices, to_pair(): lax.ppermute(value, 'feat', [(i, i ^ 1) for i in range(lax.axis_size('fea...  10.3 us
    pallas_call x1, Pallas kernels, project_x(): pl.pallas_call(functools.partial(x_body, nfeat, steps, 3), grid_spec=pltp...  8.5 us
    ppermute x8, waiting for transfers between devices, to_pair(): lax.ppermute(value, 'feat', [(i, i ^ 1) for i in range(lax.axis_size('fea...  6.68 us
    pallas_call x1, Pallas kernels, first_scores(): pl.pallas_call(functools.partial(first_body, nblk, passages), grid_spec=p...  6.21 us
    pallas_call x1, Pallas kernels, near_scores(): pl.pallas_call(near_body, in_specs=[VMEM] * 4, out_specs=[VMEM] * 3, out_...  4.24 us
    pallas_call x2, Pallas kernels, weighted_sums(): pl.pallas_call(functools.partial(sums_body, owners, len(pieces), len(befo...  3.75 us
  transfers between devices with their start and end apart: 26, of which 13 were waited for; matrix products, arithmetic and copies ran while one was open for 1% of the time, Pallas kernels for 21%

profile of v1, /device:TPU:0, one launch (start us, length us, event | category | flops | bytes accessed | tf_op | source)
XLA Modules:
  0.0 89.4 jit_solution(369404563280756814)
XLA Ops:
  0.0 8.5 %project_x.1 = (f32[128,256]{1,0:T(8,128)S(1)}, s16[144,256]{1,0:T(8,128)(2,1)S(1)}, s16[144,256]{1,0:T(8,128)(2,1)S(1)}, s16[144,256]{1,0:T(8,128)(2,1)S(1)}) custom-call(s32[1]{0:T(128)} %bitcast.me_ref, bf16[1024,7168]{1,0:T(8,128)(2,1)} %act_hbm.1, bf16[7168,128]{1,0:T(8,128)(2,1)} %proj_hbm.3), custom_call_target="tpu_custom_call" | custom-call | flops 1879048192 | bytes 16515072 | tf_op jit(solution)/shard_map/project_x/pallas_call | solution.py:109
  8.5 3.1 %collective-permute-start = (s16[144,256]{1,0:T(8,128)(2,1)S(1)}, s16[144,256]{1,0:T(8,128)(2,1)S(1)}, u32[]{:S(2)}, u32[]{:S(2)}) collective-permute-start(s16[144,256]{1,0:T(8,128)(2,1)S(1)} %get-tuple-element.38), channel_id=1, source_target_pairs={{0,4},{4,8},{8,12},{12,0},{1,5},{5,9},{9,13},{13,1},{2,6},{6,10},{... | collective-permute-start | bytes 221192 | tf_op jit(solution)/shard_map/ppermute | solution.py:729
  11.6 2.6 %collective-permute-start.1 = (s16[144,256]{1,0:T(8,128)(2,1)S(1)}, s16[144,256]{1,0:T(8,128)(2,1)S(1)}, u32[]{:S(2)}, u32[]{:S(2)}) collective-permute-start(s16[144,256]{1,0:T(8,128)(2,1)S(1)} %get-tuple-element.39), channel_id=1, source_target_pairs={{0,8},{4,12},{8,0},{12,4},{1,9},{5,13},{9,1},{13,5},{2,10},{6,14},... | collective-permute-start | bytes 221192 | tf_op jit(solution)/shard_map/ppermute | solution.py:729
  14.2 1.3 %collective-permute-start.2 = (s16[144,256]{1,0:T(8,128)(2,1)S(1)}, s16[144,256]{1,0:T(8,128)(2,1)S(1)}, u32[]{:S(2)}, u32[]{:S(2)}) collective-permute-start(s16[144,256]{1,0:T(8,128)(2,1)S(1)} %get-tuple-element.40), channel_id=1, source_target_pairs={{0,12},{4,0},{8,4},{12,8},{1,13},{5,1},{9,5},{13,9},{2,14},{6,2},{... | collective-permute-start | bytes 221192 | tf_op jit(solution)/shard_map/ppermute | solution.py:729
  15.5 0.1 copy.9
  15.6 0.2 reduce-window.9
  15.8 0.1 reduce.ends_ref
  15.9 3.4 %project_g.1 = (f32[32,1024]{1,0:T(8,128)S(1)}, s16[272,128]{1,0:T(8,128)(2,1)S(1)}, s16[272,128]{1,0:T(8,128)(2,1)S(1)}, s16[272,128]{1,0:T(8,128)(2,1)S(1)}) custom-call(s32[1]{0:T(128)} %bitcast.me_ref, bf16[1024,2048]{1,0:T(8,128)(2,1)} %grad_hbm.1, bf16[2048,128]{1,0:T(8,128)(2,1)S(1)} %copy-done.2, s32[128]{0:T(128)S(1)} %sub.3.starts_ref, ...), custom_call_target="tpu_custom_call" | custom-call | flops 536870912 | bytes 4718592 | tf_op jit(solution)/shard_map/project_g/pallas_call | solution.py:170
  19.4 0.0 collective-permute-done.1.refs_3_
  19.4 0.1 join_x_body.1.rest_0_
  19.4 1.6 %collective-permute-start.4 = (bf16[128,256]{1,0:T(8,128)(2,1)S(1)}, bf16[128,256]{1,0:T(8,128)(2,1)S(1)}, u32[]{:S(2)}, u32[]{:S(2)}) collective-permute-start(bf16[128,256]{1,0:T(8,128)(2,1)S(1)} %join_x_body.1.rest_0_), channel_id=1, source_target_pairs={{0,8},{4,12},{8,0},{12,4},{1,9},{5,13},{9,1},{13,5},{2,10},{6,14},... | collective-permute-start | bytes 196616 | tf_op jit(solution)/shard_map/ppermute | solution.py:729
  21.0 2.2 %collective-permute-start.3 = (bf16[128,256]{1,0:T(8,128)(2,1)S(1)}, bf16[128,256]{1,0:T(8,128)(2,1)S(1)}, u32[]{:S(2)}, u32[]{:S(2)}) collective-permute-start(bf16[128,256]{1,0:T(8,128)(2,1)S(1)} %join_x_body.1.rest_0_), channel_id=1, source_target_pairs={{0,4},{4,0},{8,12},{12,8},{1,5},{5,1},{9,13},{13,9},{2,6},{6,2},{1... | collective-permute-start | bytes 196616 | tf_op jit(solution)/shard_map/ppermute | solution.py:737
  23.3 0.0 collective-permute-start.6
  23.3 1.2 %collective-permute-start.7 = (s16[272,128]{1,0:T(8,128)(2,1)S(1)}, s16[272,128]{1,0:T(8,128)(2,1)S(1)}, u32[]{:S(2)}, u32[]{:S(2)}) collective-permute-start(s16[272,128]{1,0:T(8,128)(2,1)S(1)} %get-tuple-element.42), channel_id=1, source_target_pairs={{0,8},{4,12},{8,0},{12,4},{1,9},{5,13},{9,1},{13,5},{2,10},{6,14},... | collective-permute-start | bytes 208904 | tf_op jit(solution)/shard_map/ppermute | solution.py:729
  24.5 2.7 %collective-permute-start.8 = (s16[272,128]{1,0:T(8,128)(2,1)S(1)}, s16[272,128]{1,0:T(8,128)(2,1)S(1)}, u32[]{:S(2)}, u32[]{:S(2)}) collective-permute-start(s16[272,128]{1,0:T(8,128)(2,1)S(1)} %get-tuple-element.43), channel_id=1, source_target_pairs={{0,12},{4,0},{8,4},{12,8},{1,13},{5,1},{9,5},{13,9},{2,14},{6,2},{... | collective-permute-start | bytes 208904 | tf_op jit(solution)/shard_map/ppermute | solution.py:729
  27.2 0.0 collective-permute-done.4.rest_2_
  27.2 0.5 collective-permute-start.5
  27.7 1.6 %collective-permute-start.9 = (bf16[128,768]{1,0:T(8,128)(2,1)S(1)}, bf16[128,768]{1,0:T(8,128)(2,1)S(1)}, u32[]{:S(2)}, u32[]{:S(2)}) collective-permute-start(bf16[128,768]{1,0:T(8,128)(2,1)S(1)} %pack.2.refs_0_.first_ref), channel_id=1, source_target_pairs={{0,2},{2,0},{1,3},{3,1},{4,6},{6,4},{5,7},{7,5},{8,10},{10,8},{9,1... | collective-permute-start | bytes 589832 | tf_op jit(solution)/shard_map/ppermute | solution.py:729
  29.2 0.9 %collective-permute-done.6.refs_2_ = s16[272,128]{1,0:T(8,128)(2,1)S(1)} collective-permute-done((s16[272,128]{1,0:T(8,128)(2,1)S(1)}, s16[272,128]{1,0:T(8,128)(2,1)S(1)}, u32[]{:S(2)}, u32[]{:S(2)}) %collective-permute-start.6) | collective-permute-done | bytes 69664 | tf_op jit(solution)/shard_map/ppermute | solution.py:729
  30.2 1.2 %collective-permute-done.7.refs_3_ = s16[272,128]{1,0:T(8,128)(2,1)S(1)} collective-permute-done((s16[272,128]{1,0:T(8,128)(2,1)S(1)}, s16[272,128]{1,0:T(8,128)(2,1)S(1)}, u32[]{:S(2)}, u32[]{:S(2)}) %collective-permute-start.7) | collective-permute-done | bytes 69664 | tf_op jit(solution)/shard_map/ppermute | solution.py:729
  31.3 0.0 collective-permute-done.8.refs_4_
  31.3 0.1 join_g_body.1.rest_1_
  31.4 0.6 collective-permute-done.5.rest_0_
  32.0 1.5 %collective-permute-start.10 = (bf16[128,512]{1,0:T(8,128)(2,1)S(1)}, bf16[128,512]{1,0:T(8,128)(2,1)S(1)}, u32[]{:S(2)}, u32[]{:S(2)}) collective-permute-start(bf16[128,512]{1,0:T(8,128)(2,1)S(1)} %pack.3.last_ref.after_ref), channel_id=1, source_target_pairs={{0,2},{2,0},{1,3},{3,1},{4,6},{6,4},{5,7},{7,5},{8,10},{10,8},{9,1... | collective-permute-start | bytes 393224 | tf_op jit(solution)/shard_map/ppermute | solution.py:729
  33.5 2.2 %hold.1.rest_0_.held_own_ref.rest_2_ = bf16[512,4096]{1,0:T(8,128)(2,1)S(1)} custom-call(s32[1]{0:T(128)} %bitcast.me_ref, bf16[2048,4096]{1,0:T(8,128)(2,1)} %rest_3_.1, bf16[128,512]{1,0:T(8,128)(2,1)S(1)} %pack.3.last_ref.after_ref), custom_call_target="tpu_custom_call" | custom-call | bytes 8388608 | tf_op jit(solution)/shard_map/hold/pallas_call | solution.py:325
  35.7 0.1 collective-permute-start.11
  35.8 1.3 %collective-permute-done.10.last_ref = bf16[128,512]{1,0:T(8,128)(2,1)S(1)} collective-permute-done((bf16[128,512]{1,0:T(8,128)(2,1)S(1)}, bf16[128,512]{1,0:T(8,128)(2,1)S(1)}, u32[]{:S(2)}, u32[]{:S(2)}) %collective-permute-start.10) | collective-permute-done | bytes 131104 | tf_op jit(solution)/shard_map/ppermute | solution.py:729
  37.0 0.0 collective-permute-done.9.first_ref
  37.1 2.0 %copy-done = bf16[512,4096]{1,0:T(8,128)(2,1)} copy-done((bf16[512,4096]{1,0:T(8,128)(2,1)}, bf16[512,4096]{1,0:T(8,128)(2,1)S(1)}, u32[]{:S(2)}) %copy-start) | copy-done | bytes 4194328
  39.1 0.1 stack.31.place_ref
  39.1 1.5 %collective-permute-done.12.rest_3_ = bf16[160,1024]{1,0:T(8,128)(2,1)S(1)} collective-permute-done((bf16[160,1024]{1,0:T(8,128)(2,1)S(1)}, bf16[160,1024]{1,0:T(8,128)(2,1)S(1)}, u32[]{:S(2)}, u32[]{:S(2)}) %collective-permute-start.12) | collective-permute-done | bytes 327712 | tf_op jit(solution)/shard_map/ppermute | solution.py:729
  40.7 6.2 %first_scores.1 = (s16[144,512]{1,0:T(8,128)(2,1)S(1)}, f32[8,128]{1,0:T(8,128)S(1)}, bf16[128,4096]{1,0:T(8,128)(2,1)S(1)}, bf16[2,512,4096]{2,1,0:T(8,128)(2,1)S(1)}) custom-call(s32[7]{0:T(128)S(1)} %stack.31.place_ref, s32[128]{0:T(128)S(1)} %sub.3.starts_ref, s32[128]{0:T(128)S(1)} %reduce.ends_ref, bf16[160,1024]{1,0:T(8,128)(2,1)S(1)} %token_block.2.rest_0_, ...), custom_call_target="tpu_custom_call" | custom-call | flops 2147483648 | bytes 8388608 | tf_op jit(solution)/shard_map/first_scores/pallas_call | solution.py:397
  46.9 1.0 %collective-permute-start.14 = (s16[144,512]{1,0:T(8,128)(2,1)S(1)}, s16[144,512]{1,0:T(8,128)(2,1)S(1)}, u32[]{:S(2)}, u32[]{:S(2)}) collective-permute-start(s16[144,512]{1,0:T(8,128)(2,1)S(1)} %get-tuple-element.50), channel_id=1, source_target_pairs={{0,4},{4,0},{8,12},{12,8},{1,5},{5,1},{9,13},{13,9},{2,6},{6,2},{1... | collective-permute-start | bytes 442376 | tf_op jit(solution)/shard_map/ppermute | solution.py:737
  47.9 4.2 %near_scores.1 = (f32[128,512]{1,0:T(8,128)S(1)}, f32[128,512]{1,0:T(8,128)S(1)}, s16[144,512]{1,0:T(8,128)(2,1)S(1)}) custom-call(bf16[128,4096]{1,0:T(8,128)(2,1)S(1)} %get-tuple-element.44.low_ref, f32[8,128]{1,0:T(8,128)S(1)} %get-tuple-element.45.sumsq_ref, bf16[512,4096]{1,0:T(8,128)(2,1)S(1)} %copy-done.1, ...), custom_call_target="tpu_custom_call" | custom-call | flops 1610612736 | bytes 12582912 | tf_op jit(solution)/shard_map/near_scores/pallas_call | solution.py:435
  52.1 1.2 %collective-permute-start.13 = (s16[144,512]{1,0:T(8,128)(2,1)S(1)}, s16[144,512]{1,0:T(8,128)(2,1)S(1)}, u32[]{:S(2)}, u32[]{:S(2)}) collective-permute-start(s16[144,512]{1,0:T(8,128)(2,1)S(1)} %get-tuple-element.48), channel_id=1, source_target_pairs={{0,4},{4,0},{8,12},{12,8},{1,5},{5,1},{9,13},{13,9},{2,6},{6,2},{1... | collective-permute-start | bytes 442376 | tf_op jit(solution)/shard_map/ppermute | solution.py:737
  53.3 0.3 add_scores.1
  53.6 1.6 %collective-permute-start.15 = (s16[144,512]{1,0:T(8,128)(2,1)S(1)}, s16[144,512]{1,0:T(8,128)(2,1)S(1)}, u32[]{:S(2)}, u32[]{:S(2)}) collective-permute-start(s16[144,512]{1,0:T(8,128)(2,1)S(1)} %add_scores.1), channel_id=1, source_target_pairs={{0,8},{4,12},{8,0},{12,4},{1,9},{5,13},{9,1},{13,5},{2,10},{6,14},... | collective-permute-start | bytes 442376 | tf_op jit(solution)/shard_map/ppermute | solution.py:729
  55.2 5.3 %collective-permute-done.13.rest_0_ = s16[144,512]{1,0:T(8,128)(2,1)S(1)} collective-permute-done((s16[144,512]{1,0:T(8,128)(2,1)S(1)}, s16[144,512]{1,0:T(8,128)(2,1)S(1)}, u32[]{:S(2)}, u32[]{:S(2)}) %collective-permute-start.13) | collective-permute-done | bytes 147488 | tf_op jit(solution)/shard_map/ppermute | solution.py:737
  60.5 2.6 %collective-permute-done.15.rest_1_ = s16[144,512]{1,0:T(8,128)(2,1)S(1)} collective-permute-done((s16[144,512]{1,0:T(8,128)(2,1)S(1)}, s16[144,512]{1,0:T(8,128)(2,1)S(1)}, u32[]{:S(2)}, u32[]{:S(2)}) %collective-permute-start.15) | collective-permute-done | bytes 147488 | tf_op jit(solution)/shard_map/ppermute | solution.py:729
  63.1 0.5 weights.1
  63.6 0.1 collective-permute-start.17
  63.7 3.2 %collective-permute-start.19 = (bf16[80,512]{1,0:T(8,128)(2,1)S(1)}, bf16[80,512]{1,0:T(8,128)(2,1)S(1)}, u32[]{:S(2)}, u32[]{:S(2)}) collective-permute-start(bf16[80,512]{1,0:T(8,128)(2,1)S(1)} %get-tuple-element.52.rest_0_), channel_id=1, source_target_pairs={{0,4},{4,0},{8,12},{12,8},{1,5},{5,1},{9,13},{13,9},{2,6},{6,2},{1... | collective-permute-start | bytes 245768 | tf_op jit(solution)/shard_map/ppermute | solution.py:737
  66.9 0.1 collective-permute-start.16
  67.0 1.6 %collective-permute-start.20 = (bf16[64,512]{1,0:T(8,128)(2,1)S(1)}, bf16[64,512]{1,0:T(8,128)(2,1)S(1)}, u32[]{:S(2)}, u32[]{:S(2)}) collective-permute-start(bf16[64,512]{1,0:T(8,128)(2,1)S(1)} %get-tuple-element.51.rest_1_), channel_id=1, source_target_pairs={{0,4},{4,0},{8,12},{12,8},{1,5},{5,1},{9,13},{13,9},{2,6},{6,2},{1... | collective-permute-start | bytes 196616 | tf_op jit(solution)/shard_map/ppermute | solution.py:737
  68.6 2.2 %weighted_sums.2 = (f32[128,4096]{1,0:T(8,128)S(1)}, f32[128,128]{1,0:T(8,128)S(1)}, bf16[512,4096]{1,0:T(8,128)(2,1)S(1)}) custom-call(s32[1]{0:T(128)} %bitcast.me_ref, bf16[80,512]{1,0:T(8,128)(2,1)S(1)} %get-tuple-element.52.rest_0_, bf16[64,512]{1,0:T(8,128)(2,1)S(1)} %get-tuple-element.51.rest_1_, bf16[512,4096]{1,0:T(8,128)(2,1)S(1)} %copy-done.1, ...), custom_call_target="tpu_custom_call" | custom-call | flops 536870912 | bytes 4194304 | tf_op jit(solution)/shard_map/weighted_sums/pallas_call | solution.py:597
  70.8 0.4 collective-permute-done.17.piece_ref.rest_2_
  71.2 0.1 collective-permute-start.21
  71.3 1.5 %collective-permute-done.16.piece_ref.rest_3_ = bf16[64,512]{1,0:T(8,128)(2,1)S(1)} collective-permute-done((bf16[64,512]{1,0:T(8,128)(2,1)S(1)}, bf16[64,512]{1,0:T(8,128)(2,1)S(1)}, u32[]{:S(2)}, u32[]{:S(2)}) %collective-permute-start.16) | collective-permute-done | bytes 65568 | tf_op jit(solution)/shard_map/ppermute | solution.py:729
  72.8 0.5 collective-permute-start.18
  73.3 0.2 collective-permute-done.20.rest_1_
  73.5 1.6 %weighted_sums.3 = (f32[128,4096]{1,0:T(8,128)S(1)}, f32[128,128]{1,0:T(8,128)S(1)}) custom-call(s32[1]{0:T(128)} %bitcast.me_ref, bf16[80,512]{1,0:T(8,128)(2,1)S(1)} %collective-permute-done.19.rest_0_, bf16[64,512]{1,0:T(8,128)(2,1)S(1)} %collective-permute-done.20.rest_1_, bf16[80,512]{1,0:T(8,128)(2,1)S(1)} %collective-permute-done.17.piece_ref.rest_2_, ...), custom_call_target="tpu_custom_call" | custom-call | flops 1073741824 | bytes 4194304 | tf_op jit(solution)/shard_map/weighted_sums/pallas_call | solution.py:597
  75.0 0.6 collective-permute-done.21.piece_ref
  75.6 1.5 %last_sums.2 = (bf16[2,16,4224]{2,1,0:T(8,128)(2,1)S(1)}, f32[2,16,4224]{2,1,0:T(8,128)S(1)}, f32[64,128]{1,0:T(8,128)S(1)}) custom-call(s32[7]{0:T(128)S(1)} %stack.31.place_ref, bf16[80,512]{1,0:T(8,128)(2,1)S(1)} %collective-permute-done.21.piece_ref, bf16[512,4096]{1,0:T(8,128)(2,1)S(1)} %get-tuple-element.54.held_ref, ...), custom_call_target="tpu_custom_call" | custom-call | tf_op jit(solution)/shard_map/last_sums/pallas_call | solution.py:648
  77.1 0.1 collective-permute-start.24
  77.2 1.5 %last_sums.3 = (bf16[2,16,4224]{2,1,0:T(8,128)(2,1)S(1)}, f32[2,16,4224]{2,1,0:T(8,128)S(1)}) custom-call(s32[7]{0:T(128)S(1)} %stack.31.place_ref, bf16[64,512]{1,0:T(8,128)(2,1)S(1)} %collective-permute-done.18.piece_ref, bf16[512,4096]{1,0:T(8,128)(2,1)S(1)} %get-tuple-element.54.held_ref, f32[128,4096]{1,0:T(8,128)S(1)} %get-tuple-element.56.old_ref, ...), custom_call_target="tpu_custom_call" | custom-call | tf_op jit(solution)/shard_map/last_sums/pallas_call | solution.py:648
  78.7 0.6 collective-permute-start.22
  79.2 0.7 merge_core.3
  80.0 1.4 %collective-permute-start.25 = (bf16[16,4224]{1,0:T(8,128)(2,1)S(1)}, bf16[16,4224]{1,0:T(8,128)(2,1)S(1)}, u32[]{:S(2)}, u32[]{:S(2)}) collective-permute-start(bf16[16,4224]{1,0:T(8,128)(2,1)S(1)} %get-tuple-element.66), channel_id=1, source_target_pairs={{0,2},{2,0},{1,3},{3,1},{4,6},{6,4},{5,7},{7,5},{8,10},{10,8},{9,1... | collective-permute-start | bytes 405512 | tf_op jit(solution)/shard_map/ppermute | solution.py:729
  81.3 0.7 merge_core.2
  82.1 0.8 collective-permute-start.23
  82.9 3.6 %collective-permute-done.25.other_ref = bf16[16,4224]{1,0:T(8,128)(2,1)S(1)} collective-permute-done((bf16[16,4224]{1,0:T(8,128)(2,1)S(1)}, bf16[16,4224]{1,0:T(8,128)(2,1)S(1)}, u32[]{:S(2)}, u32[]{:S(2)}) %collective-permute-start.25) | collective-permute-done | bytes 135200 | tf_op jit(solution)/shard_map/ppermute | solution.py:729
  86.5 0.1 merge_last.2.rest_0_
  86.6 1.8 %collective-permute-done.23.other_ref = bf16[16,4224]{1,0:T(8,128)(2,1)S(1)} collective-permute-done((bf16[16,4224]{1,0:T(8,128)(2,1)S(1)}, bf16[16,4224]{1,0:T(8,128)(2,1)S(1)}, u32[]{:S(2)}, u32[]{:S(2)}) %collective-permute-start.23) | collective-permute-done | bytes 135200 | tf_op jit(solution)/shard_map/ppermute | solution.py:729
  88.5 0.9 %merge_last.3 = f32[32,4096]{1,0:T(8,128)} custom-call(f32[16,4224]{1,0:T(8,128)S(1)} %get-tuple-element.61.keep_ref, bf16[16,4224]{1,0:T(8,128)(2,1)S(1)} %collective-permute-done.23.other_ref, f32[16,4096]{1,0:T(8,128)S(1)} %merge_last.2.rest_0_), custom_call_target="tpu_custom_call" | custom-call | tf_op jit(solution)/shard_map/merge_last/pallas_call | solution.py:717
  (26 shorter events, 0.1 us)
Async XLA Ops:
  0.0 15.5 %copy-start.4 = (s32[128]{0:T(128)S(1)}, s32[128]{0:T(128)}, u32[]{:S(2)}) copy-start(s32[128]{0:T(128)} %param.11) | copy-start | bytes 1540
  0.0 15.9 %copy-start.2 = (bf16[2048,128]{1,0:T(8,128)(2,1)S(1)}, bf16[2048,128]{1,0:T(8,128)(2,1)}, u32[]{:S(2)}) copy-start(bf16[2048,128]{1,0:T(8,128)(2,1)} %proj_hbm.2) | copy-start | bytes 1572868
  8.5 10.8 %collective-permute-start = (s16[144,256]{1,0:T(8,128)(2,1)S(1)}, s16[144,256]{1,0:T(8,128)(2,1)S(1)}, u32[]{:S(2)}, u32[]{:S(2)}) collective-permute-start(s16[144,256]{1,0:T(8,128)(2,1)S(1)} %get-tuple-element.38), channel_id=1, source_target_pairs={{0,4},{4,8},{8,12},{12,0},{1,5},{5,9},{9,13},{13,1},{2,6},{6,10},{... | collective-permute-start | bytes 221192 | tf_op jit(solution)/shard_map/ppermute | solution.py:729
  11.6 7.8 %collective-permute-start.1 = (s16[144,256]{1,0:T(8,128)(2,1)S(1)}, s16[144,256]{1,0:T(8,128)(2,1)S(1)}, u32[]{:S(2)}, u32[]{:S(2)}) collective-permute-start(s16[144,256]{1,0:T(8,128)(2,1)S(1)} %get-tuple-element.39), channel_id=1, source_target_pairs={{0,8},{4,12},{8,0},{12,4},{1,9},{5,13},{9,1},{13,5},{2,10},{6,14},... | collective-permute-start | bytes 221192 | tf_op jit(solution)/shard_map/ppermute | solution.py:729
  14.2 5.2 %collective-permute-start.2 = (s16[144,256]{1,0:T(8,128)(2,1)S(1)}, s16[144,256]{1,0:T(8,128)(2,1)S(1)}, u32[]{:S(2)}, u32[]{:S(2)}) collective-permute-start(s16[144,256]{1,0:T(8,128)(2,1)S(1)} %get-tuple-element.40), channel_id=1, source_target_pairs={{0,12},{4,0},{8,4},{12,8},{1,13},{5,1},{9,5},{13,9},{2,14},{6,2},{... | collective-permute-start | bytes 221192 | tf_op jit(solution)/shard_map/ppermute | solution.py:729
  19.4 7.7 %collective-permute-start.4 = (bf16[128,256]{1,0:T(8,128)(2,1)S(1)}, bf16[128,256]{1,0:T(8,128)(2,1)S(1)}, u32[]{:S(2)}, u32[]{:S(2)}) collective-permute-start(bf16[128,256]{1,0:T(8,128)(2,1)S(1)} %join_x_body.1.rest_0_), channel_id=1, source_target_pairs={{0,8},{4,12},{8,0},{12,4},{1,9},{5,13},{9,1},{13,5},{2,10},{6,14},... | collective-permute-start | bytes 196616 | tf_op jit(solution)/shard_map/ppermute | solution.py:729
  21.0 6.6 %collective-permute-start.3 = (bf16[128,256]{1,0:T(8,128)(2,1)S(1)}, bf16[128,256]{1,0:T(8,128)(2,1)S(1)}, u32[]{:S(2)}, u32[]{:S(2)}) collective-permute-start(bf16[128,256]{1,0:T(8,128)(2,1)S(1)} %join_x_body.1.rest_0_), channel_id=1, source_target_pairs={{0,4},{4,0},{8,12},{12,8},{1,5},{5,1},{9,13},{13,9},{2,6},{6,2},{1... | collective-permute-start | bytes 196616 | tf_op jit(solution)/shard_map/ppermute | solution.py:737
  23.3 6.9 %collective-permute-start.6 = (s16[272,128]{1,0:T(8,128)(2,1)S(1)}, s16[272,128]{1,0:T(8,128)(2,1)S(1)}, u32[]{:S(2)}, u32[]{:S(2)}) collective-permute-start(s16[272,128]{1,0:T(8,128)(2,1)S(1)} %get-tuple-element.41), channel_id=1, source_target_pairs={{0,4},{4,8},{8,12},{12,0},{1,5},{5,9},{9,13},{13,1},{2,6},{6,10},{... | collective-permute-start | bytes 208904 | tf_op jit(solution)/shard_map/ppermute | solution.py:729
  23.3 8.0 %collective-permute-start.7 = (s16[272,128]{1,0:T(8,128)(2,1)S(1)}, s16[272,128]{1,0:T(8,128)(2,1)S(1)}, u32[]{:S(2)}, u32[]{:S(2)}) collective-permute-start(s16[272,128]{1,0:T(8,128)(2,1)S(1)} %get-tuple-element.42), channel_id=1, source_target_pairs={{0,8},{4,12},{8,0},{12,4},{1,9},{5,13},{9,1},{13,5},{2,10},{6,14},... | collective-permute-start | bytes 208904 | tf_op jit(solution)/shard_map/ppermute | solution.py:729
  24.5 6.9 %collective-permute-start.8 = (s16[272,128]{1,0:T(8,128)(2,1)S(1)}, s16[272,128]{1,0:T(8,128)(2,1)S(1)}, u32[]{:S(2)}, u32[]{:S(2)}) collective-permute-start(s16[272,128]{1,0:T(8,128)(2,1)S(1)} %get-tuple-element.43), channel_id=1, source_target_pairs={{0,12},{4,0},{8,4},{12,8},{1,13},{5,1},{9,5},{13,9},{2,14},{6,2},{... | collective-permute-start | bytes 208904 | tf_op jit(solution)/shard_map/ppermute | solution.py:729
  27.2 4.8 %collective-permute-start.5 = (bf16[128,256]{1,0:T(8,128)(2,1)S(1)}, bf16[128,256]{1,0:T(8,128)(2,1)S(1)}, u32[]{:S(2)}, u32[]{:S(2)}) collective-permute-start(bf16[128,256]{1,0:T(8,128)(2,1)S(1)} %collective-permute-done.4.rest_2_), channel_id=1, source_target_pairs={{0,4},{4,0},{8,12},{12,8},{1,5},{5,1},{9,13},{13,9},{2,6},{6,2},{1... | collective-permute-start | bytes 196616 | tf_op jit(solution)/shard_map/ppermute | solution.py:737
  27.7 9.4 %collective-permute-start.9 = (bf16[128,768]{1,0:T(8,128)(2,1)S(1)}, bf16[128,768]{1,0:T(8,128)(2,1)S(1)}, u32[]{:S(2)}, u32[]{:S(2)}) collective-permute-start(bf16[128,768]{1,0:T(8,128)(2,1)S(1)} %pack.2.refs_0_.first_ref), channel_id=1, source_target_pairs={{0,2},{2,0},{1,3},{3,1},{4,6},{6,4},{5,7},{7,5},{8,10},{10,8},{9,1... | collective-permute-start | bytes 589832 | tf_op jit(solution)/shard_map/ppermute | solution.py:729
  32.0 5.0 %collective-permute-start.10 = (bf16[128,512]{1,0:T(8,128)(2,1)S(1)}, bf16[128,512]{1,0:T(8,128)(2,1)S(1)}, u32[]{:S(2)}, u32[]{:S(2)}) collective-permute-start(bf16[128,512]{1,0:T(8,128)(2,1)S(1)} %pack.3.last_ref.after_ref), channel_id=1, source_target_pairs={{0,2},{2,0},{1,3},{3,1},{4,6},{6,4},{5,7},{7,5},{8,10},{10,8},{9,1... | collective-permute-start | bytes 393224 | tf_op jit(solution)/shard_map/ppermute | solution.py:729
  35.7 3.4 %collective-permute-start.11 = (bf16[160,1024]{1,0:T(8,128)(2,1)S(1)}, bf16[160,1024]{1,0:T(8,128)(2,1)S(1)}, u32[]{:S(2)}, u32[]{:S(2)}) collective-permute-start(bf16[160,1024]{1,0:T(8,128)(2,1)S(1)} %token_block.2.rest_0_), channel_id=1, source_target_pairs={{0,1},{1,0},{2,3},{3,2},{4,5},{5,4},{6,7},{7,6},{8,9},{9,8},{10,11... | collective-permute-start | bytes 983048 | tf_op jit(solution)/shard_map/ppermute | solution.py:729
  37.1 2.0 %copy-start = (bf16[512,4096]{1,0:T(8,128)(2,1)}, bf16[512,4096]{1,0:T(8,128)(2,1)S(1)}, u32[]{:S(2)}) copy-start(bf16[512,4096]{1,0:T(8,128)(2,1)S(1)} %hold.1.rest_0_.held_own_ref.rest_2_) | copy-start | bytes 12582916
  39.0 1.6 %collective-permute-start.12 = (bf16[160,1024]{1,0:T(8,128)(2,1)S(1)}, bf16[160,1024]{1,0:T(8,128)(2,1)S(1)}, u32[]{:S(2)}, u32[]{:S(2)}) collective-permute-start(bf16[160,1024]{1,0:T(8,128)(2,1)S(1)} %token_block.3.rest_1_), channel_id=1, source_target_pairs={{0,1},{1,0},{2,3},{3,2},{4,5},{5,4},{6,7},{7,6},{8,9},{9,8},{10,11... | collective-permute-start | bytes 983048 | tf_op jit(solution)/shard_map/ppermute | solution.py:729
  39.1 8.7 %copy-start.1 = (bf16[512,4096]{1,0:T(8,128)(2,1)S(1)}, bf16[512,4096]{1,0:T(8,128)(2,1)}, u32[]{:S(2)}) copy-start(bf16[512,4096]{1,0:T(8,128)(2,1)} %copy-done) | copy-start | bytes 12582916
  46.9 6.4 %collective-permute-start.14 = (s16[144,512]{1,0:T(8,128)(2,1)S(1)}, s16[144,512]{1,0:T(8,128)(2,1)S(1)}, u32[]{:S(2)}, u32[]{:S(2)}) collective-permute-start(s16[144,512]{1,0:T(8,128)(2,1)S(1)} %get-tuple-element.50), channel_id=1, source_target_pairs={{0,4},{4,0},{8,12},{12,8},{1,5},{5,1},{9,13},{13,9},{2,6},{6,2},{1... | collective-permute-start | bytes 442376 | tf_op jit(solution)/shard_map/ppermute | solution.py:737
  47.9 15.2 %copy-start.3 = (s32[2048]{0:T(1024)S(1)}, s32[2048]{0:T(1024)}, u32[]{:S(2)}) copy-start(s32[2048]{0:T(1024)} %param.13) | copy-start | bytes 24580
  52.1 8.4 %collective-permute-start.13 = (s16[144,512]{1,0:T(8,128)(2,1)S(1)}, s16[144,512]{1,0:T(8,128)(2,1)S(1)}, u32[]{:S(2)}, u32[]{:S(2)}) collective-permute-start(s16[144,512]{1,0:T(8,128)(2,1)S(1)} %get-tuple-element.48), channel_id=1, source_target_pairs={{0,4},{4,0},{8,12},{12,8},{1,5},{5,1},{9,13},{13,9},{2,6},{6,2},{1... | collective-permute-start | bytes 442376 | tf_op jit(solution)/shard_map/ppermute | solution.py:737
  53.6 9.5 %collective-permute-start.15 = (s16[144,512]{1,0:T(8,128)(2,1)S(1)}, s16[144,512]{1,0:T(8,128)(2,1)S(1)}, u32[]{:S(2)}, u32[]{:S(2)}) collective-permute-start(s16[144,512]{1,0:T(8,128)(2,1)S(1)} %add_scores.1), channel_id=1, source_target_pairs={{0,8},{4,12},{8,0},{12,4},{1,9},{5,13},{9,1},{13,5},{2,10},{6,14},... | collective-permute-start | bytes 442376 | tf_op jit(solution)/shard_map/ppermute | solution.py:729
  63.6 7.6 %collective-permute-start.17 = (bf16[80,512]{1,0:T(8,128)(2,1)S(1)}, bf16[80,512]{1,0:T(8,128)(2,1)S(1)}, u32[]{:S(2)}, u32[]{:S(2)}) collective-permute-start(bf16[80,512]{1,0:T(8,128)(2,1)S(1)} %get-tuple-element.52.rest_0_), channel_id=1, source_target_pairs={{0,8},{4,12},{8,0},{12,4},{1,9},{5,13},{9,1},{13,5},{2,10},{6,14},... | collective-permute-start | bytes 245768 | tf_op jit(solution)/shard_map/ppermute | solution.py:729
  63.7 9.8 %collective-permute-start.19 = (bf16[80,512]{1,0:T(8,128)(2,1)S(1)}, bf16[80,512]{1,0:T(8,128)(2,1)S(1)}, u32[]{:S(2)}, u32[]{:S(2)}) collective-permute-start(bf16[80,512]{1,0:T(8,128)(2,1)S(1)} %get-tuple-element.52.rest_0_), channel_id=1, source_target_pairs={{0,4},{4,0},{8,12},{12,8},{1,5},{5,1},{9,13},{13,9},{2,6},{6,2},{1... | collective-permute-start | bytes 245768 | tf_op jit(solution)/shard_map/ppermute | solution.py:737
  66.9 5.9 %collective-permute-start.16 = (bf16[64,512]{1,0:T(8,128)(2,1)S(1)}, bf16[64,512]{1,0:T(8,128)(2,1)S(1)}, u32[]{:S(2)}, u32[]{:S(2)}) collective-permute-start(bf16[64,512]{1,0:T(8,128)(2,1)S(1)} %get-tuple-element.51.rest_1_), channel_id=1, source_target_pairs={{0,8},{4,12},{8,0},{12,4},{1,9},{5,13},{9,1},{13,5},{2,10},{6,14},... | collective-permute-start | bytes 196616 | tf_op jit(solution)/shard_map/ppermute | solution.py:729
  67.0 6.5 %collective-permute-start.20 = (bf16[64,512]{1,0:T(8,128)(2,1)S(1)}, bf16[64,512]{1,0:T(8,128)(2,1)S(1)}, u32[]{:S(2)}, u32[]{:S(2)}) collective-permute-start(bf16[64,512]{1,0:T(8,128)(2,1)S(1)} %get-tuple-element.51.rest_1_), channel_id=1, source_target_pairs={{0,4},{4,0},{8,12},{12,8},{1,5},{5,1},{9,13},{13,9},{2,6},{6,2},{1... | collective-permute-start | bytes 196616 | tf_op jit(solution)/shard_map/ppermute | solution.py:737
  71.2 4.4 %collective-permute-start.21 = (bf16[80,512]{1,0:T(8,128)(2,1)S(1)}, bf16[80,512]{1,0:T(8,128)(2,1)S(1)}, u32[]{:S(2)}, u32[]{:S(2)}) collective-permute-start(bf16[80,512]{1,0:T(8,128)(2,1)S(1)} %relay.2.rest_0_), channel_id=1, source_target_pairs={{0,4},{4,0},{8,12},{12,8},{1,5},{5,1},{9,13},{13,9},{2,6},{6,2},{1... | collective-permute-start | bytes 245768 | tf_op jit(solution)/shard_map/ppermute | solution.py:737
  72.8 4.4 %collective-permute-start.18 = (bf16[64,512]{1,0:T(8,128)(2,1)S(1)}, bf16[64,512]{1,0:T(8,128)(2,1)S(1)}, u32[]{:S(2)}, u32[]{:S(2)}) collective-permute-start(bf16[64,512]{1,0:T(8,128)(2,1)S(1)} %relay.3.rest_7_), channel_id=1, source_target_pairs={{0,4},{4,0},{8,12},{12,8},{1,5},{5,1},{9,13},{13,9},{2,6},{6,2},{1... | collective-permute-start | bytes 196616 | tf_op jit(solution)/shard_map/ppermute | solution.py:737
  77.1 2.1 %collective-permute-start.24 = (bf16[2,16,4224]{2,1,0:T(8,128)(2,1)S(1)}, bf16[2,16,4224]{2,1,0:T(8,128)(2,1)S(1)}, u32[]{:S(2)}, u32[]{:S(2)}) collective-permute-start(bf16[2,16,4224]{2,1,0:T(8,128)(2,1)S(1)} %get-tuple-element.64), channel_id=1, source_target_pairs={{0,1},{1,0},{2,3},{3,2},{4,5},{5,4},{6,7},{7,6},{8,9},{9,8},{10,11... | collective-permute-start | bytes 811016 | tf_op jit(solution)/shard_map/ppermute | solution.py:729
  78.7 2.6 %collective-permute-start.22 = (bf16[2,16,4224]{2,1,0:T(8,128)(2,1)S(1)}, bf16[2,16,4224]{2,1,0:T(8,128)(2,1)S(1)}, u32[]{:S(2)}, u32[]{:S(2)}) collective-permute-start(bf16[2,16,4224]{2,1,0:T(8,128)(2,1)S(1)} %get-tuple-element.60), channel_id=1, source_target_pairs={{0,1},{1,0},{2,3},{3,2},{4,5},{5,4},{6,7},{7,6},{8,9},{9,8},{10,11... | collective-permute-start | bytes 811016 | tf_op jit(solution)/shard_map/ppermute | solution.py:729
  80.0 6.5 %collective-permute-start.25 = (bf16[16,4224]{1,0:T(8,128)(2,1)S(1)}, bf16[16,4224]{1,0:T(8,128)(2,1)S(1)}, u32[]{:S(2)}, u32[]{:S(2)}) collective-permute-start(bf16[16,4224]{1,0:T(8,128)(2,1)S(1)} %get-tuple-element.66), channel_id=1, source_target_pairs={{0,2},{2,0},{1,3},{3,1},{4,6},{6,4},{5,7},{7,5},{8,10},{10,8},{9,1... | collective-permute-start | bytes 405512 | tf_op jit(solution)/shard_map/ppermute | solution.py:729
  82.1 6.4 %collective-permute-start.23 = (bf16[16,4224]{1,0:T(8,128)(2,1)S(1)}, bf16[16,4224]{1,0:T(8,128)(2,1)S(1)}, u32[]{:S(2)}, u32[]{:S(2)}) collective-permute-start(bf16[16,4224]{1,0:T(8,128)(2,1)S(1)} %get-tuple-element.62), channel_id=1, source_target_pairs={{0,2},{2,0},{1,3},{3,1},{4,6},{6,4},{5,7},{7,5},{8,10},{10,8},{9,1... | collective-permute-start | bytes 405512 | tf_op jit(solution)/shard_map/ppermute | solution.py:729

commit v2 on v1

--- a/solution.py
+++ b/solution.py
@@ -246,8 +246,7 @@
     )(*pieces, *more)
 
 
-def token_body(width, me_ref, first_ref, last_ref, *rest):
-    out_ref = rest[-1]
+def token_body(width, me_ref, first_ref, last_ref, out_ref):
     rank = first_ref.shape[0]
     size = last_ref.shape[1] // 2
     pieces = [first_ref[:, n * size:(n + 1) * size] for n in range(3)] + [last_ref[:, :size]]
@@ -257,17 +256,17 @@
         out_ref[rank:, n * size:(n + 1) * size] = last_ref[n * width:(n + 1) * width, size:]
 
 
-def token_block(me, first, last, width, after=()):
+def token_block(me, first, last, width):
     rank, size = last.shape
     return pl.pallas_call(
         functools.partial(token_body, width),
         grid_spec=pltpu.PrefetchScalarGridSpec(
-            num_scalar_prefetch=1, grid=(), in_specs=[VMEM] * 2 + [ANY] * len(after), out_specs=VMEM
+            num_scalar_prefetch=1, grid=(), in_specs=[VMEM] * 2, out_specs=VMEM
         ),
         out_shape=jax.ShapeDtypeStruct((rank + width, rank // width * size // 2), BF16),
         compiler_params=params(),
         name="token_block",
-    )(me, first, last, *after)
+    )(me, first, last)
 
 
 def turn(row):
@@ -311,31 +310,6 @@
     level = scale_level(jnp.max(jnp.abs(value), axis=0, keepdims=True))
     out_ref[:passages, :] = to_short(value * (FULL / value_of(level)))
     out_ref[passages:, :] = code_rows([level, coarse, fine], quarter).astype(jnp.int32).astype(jnp.int16)
-
-
-def hold_body(me_ref, corpus_hbm, after_ref, held_ref, sem):
-    size = held_ref.shape[0]
-    load = pltpu.make_async_copy(corpus_hbm.at[pl.ds(pl.multiple_of(me_ref[0] * size, size), size), :], held_ref, sem)
-    load.start()
-    load.wait()
-
-
-def hold(me, corpus, nfeat, after):
-    rows, depth = corpus.shape
-    return pl.pallas_call(
-        hold_body,
-        grid_spec=pltpu.PrefetchScalarGridSpec(
-            num_scalar_prefetch=1,
-            grid=(),
-            in_specs=[HBM, ANY],
-            out_specs=VMEM,
-            scratch_shapes=[pltpu.SemaphoreType.DMA],
-        ),
-        out_shape=jax.ShapeDtypeStruct((rows // nfeat, depth), BF16),
-        compiler_params=params(34),
-        cost_estimate=pl.CostEstimate(flops=0, bytes_accessed=4 * rows // nfeat * depth, transcendentals=0),
-        name="hold",
-    )(me, corpus, after)
 
 
 def first_body(nblk, passages, place_ref, starts_ref, ends_ref, *rest):
@@ -353,29 +327,30 @@
     width = height - rank
     for n in range(nblk):
         tokens[:, pl.ds(pl.multiple_of(place_ref[3 + n] * tok, tok), tok)] = blocks[n][...]
-    group = LANES // width
+    group = 8
     window = -(-group * LONGEST // LANES) * LANES + LANES
 
     def step(i, carry):
-        first = i * group
+        first = pl.multiple_of(i * group, group)
         base = jnp.minimum((starts_ref[first] // LANES) * LANES, nblk * tok - window)
         here = pl.ds(pl.multiple_of(base, LANES), window)
-        g_part = tokens[rank:, here]
-        token = base + lax.broadcasted_iota(jnp.int32, (CODES, window), 1)
-        stack = []
+        token = base + lax.broadcasted_iota(jnp.int32, (group, window), 1)
+        row = lax.broadcasted_iota(jnp.int32, (group, window), 0)
+        start = jnp.zeros((group, window), jnp.int32)
+        end = start
         for q in range(group):
-            inside = (token >= starts_ref[first + q]) & (token < ends_ref[first + q])
-            member = jnp.where(inside, 1.0, 0.0).astype(BF16)
-            stack.append(g_part * jnp.concatenate([member] * (width // CODES), axis=0))
-        grad[pl.ds(pl.multiple_of(i * LANES, LANES), LANES), :] = lax.dot_general(
-            jnp.concatenate(stack, axis=0), tokens[:rank, here], (((1,), (1,)), ((), ())), preferred_element_type=F32
-        )
+            start = jnp.where(row == q, starts_ref[first + q], start)
+            end = jnp.where(row == q, ends_ref[first + q], end)
+        member = jnp.where((token >= start) & (token < end), 1.0, 0.0)
+        terms = tokens[rank:, here].astype(F32)[:, None, :] * member[None, :, :]
+        product = turned_dot(terms.reshape(width * group, window).astype(BF16), tokens[:rank, here])
+        grad[:, pl.ds(first, group), :] = product.reshape(width, group, rank)
         return carry
 
-    lax.fori_loop(0, passages // group, step, 0, unroll=4)
+    lax.fori_loop(0, passages // group, step, 0, unroll=2)
     squares = jnp.zeros((passages, LANES), F32)
     for a in range(width):
-        column = grad[pl.ds(a, passages, stride=width), :]
+        column = grad[a]
         squares = squares + column * column
         low[:, a * LANES:(a + 1) * LANES] = column.astype(BF16)
     sumsq = jnp.sum(jnp.transpose(squares), axis=0, keepdims=True)
@@ -404,7 +379,7 @@
             scratch_shapes=[
                 pltpu.VMEM((1, quarter, depth), BF16),
                 pltpu.VMEM((height, nblk * tok), BF16),
-                pltpu.VMEM((passages * depth // LANES, LANES), F32),
+                pltpu.VMEM((depth // LANES, passages, LANES), F32),
                 pltpu.SemaphoreType.DMA((1,)),
                 pltpu.SemaphoreType.DMA((nfeat - 2,)),
             ],
@@ -421,27 +396,75 @@
     )(place, starts, ends, *blocks, corpus)
 
 
-def near_body(low_ref, sumsq_ref, held_own_ref, held_ref, own_ref, across_ref, beside_ref):
+def near_body(low_ref, sumsq_ref, held_ref, across_ref, beside_ref):
     sumsq = sumsq_ref[0:1, :]
     norm = turn(lax.rsqrt(norm_of(sumsq)))
     write_scores(norm * turned_dot(low_ref[...], held_ref[0]), sumsq, beside_ref)
     across_ref[...] = norm * turned_dot(low_ref[...], held_ref[1])
-    own_ref[...] = norm * turned_dot(low_ref[...], held_own_ref[...])
-
-
-def near_scores(low, sumsq, held_own, held):
+
+
+def near_scores(low, sumsq, held):
     passages, depth = low.shape
     quarter = held.shape[1]
     return pl.pallas_call(
         near_body,
-        in_specs=[VMEM] * 4,
-        out_specs=[VMEM] * 3,
-        out_shape=[jax.ShapeDtypeStruct((passages, quarter), F32)] * 2
-        + [jax.ShapeDtypeStruct((passages + CODES, quarter), jnp.int16)],
+        in_specs=[VMEM] * 3,
+        out_specs=[VMEM] * 2,
+        out_shape=[
+            jax.ShapeDtypeStruct((passages, quarter), F32),
+            jax.ShapeDtypeStruct((passages + CODES, quarter), jnp.int16),
+        ],
         compiler_params=params(8),
-        cost_estimate=pl.CostEstimate(flops=6 * passages * depth * quarter, bytes_accessed=6 * quarter * depth, transcendentals=0),
+        cost_estimate=pl.CostEstimate(flops=4 * passages * depth * quarter, bytes_accessed=4 * quarter * depth, transcendentals=0),
         name="near_scores",
-    )(low, sumsq, held_own, held)
+    )(low, sumsq, held)
+
+
+def own_body(me_ref, low_ref, sumsq_ref, corpus_hbm, after_ref, own_ref, held_ref, sems):
+    sources = sources_of(me_ref[0])
+    loads = loads_of(corpus_hbm, held_ref, sems, [sources[0], sources[3]], 1)
+    for load in loads:
+        load.start()
+    norm = turn(lax.rsqrt(norm_of(sumsq_ref[0:1, :])))
+    loads[0].wait()
+    own_ref[...] = norm * turned_dot(low_ref[...], held_ref[0])
+    loads[1].wait()
+
+
+def own_scores(me, low, sumsq, corpus, nfeat, after):
+    passages, depth = low.shape
+    quarter = corpus.shape[0] // nfeat
+    return pl.pallas_call(
+        own_body,
+        grid_spec=pltpu.PrefetchScalarGridSpec(
+            num_scalar_prefetch=1,
+            grid=(),
+            in_specs=[VMEM] * 2 + [HBM, ANY],
+            out_specs=[VMEM] * 2,
+            scratch_shapes=[pltpu.SemaphoreType.DMA((2,))],
+        ),
+        out_shape=[jax.ShapeDtypeStruct((passages, quarter), F32), jax.ShapeDtypeStruct((2, quarter, depth), BF16)],
+        compiler_params=params(30),
+        cost_estimate=pl.CostEstimate(flops=2 * passages * depth * quarter, bytes_accessed=4 * quarter * depth, transcendentals=0),
+        name="own_scores",
+    )(me, low, sumsq, corpus, after)
+
+
+def open_body(message_ref, after_ref, score_ref, sumsq_ref):
+    score_ref[...], sumsq = read_scores(message_ref)
+    sumsq_ref[...] = jnp.broadcast_to(sumsq, sumsq_ref.shape)
+
+
+def open_scores(message, after):
+    passages, size = message.shape[0] - CODES, message.shape[1]
+    return pl.pallas_call(
+        open_body,
+        in_specs=[VMEM, ANY],
+        out_specs=[VMEM] * 2,
+        out_shape=[jax.ShapeDtypeStruct((passages, size), F32), jax.ShapeDtypeStruct((8, passages), F32)],
+        compiler_params=params(8),
+        name="open_scores",
+    )(message, after)
 
 
 def split3(value):
@@ -498,10 +521,10 @@
     return jnp.concatenate([value[(2 * n + half) * size:(2 * n + half + 1) * size] for n in range(owners)], axis=0)
 
 
-def weight_body(owners, me_ref, owner_ref, own_ref, sumsq_ref, *rest):
-    *messages, first_ref, second_ref = rest
+def weight_body(owners, me_ref, owner_ref, own_ref, sumsq_ref, open_ref, open_sumsq_ref, message_ref, first_ref, second_ref, whole_ref):
     passages, rows = own_ref.shape
-    value, _ = add_terms([(own_ref[...], sumsq_ref[0:1, :])] + [read_scores(message) for message in messages])
+    opened = open_ref[...], open_sumsq_ref[0:1, :]
+    value, _ = add_terms([(own_ref[...], sumsq_ref[0:1, :]), opened, read_scores(message_ref)])
     score = value * (2.5 / math.sqrt(K))
     owner = owner_ref[:, pl.ds(pl.multiple_of(me_ref[0] * rows, rows), rows)]
     owned = owner == lax.broadcasted_iota(jnp.int32, (passages, rows), 0)
@@ -512,23 +535,27 @@
     first_ref[:passages // 2, :] = half_of(weight, 0, owners).astype(BF16)
     first_ref[passages // 2:, :] = code_rows(split3(turn_back(top)) + split3(turn_back(total)), rows).astype(BF16)
     second_ref[...] = half_of(weight, 1, owners).astype(BF16)
-
-
-def weights_of(me, owner, own, sumsq, messages, owners):
+    size = first_ref.shape[0]
+    whole_ref[:size, :] = first_ref[...]
+    whole_ref[size:, :] = second_ref[...]
+
+
+def weights_of(me, owner, own, sumsq, opened, message, owners):
     passages, rows = own.shape
     return pl.pallas_call(
         functools.partial(weight_body, owners),
         grid_spec=pltpu.PrefetchScalarGridSpec(
-            num_scalar_prefetch=1, grid=(), in_specs=[VMEM] * (3 + len(messages)), out_specs=[VMEM] * 2
+            num_scalar_prefetch=1, grid=(), in_specs=[VMEM] * 6, out_specs=[VMEM] * 3
         ),
         out_shape=[
             jax.ShapeDtypeStruct((passages // 2 + CODES, rows), BF16),
             jax.ShapeDtypeStruct((passages // 2, rows), BF16),
+            jax.ShapeDtypeStruct((passages + CODES, rows), BF16),
         ],
         compiler_params=params(8),
         cost_estimate=pl.CostEstimate(flops=8 * passages * rows, bytes_accessed=16 * passages * rows, transcendentals=passages * rows),
         name="weights",
-    )(me, owner.reshape(1, -1), own, sumsq, *messages)
+    )(me, owner.reshape(1, -1), own, sumsq, *opened, message)
 
 
 def running_stats(owners, codes, before):
@@ -567,81 +594,78 @@
     return jnp.where(lane == 0, top, total)
 
 
-def sums_body(owners, sources, started, fetch, me_ref, *rest):
-    count = 2 * sources
-    parts, held_ref, rest = rest[:count], rest[count], rest[count + 1:]
-    before, rest = rest[:2 * started], rest[2 * started:]
-    if fetch:
-        corpus_hbm, acc_ref, stats_ref, fetch_ref, sem = rest
-        size = fetch_ref.shape[0]
-        at = pl.multiple_of(sources_of(me_ref[0])[fetch] * size, size)
-        load = pltpu.make_async_copy(corpus_hbm.at[pl.ds(at, size), :], fetch_ref, sem)
-        load.start()
-    else:
-        acc_ref, stats_ref = rest[-2:]
-    pieces = [parts[2 * n:2 * n + 2] for n in range(sources)]
-    quarters = [held_ref] if sources == 1 else [held_ref.at[n] for n in range(sources)]
-    top, total, factors = running_stats(owners, parts[::2], before[1] if before else None)
+def sums_body(owners, counts, started, *rest):
+    pieces = []
+    for count in counts:
+        parts, rest = rest[:count], rest[count:]
+        if count == 1:
+            size = (parts[0].shape[0] - CODES) // 2
+            parts = parts[0].at[pl.ds(0, size + CODES), :], parts[0].at[pl.ds(size + CODES, size), :]
+        pieces.append(parts)
+    held_ref, rest = rest[0], rest[1:]
+    before, acc_ref, stats_ref = rest[:2 * started], *rest[-2:]
+    quarters = [held_ref.at[n] for n in range(len(counts))]
+    codes = [piece[0] for piece in pieces]
+    top, total, factors = running_stats(owners, codes, before[1] if before else None)
     weights = [jnp.concatenate([piece[0][:piece[1].shape[0], :], piece[1][...]], axis=0) for piece in pieces]
     add_sums(weights, quarters, factors, before[0] if before else None, acc_ref)
     stats_ref[...] = stats_tile(top, total)
-    if fetch:
-        load.wait()
-
-
-def weighted_sums(me, owners, pieces, held, before, corpus=None, fetch=0, after=()):
+
+
+def weighted_sums(owners, pieces, held, before, after=()):
     parts = [part for piece in pieces for part in piece]
-    passages = 2 * parts[1].shape[0]
-    quarter, depth = held.shape[-2:]
-    fetched = [jax.ShapeDtypeStruct((quarter, depth), BF16)] if fetch else []
-    return pl.pallas_call(
-        functools.partial(sums_body, owners, len(pieces), len(before) // 2, fetch),
-        grid_spec=pltpu.PrefetchScalarGridSpec(
-            num_scalar_prefetch=1,
-            grid=(),
-            in_specs=[VMEM] * (len(parts) + 1 + len(before)) + [HBM] * len(fetched) + [ANY] * len(after),
-            out_specs=[VMEM] * (2 + len(fetched)),
-            scratch_shapes=[pltpu.SemaphoreType.DMA] * len(fetched),
-        ),
-        out_shape=[jax.ShapeDtypeStruct((passages, depth), F32), jax.ShapeDtypeStruct((passages, LANES), F32)] + fetched,
-        compiler_params=params(30 if fetch else 8),
+    passages = 2 * pieces[-1][1].shape[0]
+    _, quarter, depth = held.shape
+    return pl.pallas_call(
+        functools.partial(sums_body, owners, tuple(len(piece) for piece in pieces), len(before) // 2),
+        in_specs=[VMEM] * (len(parts) + 1 + len(before)) + [ANY] * len(after),
+        out_specs=[VMEM] * 2,
+        out_shape=[jax.ShapeDtypeStruct((passages, depth), F32), jax.ShapeDtypeStruct((passages, LANES), F32)],
+        compiler_params=params(8),
         cost_estimate=pl.CostEstimate(flops=2 * passages * quarter * len(pieces) * depth, bytes_accessed=2 * quarter * depth, transcendentals=0),
         name="weighted_sums",
-    )(me, *parts, held, *before, *([corpus] if fetch else []), *after)
+    )(*parts, held, *before, *after)
 
 
 def last_sums_body(half, nrows, nsub, place_ref, piece_ref, held_ref, old_ref, stats_ref, *rest):
-    send_ref, keep_ref = rest[:2] if half == 0 else rest[-3:-1]
-    acc = rest[-1]
+    send_ref, keep_ref, later_ref, columns_ref = rest if half == 0 else rest[:2] + (None, rest[2])
     span = send_ref.shape[1]
-    passages, depth = acc.shape
+    depth = held_ref.shape[2]
+    passages = columns_ref.shape[0]
     core = place_ref[1]
     if half == 0:
         top, total, factors = running_stats(nrows * nsub, [piece_ref], stats_ref)
         share = 1.0 / jnp.maximum(total, 1e-30)
         level = top + jnp.log(jnp.maximum(total, 1e-30))
         columns = [factors[0] * share, factors[1] * share, level]
-        lane = lax.broadcasted_iota(jnp.int32, (passages, LANES), 1)
-        later = [column[passages:] for column in columns]
-        rest[2][...] = jnp.where(lane == 0, later[0], jnp.where(lane == 1, later[1], later[2]))
-        columns = [column[:passages] for column in columns]
+        lane = lax.broadcasted_iota(jnp.int32, (2 * passages, LANES), 1)
+        tile = jnp.where(lane == 0, columns[0], jnp.where(lane == 1, columns[1], columns[2]))
+        columns_ref[...] = tile[:passages]
+        later_ref[...] = tile[passages:]
     else:
-        columns = [stats_ref[:, n:n + 1] for n in range(3)]
-    old = old_ref.at[pl.ds(half * passages, passages), :]
-    add_sums([piece_ref[:passages, :]], [held_ref], columns[:2], old, acc)
-    mine = [pl.multiple_of((x * nsub + core) * span, span) for x in range(nrows)]
-    other = [pl.multiple_of((x * nsub + (nsub - 1 - core)) * span, span) for x in range(nrows)]
+        columns_ref[...] = stats_ref[...]
+    starts = [x * nsub + (nsub - 1 - core) for x in range(nrows)] + [x * nsub + core for x in range(nrows)]
+    rows = [pl.ds(pl.multiple_of(n * span, span), span) for n in starts]
+    old_rows = [pl.ds(pl.multiple_of(half * passages + n * span, span), span) for n in starts]
+    weight = jnp.concatenate([piece_ref[r, :] for r in rows], axis=0)
+    columns = jnp.concatenate([columns_ref[r, :] for r in rows], axis=0)
+    new_factor, old_factor, level = columns[:, 0:1], columns[:, 1:2], columns[:, 2:3]
+    step = 512
+    for at in range(0, depth, step):
+        here = slice(at, at + step)
+        old = jnp.concatenate([old_ref[r, here] for r in old_rows], axis=0)
+        value = new_factor * jnp.dot(weight, held_ref[1, :, here], preferred_element_type=F32) + old_factor * old
+        for x in range(nrows):
+            send_ref[x, :, here] = value[x * span:(x + 1) * span].astype(BF16)
+            keep_ref[x, :, here] = value[(nrows + x) * span:(nrows + x + 1) * span]
+    level = jnp.broadcast_to(level, (passages, LANES))
     for x in range(nrows):
-        keep_ref[x, :, :depth] = acc[pl.ds(mine[x], span), :]
-        send_ref[x, :, :depth] = acc[pl.ds(other[x], span), :].astype(BF16)
-    acc[:, 0:LANES] = jnp.broadcast_to(columns[2], (passages, LANES))
-    for x in range(nrows):
-        keep_ref[x, :, depth:] = acc[pl.ds(mine[x], span), 0:LANES]
-        send_ref[x, :, depth:] = pack_level(acc[pl.ds(other[x], span), 0:LANES])
+        send_ref[x, :, depth:] = pack_level(level[x * span:(x + 1) * span])
+        keep_ref[x, :, depth:] = level[(nrows + x) * span:(nrows + x + 1) * span]
 
 
 def last_sums(place, half, piece, held, sums, stats, nrows, nsub):
-    quarter, depth = held.shape
+    _, quarter, depth = held.shape
     passages = sums.shape[0] // 2
     shape = (nrows, passages // (nrows * nsub), depth + LANES)
     ratios = [jax.ShapeDtypeStruct((passages, LANES), F32)] * (1 - half)
@@ -652,7 +676,7 @@
             grid=(),
             in_specs=[VMEM] * 4,
             out_specs=[VMEM] * (3 - half),
-            scratch_shapes=[pltpu.VMEM((passages, depth), F32)],
+            scratch_shapes=[pltpu.VMEM((passages, LANES), F32)],
         ),
         out_shape=[jax.ShapeDtypeStruct(shape, BF16), jax.ShapeDtypeStruct(shape, F32)] + ratios,
         compiler_params=params(),
@@ -756,16 +780,15 @@
     )(piece, *after)
 
 
-def gather_tokens(me, g_own, g_others, piece, meanwhile):
+def gather_tokens(me, g_own, g_others, piece):
     across, beside = shift(piece, "feat", 2), to_pair(piece)
     first = pack([piece, beside, across])
     g_low = join(join_g_body, [g_own] + g_others, (first,))
     last = pack([to_pair(across)], [g_low])
-    done = meanwhile(last)
     width = g_low.shape[0]
     here = token_block(me, first, last, width)
-    there = token_block(me, shift(first, "rows", 1), shift(last, "rows", 1), width, (done,))
-    return [here, there, shift(here, "sub", 1), shift(there, "sub", 1)], [(0, 0), (1, 0), (0, 1), (1, 1)], done
+    there = token_block(me, shift(first, "rows", 1), shift(last, "rows", 1), width)
+    return [here, there, shift(here, "sub", 1), shift(there, "sub", 1)], [(0, 0), (1, 0), (0, 1), (1, 1)]
 
 
 def fast(activations, out_grads, proj_in, proj_out, lengths, corpus, owner):
@@ -777,25 +800,24 @@
     x_parts = project_x(me, activations, proj_in, nfeat)
     g_parts = project_g(me, out_grads, proj_out, nfeat, starts, ends)
     x_piece = join(join_x_body, scatter_parts(x_parts), g_parts[:1])
-    blocks, back, held_own = gather_tokens(
-        me, g_parts[0], scatter_parts(g_parts)[1:], x_piece, lambda after: hold(me, corpus, nfeat, after)
-    )
+    blocks, back = gather_tokens(me, g_parts[0], scatter_parts(g_parts)[1:], x_piece)
     order = [(row ^ d) * nsub + (sub ^ c) for d, c in back]
     place = jnp.stack([feat, sub, row] + order)
     message, sumsq, low, held = first_scores(place, starts, ends, blocks, corpus, nfeat)
-    own, across, beside = near_scores(low, sumsq, held_own, held)
+    across, beside = near_scores(low, sumsq, held)
     across = add_scores(across, sumsq, to_pair(message))
+    own, held_far = own_scores(me, low, sumsq, corpus, nfeat, across)
     owners = nrows * nsub
-    messages = [to_pair(beside), shift(across, "feat", 2)]
-    pieces = weights_of(me, owner, own, sumsq, messages, owners)
-    beside, across = [to_pair(p) for p in pieces], [shift(p, "feat", 2) for p in pieces]
-    *sums, fetched = weighted_sums(me, owners, [pieces], held_own, (), corpus, 3)
+    opened = open_scores(to_pair(beside), own)
+    *pieces, whole_piece = weights_of(me, owner, own, sumsq, opened, shift(across, "feat", 2), owners)
+    across, beside = [shift(p, "feat", 2) for p in pieces], [to_pair(whole_piece)]
+    sums = weighted_sums(owners, [pieces], held_far, ())
     relayed = [relay(across[0], sums[1])]
     relayed.append(relay(across[1], relayed[0]))
     last = [to_pair(p) for p in relayed]
-    sums = weighted_sums(me, owners, [beside, across], held, sums, after=relayed[1:])
-    *first, ratios = last_sums(place, 0, last[0], fetched, *sums, nrows, nsub)
-    halves = [first, last_sums(place, 1, last[1], fetched, sums[0], ratios, nrows, nsub)]
+    sums = weighted_sums(owners, [beside, across], held, sums, after=relayed[1:])
+    *first, ratios = last_sums(place, 0, last[0], held_far, *sums, nrows, nsub)
+    halves = [first, last_sums(place, 1, last[1], held_far, sums[0], ratios, nrows, nsub)]
     ended = [merge_core(place, keep, shift(send, "sub", 1)) for send, keep in halves]
     out = ()
     for send, keep in ended:

time: 89.6 us -> 88 us (0.982)
  waiting for transfers between devices: 21.5 us -> 24.9 us
  local copies, waits for them, and re-layouts: 2.17 us -> 0.21 us
  Pallas kernels: 34.7 us -> 32.8 us
  starting transfers between devices: 30.4 us -> 29.4 us
    ppermute x18, waiting for transfers between devices: 14.8 us -> 22.4 us  [shift(): lax.ppermute(value, axis, [(i, (i + by) % count) for i in range(count)])]
    ppermute x8 -> x7, waiting for transfers between devices: 6.68 us -> 2.46 us  [to_pair(): lax.ppermute(value, 'feat', [(i, i ^ 1) for i in range(lax.axis_size('fea...]
    ppermute x8 -> x7, starting transfers between devices: 10.3 us -> 6.24 us  [to_pair(): lax.ppermute(value, 'feat', [(i, i ^ 1) for i in range(lax.axis_size('fea...]
    ppermute x18, starting transfers between devices: 20.1 us -> 23.1 us  [shift(): lax.ppermute(value, axis, [(i, (i + by) % count) for i in range(count)])]
    unnamed x10 -> x6, local copies, waits for them, and re-layouts: 1.97 us -> 0.01 us
    pallas_call x4 -> x5, Pallas kernels: 10.2 us -> 8.79 us  [the longest x1 3.7 us: own_scores(): pl.pallas_call(own_body, grid_spec=pltpu.PrefetchScalarGridSpec(num_scala...]
  transfers between devices with their start and end apart: 26 -> 25, of which waited for: 13 -> 12; matrix products, arithmetic and copies ran while one was open for 1% -> 1% of each run, Pallas kernels for 21% -> 19%
where the time goes in v2:
time: 88 us; the launch traced here: 87.8 us
  Pallas kernels  32.8 us (37%)
  starting transfers between devices  29.4 us (33%)
  waiting for transfers between devices  24.9 us (28%)
    ppermute x18, starting transfers between devices, shift(): lax.ppermute(value, axis, [(i, (i + by) % count) for i in range(count)])  23.1 us
    ppermute x18, waiting for transfers between devices, shift(): lax.ppermute(value, axis, [(i, (i + by) % count) for i in range(count)])  22.4 us
    pallas_call x1, Pallas kernels, project_x(): pl.pallas_call(functools.partial(x_body, nfeat, steps, 3), grid_spec=pltp...  8.5 us
    ppermute x7, starting transfers between devices, to_pair(): lax.ppermute(value, 'feat', [(i, i ^ 1) for i in range(lax.axis_size('fea...  6.24 us
    pallas_call x1, Pallas kernels, first_scores(): pl.pallas_call(functools.partial(first_body, nblk, passages), grid_spec=p...  5.8 us
    pallas_call x1, Pallas kernels, own_scores(): pl.pallas_call(own_body, grid_spec=pltpu.PrefetchScalarGridSpec(num_scala...  3.7 us
    pallas_call x1, Pallas kernels, project_g(): pl.pallas_call(functools.partial(g_body, nfeat, steps), grid_spec=pltpu.P...  3.4 us
    pallas_call x1, Pallas kernels, near_scores(): pl.pallas_call(near_body, in_specs=[VMEM] * 3, out_specs=[VMEM] * 2, out_...  2.89 us
  transfers between devices with their start and end apart: 25, of which 12 were waited for; matrix products, arithmetic and copies ran while one was open for 1% of the time, Pallas kernels for 19%

profile of v2, /device:TPU:0, one launch (start us, length us, event | category | flops | bytes accessed | tf_op | source)
XLA Modules:
  0.0 87.8 jit_solution(4781772641832531725)
XLA Ops:
  0.0 8.5 %project_x.1 = (f32[128,256]{1,0:T(8,128)S(1)}, s16[144,256]{1,0:T(8,128)(2,1)S(1)}, s16[144,256]{1,0:T(8,128)(2,1)S(1)}, s16[144,256]{1,0:T(8,128)(2,1)S(1)}) custom-call(s32[1]{0:T(128)} %bitcast.me_ref, bf16[1024,7168]{1,0:T(8,128)(2,1)} %act_hbm.1, bf16[7168,128]{1,0:T(8,128)(2,1)} %proj_hbm.3), custom_call_target="tpu_custom_call" | custom-call | flops 1879048192 | bytes 16515072 | tf_op jit(solution)/shard_map/project_x/pallas_call | solution.py:109
  8.5 3.1 %collective-permute-start = (s16[144,256]{1,0:T(8,128)(2,1)S(1)}, s16[144,256]{1,0:T(8,128)(2,1)S(1)}, u32[]{:S(2)}, u32[]{:S(2)}) collective-permute-start(s16[144,256]{1,0:T(8,128)(2,1)S(1)} %get-tuple-element.41), channel_id=1, source_target_pairs={{0,4},{4,8},{8,12},{12,0},{1,5},{5,9},{9,13},{13,1},{2,6},{6,10},{... | collective-permute-start | bytes 221192 | tf_op jit(solution)/shard_map/ppermute | solution.py:753
  11.6 2.6 %collective-permute-start.1 = (s16[144,256]{1,0:T(8,128)(2,1)S(1)}, s16[144,256]{1,0:T(8,128)(2,1)S(1)}, u32[]{:S(2)}, u32[]{:S(2)}) collective-permute-start(s16[144,256]{1,0:T(8,128)(2,1)S(1)} %get-tuple-element.42), channel_id=1, source_target_pairs={{0,8},{4,12},{8,0},{12,4},{1,9},{5,13},{9,1},{13,5},{2,10},{6,14},... | collective-permute-start | bytes 221192 | tf_op jit(solution)/shard_map/ppermute | solution.py:753
  14.2 1.3 %collective-permute-start.2 = (s16[144,256]{1,0:T(8,128)(2,1)S(1)}, s16[144,256]{1,0:T(8,128)(2,1)S(1)}, u32[]{:S(2)}, u32[]{:S(2)}) collective-permute-start(s16[144,256]{1,0:T(8,128)(2,1)S(1)} %get-tuple-element.43), channel_id=1, source_target_pairs={{0,12},{4,0},{8,4},{12,8},{1,13},{5,1},{9,5},{13,9},{2,14},{6,2},{... | collective-permute-start | bytes 221192 | tf_op jit(solution)/shard_map/ppermute | solution.py:753
  15.5 0.1 copy.9
  15.6 0.2 reduce-window.9
  15.8 0.1 reduce.ends_ref
  15.9 3.4 %project_g.1 = (f32[32,1024]{1,0:T(8,128)S(1)}, s16[272,128]{1,0:T(8,128)(2,1)S(1)}, s16[272,128]{1,0:T(8,128)(2,1)S(1)}, s16[272,128]{1,0:T(8,128)(2,1)S(1)}) custom-call(s32[1]{0:T(128)} %bitcast.me_ref, bf16[1024,2048]{1,0:T(8,128)(2,1)} %grad_hbm.1, bf16[2048,128]{1,0:T(8,128)(2,1)S(1)} %copy-done, s32[128]{0:T(128)S(1)} %sub.3.starts_ref, ...), custom_call_target="tpu_custom_call" | custom-call | flops 536870912 | bytes 4718592 | tf_op jit(solution)/shard_map/project_g/pallas_call | solution.py:170
  19.3 0.0 collective-permute-done.refs_2_
  19.4 0.0 collective-permute-done.1.refs_3_
  19.4 0.1 join_x_body.1.rest_0_
  19.4 1.6 %collective-permute-start.4 = (bf16[128,256]{1,0:T(8,128)(2,1)S(1)}, bf16[128,256]{1,0:T(8,128)(2,1)S(1)}, u32[]{:S(2)}, u32[]{:S(2)}) collective-permute-start(bf16[128,256]{1,0:T(8,128)(2,1)S(1)} %join_x_body.1.rest_0_), channel_id=1, source_target_pairs={{0,8},{4,12},{8,0},{12,4},{1,9},{5,13},{9,1},{13,5},{2,10},{6,14},... | collective-permute-start | bytes 196616 | tf_op jit(solution)/shard_map/ppermute | solution.py:753
  21.0 2.2 %collective-permute-start.3 = (bf16[128,256]{1,0:T(8,128)(2,1)S(1)}, bf16[128,256]{1,0:T(8,128)(2,1)S(1)}, u32[]{:S(2)}, u32[]{:S(2)}) collective-permute-start(bf16[128,256]{1,0:T(8,128)(2,1)S(1)} %join_x_body.1.rest_0_), channel_id=1, source_target_pairs={{0,4},{4,0},{8,12},{12,8},{1,5},{5,1},{9,13},{13,9},{2,6},{6,2},{1... | collective-permute-start | bytes 196616 | tf_op jit(solution)/shard_map/ppermute | solution.py:761
  23.3 0.0 collective-permute-start.6
  23.3 1.2 %collective-permute-start.7 = (s16[272,128]{1,0:T(8,128)(2,1)S(1)}, s16[272,128]{1,0:T(8,128)(2,1)S(1)}, u32[]{:S(2)}, u32[]{:S(2)}) collective-permute-start(s16[272,128]{1,0:T(8,128)(2,1)S(1)} %get-tuple-element.45), channel_id=1, source_target_pairs={{0,8},{4,12},{8,0},{12,4},{1,9},{5,13},{9,1},{13,5},{2,10},{6,14},... | collective-permute-start | bytes 208904 | tf_op jit(solution)/shard_map/ppermute | solution.py:753
  24.5 2.7 %collective-permute-start.8 = (s16[272,128]{1,0:T(8,128)(2,1)S(1)}, s16[272,128]{1,0:T(8,128)(2,1)S(1)}, u32[]{:S(2)}, u32[]{:S(2)}) collective-permute-start(s16[272,128]{1,0:T(8,128)(2,1)S(1)} %get-tuple-element.46), channel_id=1, source_target_pairs={{0,12},{4,0},{8,4},{12,8},{1,13},{5,1},{9,5},{13,9},{2,14},{6,2},{... | collective-permute-start | bytes 208904 | tf_op jit(solution)/shard_map/ppermute | solution.py:753
  27.2 0.5 collective-permute-start.5
  27.6 0.0 collective-permute-done.3.rest_1_
  27.7 1.6 %collective-permute-start.9 = (bf16[128,768]{1,0:T(8,128)(2,1)S(1)}, bf16[128,768]{1,0:T(8,128)(2,1)S(1)}, u32[]{:S(2)}, u32[]{:S(2)}) collective-permute-start(bf16[128,768]{1,0:T(8,128)(2,1)S(1)} %pack.2.refs_0_.first_ref), channel_id=1, source_target_pairs={{0,2},{2,0},{1,3},{3,1},{4,6},{6,4},{5,7},{7,5},{8,10},{10,8},{9,1... | collective-permute-start | bytes 589832 | tf_op jit(solution)/shard_map/ppermute | solution.py:753
  29.2 0.9 %collective-permute-done.6.refs_2_ = s16[272,128]{1,0:T(8,128)(2,1)S(1)} collective-permute-done((s16[272,128]{1,0:T(8,128)(2,1)S(1)}, s16[272,128]{1,0:T(8,128)(2,1)S(1)}, u32[]{:S(2)}, u32[]{:S(2)}) %collective-permute-start.6) | collective-permute-done | bytes 69664 | tf_op jit(solution)/shard_map/ppermute | solution.py:753
  30.2 1.2 %collective-permute-done.7.refs_3_ = s16[272,128]{1,0:T(8,128)(2,1)S(1)} collective-permute-done((s16[272,128]{1,0:T(8,128)(2,1)S(1)}, s16[272,128]{1,0:T(8,128)(2,1)S(1)}, u32[]{:S(2)}, u32[]{:S(2)}) %collective-permute-start.7) | collective-permute-done | bytes 69664 | tf_op jit(solution)/shard_map/ppermute | solution.py:753
  31.3 0.0 collective-permute-done.8.refs_4_
  31.3 0.1 join_g_body.1.rest_1_
  31.4 0.6 collective-permute-done.5.rest_0_
  32.0 1.5 %collective-permute-start.10 = (bf16[128,512]{1,0:T(8,128)(2,1)S(1)}, bf16[128,512]{1,0:T(8,128)(2,1)S(1)}, u32[]{:S(2)}, u32[]{:S(2)}) collective-permute-start(bf16[128,512]{1,0:T(8,128)(2,1)S(1)} %pack.3.last_ref), channel_id=1, source_target_pairs={{0,2},{2,0},{1,3},{3,1},{4,6},{6,4},{5,7},{7,5},{8,10},{10,8},{9,1... | collective-permute-start | bytes 393224 | tf_op jit(solution)/shard_map/ppermute | solution.py:753
  33.5 0.1 collective-permute-start.11
  33.6 3.5 %collective-permute-done.10.last_ref = bf16[128,512]{1,0:T(8,128)(2,1)S(1)} collective-permute-done((bf16[128,512]{1,0:T(8,128)(2,1)S(1)}, bf16[128,512]{1,0:T(8,128)(2,1)S(1)}, u32[]{:S(2)}, u32[]{:S(2)}) %collective-permute-start.10) | collective-permute-done | bytes 131104 | tf_op jit(solution)/shard_map/ppermute | solution.py:753
  37.1 0.1 collective-permute-start.12
  37.2 0.1 stack.31.place_ref
  37.3 1.5 %collective-permute-done.12.rest_3_ = bf16[160,1024]{1,0:T(8,128)(2,1)S(1)} collective-permute-done((bf16[160,1024]{1,0:T(8,128)(2,1)S(1)}, bf16[160,1024]{1,0:T(8,128)(2,1)S(1)}, u32[]{:S(2)}, u32[]{:S(2)}) %collective-permute-start.12) | collective-permute-done | bytes 327712 | tf_op jit(solution)/shard_map/ppermute | solution.py:753
  38.8 5.8 %first_scores.1 = (s16[144,512]{1,0:T(8,128)(2,1)S(1)}, f32[8,128]{1,0:T(8,128)S(1)}, bf16[128,4096]{1,0:T(8,128)(2,1)S(1)}, bf16[2,512,4096]{2,1,0:T(8,128)(2,1)S(1)}) custom-call(s32[7]{0:T(128)S(1)} %stack.31.place_ref, s32[128]{0:T(128)S(1)} %sub.3.starts_ref, s32[128]{0:T(128)S(1)} %reduce.ends_ref, bf16[160,1024]{1,0:T(8,128)(2,1)S(1)} %token_block.2.rest_0_, ...), custom_call_target="tpu_custom_call" | custom-call | flops 2147483648 | bytes 8388608 | tf_op jit(solution)/shard_map/first_scores/pallas_call | solution.py:372
  44.6 1.0 %collective-permute-start.13 = (s16[144,512]{1,0:T(8,128)(2,1)S(1)}, s16[144,512]{1,0:T(8,128)(2,1)S(1)}, u32[]{:S(2)}, u32[]{:S(2)}) collective-permute-start(s16[144,512]{1,0:T(8,128)(2,1)S(1)} %get-tuple-element.51), channel_id=1, source_target_pairs={{0,4},{4,0},{8,12},{12,8},{1,5},{5,1},{9,13},{13,9},{2,6},{6,2},{1... | collective-permute-start | bytes 442376 | tf_op jit(solution)/shard_map/ppermute | solution.py:761
  45.6 2.9 %near_scores.1 = (f32[128,512]{1,0:T(8,128)S(1)}, s16[144,512]{1,0:T(8,128)(2,1)S(1)}) custom-call(bf16[128,4096]{1,0:T(8,128)(2,1)S(1)} %get-tuple-element.47.low_ref, f32[8,128]{1,0:T(8,128)S(1)} %get-tuple-element.48.sumsq_ref, bf16[2,512,4096]{2,1,0:T(8,128)(2,1)S(1)} %get-tuple-element.49.held_ref.rest_3_), custom_call_target="tpu_custom_call" | custom-call | flops 1073741824 | bytes 8388608 | tf_op jit(solution)/shard_map/near_scores/pallas_call | solution.py:409
  48.5 1.2 %collective-permute-start.14 = (s16[144,512]{1,0:T(8,128)(2,1)S(1)}, s16[144,512]{1,0:T(8,128)(2,1)S(1)}, u32[]{:S(2)}, u32[]{:S(2)}) collective-permute-start(s16[144,512]{1,0:T(8,128)(2,1)S(1)} %get-tuple-element.53), channel_id=1, source_target_pairs={{0,4},{4,0},{8,12},{12,8},{1,5},{5,1},{9,13},{13,9},{2,6},{6,2},{1... | collective-permute-start | bytes 442376 | tf_op jit(solution)/shard_map/ppermute | solution.py:761
  49.6 0.9 %collective-permute-done.13.message_ref = s16[144,512]{1,0:T(8,128)(2,1)S(1)} collective-permute-done((s16[144,512]{1,0:T(8,128)(2,1)S(1)}, s16[144,512]{1,0:T(8,128)(2,1)S(1)}, u32[]{:S(2)}, u32[]{:S(2)}) %collective-permute-start.13) | collective-permute-done | bytes 147488 | tf_op jit(solution)/shard_map/ppermute | solution.py:761
  50.5 0.3 add_scores.1.after_ref
  50.8 0.0 copy-start.1
  50.8 1.6 %collective-permute-start.15 = (s16[144,512]{1,0:T(8,128)(2,1)S(1)}, s16[144,512]{1,0:T(8,128)(2,1)S(1)}, u32[]{:S(2)}, u32[]{:S(2)}) collective-permute-start(s16[144,512]{1,0:T(8,128)(2,1)S(1)} %add_scores.1.after_ref), channel_id=1, source_target_pairs={{0,8},{4,12},{8,0},{12,4},{1,9},{5,13},{9,1},{13,5},{2,10},{6,14},... | collective-permute-start | bytes 442376 | tf_op jit(solution)/shard_map/ppermute | solution.py:753
  52.4 3.7 %own_scores.1 = (f32[128,512]{1,0:T(8,128)S(1)}, bf16[2,512,4096]{2,1,0:T(8,128)(2,1)S(1)}) custom-call(s32[1]{0:T(128)} %bitcast.me_ref, bf16[128,4096]{1,0:T(8,128)(2,1)S(1)} %get-tuple-element.47.low_ref, f32[8,128]{1,0:T(8,128)S(1)} %get-tuple-element.48.sumsq_ref, bf16[2048,4096]{1,0:T(8,128)(2,1)} %corpus_hbm.1, s16[144,512]{1,0:T(8,128)(2,1)S(1)} %add_scores.1.after_ref), custom_call_target="tpu_custom_call" | custom-call | flops 536870912 | bytes 8388608 | tf_op jit(solution)/shard_map/own_scores/pallas_call | solution.py:437
  56.2 0.0 collective-permute-done.14.message_ref
  56.2 3.9 %collective-permute-done.15.message_ref = s16[144,512]{1,0:T(8,128)(2,1)S(1)} collective-permute-done((s16[144,512]{1,0:T(8,128)(2,1)S(1)}, s16[144,512]{1,0:T(8,128)(2,1)S(1)}, u32[]{:S(2)}, u32[]{:S(2)}) %collective-permute-start.15) | collective-permute-done | bytes 147488 | tf_op jit(solution)/shard_map/ppermute | solution.py:753
  60.1 0.5 weights.1
  60.6 0.1 collective-permute-start.19
  60.6 3.1 %collective-permute-start.17 = (bf16[80,512]{1,0:T(8,128)(2,1)S(1)}, bf16[80,512]{1,0:T(8,128)(2,1)S(1)}, u32[]{:S(2)}, u32[]{:S(2)}) collective-permute-start(bf16[80,512]{1,0:T(8,128)(2,1)S(1)} %get-tuple-element.57.rest_0_), channel_id=1, source_target_pairs={{0,8},{4,12},{8,0},{12,4},{1,9},{5,13},{9,1},{13,5},{2,10},{6,14},... | collective-permute-start | bytes 245768 | tf_op jit(solution)/shard_map/ppermute | solution.py:753
  63.7 0.0 collective-permute-start.16
  63.8 0.7 weighted_sums.2
  64.5 5.2 %collective-permute-done.17.piece_ref.rest_1_ = bf16[80,512]{1,0:T(8,128)(2,1)S(1)} collective-permute-done((bf16[80,512]{1,0:T(8,128)(2,1)S(1)}, bf16[80,512]{1,0:T(8,128)(2,1)S(1)}, u32[]{:S(2)}, u32[]{:S(2)}) %collective-permute-start.17) | collective-permute-done | bytes 81952 | tf_op jit(solution)/shard_map/ppermute | solution.py:753
  69.7 0.8 collective-permute-done.16.piece_ref.rest_2_
  70.5 1.3 %collective-permute-start.18 = (bf16[64,512]{1,0:T(8,128)(2,1)S(1)}, bf16[64,512]{1,0:T(8,128)(2,1)S(1)}, u32[]{:S(2)}, u32[]{:S(2)}) collective-permute-start(bf16[64,512]{1,0:T(8,128)(2,1)S(1)} %relay.3.rest_6_), channel_id=1, source_target_pairs={{0,4},{4,0},{8,12},{12,8},{1,5},{5,1},{9,13},{13,9},{2,6},{6,2},{1... | collective-permute-start | bytes 196616 | tf_op jit(solution)/shard_map/ppermute | solution.py:761
  71.8 0.0 collective-permute-done.19.rest_0_
  71.8 1.4 %weighted_sums.3 = (f32[128,4096]{1,0:T(8,128)S(1)}, f32[128,128]{1,0:T(8,128)S(1)}) custom-call(bf16[144,512]{1,0:T(8,128)(2,1)S(1)} %collective-permute-done.19.rest_0_, bf16[80,512]{1,0:T(8,128)(2,1)S(1)} %collective-permute-done.17.piece_ref.rest_1_, bf16[64,512]{1,0:T(8,128)(2,1)S(1)} %collective-permute-done.16.piece_ref.rest_2_, ...), custom_call_target="tpu_custom_call" | custom-call | flops 1073741824 | bytes 4194304 | tf_op jit(solution)/shard_map/weighted_sums/pallas_call | solution.py:619
  73.3 1.0 %collective-permute-done.20.piece_ref = bf16[80,512]{1,0:T(8,128)(2,1)S(1)} collective-permute-done((bf16[80,512]{1,0:T(8,128)(2,1)S(1)}, bf16[80,512]{1,0:T(8,128)(2,1)S(1)}, u32[]{:S(2)}, u32[]{:S(2)}) %collective-permute-start.20) | collective-permute-done | bytes 81952 | tf_op jit(solution)/shard_map/ppermute | solution.py:761
  74.2 1.4 %last_sums.2 = (bf16[2,16,4224]{2,1,0:T(8,128)(2,1)S(1)}, f32[2,16,4224]{2,1,0:T(8,128)S(1)}, f32[64,128]{1,0:T(8,128)S(1)}) custom-call(s32[7]{0:T(128)S(1)} %stack.31.place_ref, bf16[80,512]{1,0:T(8,128)(2,1)S(1)} %collective-permute-done.20.piece_ref, bf16[2,512,4096]{2,1,0:T(8,128)(2,1)S(1)} %get-tuple-element.58.rest_2_.held_ref, ...), custom_call_target="tpu_custom_call" | custom-call | tf_op jit(solution)/shard_map/last_sums/pallas_call | solution.py:672
  75.7 0.1 collective-permute-start.23
  75.8 1.4 %last_sums.3 = (bf16[2,16,4224]{2,1,0:T(8,128)(2,1)S(1)}, f32[2,16,4224]{2,1,0:T(8,128)S(1)}) custom-call(s32[7]{0:T(128)S(1)} %stack.31.place_ref, bf16[64,512]{1,0:T(8,128)(2,1)S(1)} %collective-permute-done.18.piece_ref, bf16[2,512,4096]{2,1,0:T(8,128)(2,1)S(1)} %get-tuple-element.58.rest_2_.held_ref, f32[128,4096]{1,0:T(8,128)S(1)} %get-tuple-element.62.old_ref, ...), custom_call_target="tpu_custom_call" | custom-call | tf_op jit(solution)/shard_map/last_sums/pallas_call | solution.py:672
  77.2 0.6 collective-permute-start.21
  77.7 0.7 merge_core.3
  78.4 0.5 collective-permute-start.24
  78.9 0.7 merge_core.2
  79.6 1.7 %collective-permute-start.22 = (bf16[16,4224]{1,0:T(8,128)(2,1)S(1)}, bf16[16,4224]{1,0:T(8,128)(2,1)S(1)}, u32[]{:S(2)}, u32[]{:S(2)}) collective-permute-start(bf16[16,4224]{1,0:T(8,128)(2,1)S(1)} %get-tuple-element.68), channel_id=1, source_target_pairs={{0,2},{2,0},{1,3},{3,1},{4,6},{6,4},{5,7},{7,5},{8,10},{10,8},{9,1... | collective-permute-start | bytes 405512 | tf_op jit(solution)/shard_map/ppermute | solution.py:753
  81.3 3.6 %collective-permute-done.24.other_ref = bf16[16,4224]{1,0:T(8,128)(2,1)S(1)} collective-permute-done((bf16[16,4224]{1,0:T(8,128)(2,1)S(1)}, bf16[16,4224]{1,0:T(8,128)(2,1)S(1)}, u32[]{:S(2)}, u32[]{:S(2)}) %collective-permute-start.24) | collective-permute-done | bytes 135200 | tf_op jit(solution)/shard_map/ppermute | solution.py:753
  85.0 0.1 merge_last.2.rest_0_
  85.1 1.8 %collective-permute-done.22.other_ref = bf16[16,4224]{1,0:T(8,128)(2,1)S(1)} collective-permute-done((bf16[16,4224]{1,0:T(8,128)(2,1)S(1)}, bf16[16,4224]{1,0:T(8,128)(2,1)S(1)}, u32[]{:S(2)}, u32[]{:S(2)}) %collective-permute-start.22) | collective-permute-done | bytes 135200 | tf_op jit(solution)/shard_map/ppermute | solution.py:753
  86.9 0.9 %merge_last.3 = f32[32,4096]{1,0:T(8,128)} custom-call(f32[16,4224]{1,0:T(8,128)S(1)} %get-tuple-element.67.keep_ref, bf16[16,4224]{1,0:T(8,128)(2,1)S(1)} %collective-permute-done.22.other_ref, f32[16,4096]{1,0:T(8,128)S(1)} %merge_last.2.rest_0_), custom_call_target="tpu_custom_call" | custom-call | tf_op jit(solution)/shard_map/merge_last/pallas_call | solution.py:741
  (21 shorter events, 0.2 us)
Async XLA Ops:
  0.0 15.5 %copy-start.2 = (s32[128]{0:T(128)S(1)}, s32[128]{0:T(128)}, u32[]{:S(2)}) copy-start(s32[128]{0:T(128)} %param.11) | copy-start | bytes 1540
  0.0 15.9 %copy-start = (bf16[2048,128]{1,0:T(8,128)(2,1)S(1)}, bf16[2048,128]{1,0:T(8,128)(2,1)}, u32[]{:S(2)}) copy-start(bf16[2048,128]{1,0:T(8,128)(2,1)} %proj_hbm.2) | copy-start | bytes 1572868
  8.5 10.8 %collective-permute-start = (s16[144,256]{1,0:T(8,128)(2,1)S(1)}, s16[144,256]{1,0:T(8,128)(2,1)S(1)}, u32[]{:S(2)}, u32[]{:S(2)}) collective-permute-start(s16[144,256]{1,0:T(8,128)(2,1)S(1)} %get-tuple-element.41), channel_id=1, source_target_pairs={{0,4},{4,8},{8,12},{12,0},{1,5},{5,9},{9,13},{13,1},{2,6},{6,10},{... | collective-permute-start | bytes 221192 | tf_op jit(solution)/shard_map/ppermute | solution.py:753
  11.6 7.8 %collective-permute-start.1 = (s16[144,256]{1,0:T(8,128)(2,1)S(1)}, s16[144,256]{1,0:T(8,128)(2,1)S(1)}, u32[]{:S(2)}, u32[]{:S(2)}) collective-permute-start(s16[144,256]{1,0:T(8,128)(2,1)S(1)} %get-tuple-element.42), channel_id=1, source_target_pairs={{0,8},{4,12},{8,0},{12,4},{1,9},{5,13},{9,1},{13,5},{2,10},{6,14},... | collective-permute-start | bytes 221192 | tf_op jit(solution)/shard_map/ppermute | solution.py:753
  14.2 5.2 %collective-permute-start.2 = (s16[144,256]{1,0:T(8,128)(2,1)S(1)}, s16[144,256]{1,0:T(8,128)(2,1)S(1)}, u32[]{:S(2)}, u32[]{:S(2)}) collective-permute-start(s16[144,256]{1,0:T(8,128)(2,1)S(1)} %get-tuple-element.43), channel_id=1, source_target_pairs={{0,12},{4,0},{8,4},{12,8},{1,13},{5,1},{9,5},{13,9},{2,14},{6,2},{... | collective-permute-start | bytes 221192 | tf_op jit(solution)/shard_map/ppermute | solution.py:753
  19.4 7.7 %collective-permute-start.4 = (bf16[128,256]{1,0:T(8,128)(2,1)S(1)}, bf16[128,256]{1,0:T(8,128)(2,1)S(1)}, u32[]{:S(2)}, u32[]{:S(2)}) collective-permute-start(bf16[128,256]{1,0:T(8,128)(2,1)S(1)} %join_x_body.1.rest_0_), channel_id=1, source_target_pairs={{0,8},{4,12},{8,0},{12,4},{1,9},{5,13},{9,1},{13,5},{2,10},{6,14},... | collective-permute-start | bytes 196616 | tf_op jit(solution)/shard_map/ppermute | solution.py:753
  21.0 6.6 %collective-permute-start.3 = (bf16[128,256]{1,0:T(8,128)(2,1)S(1)}, bf16[128,256]{1,0:T(8,128)(2,1)S(1)}, u32[]{:S(2)}, u32[]{:S(2)}) collective-permute-start(bf16[128,256]{1,0:T(8,128)(2,1)S(1)} %join_x_body.1.rest_0_), channel_id=1, source_target_pairs={{0,4},{4,0},{8,12},{12,8},{1,5},{5,1},{9,13},{13,9},{2,6},{6,2},{1... | collective-permute-start | bytes 196616 | tf_op jit(solution)/shard_map/ppermute | solution.py:761
  23.3 6.9 %collective-permute-start.6 = (s16[272,128]{1,0:T(8,128)(2,1)S(1)}, s16[272,128]{1,0:T(8,128)(2,1)S(1)}, u32[]{:S(2)}, u32[]{:S(2)}) collective-permute-start(s16[272,128]{1,0:T(8,128)(2,1)S(1)} %get-tuple-element.44), channel_id=1, source_target_pairs={{0,4},{4,8},{8,12},{12,0},{1,5},{5,9},{9,13},{13,1},{2,6},{6,10},{... | collective-permute-start | bytes 208904 | tf_op jit(solution)/shard_map/ppermute | solution.py:753
  23.3 8.0 %collective-permute-start.7 = (s16[272,128]{1,0:T(8,128)(2,1)S(1)}, s16[272,128]{1,0:T(8,128)(2,1)S(1)}, u32[]{:S(2)}, u32[]{:S(2)}) collective-permute-start(s16[272,128]{1,0:T(8,128)(2,1)S(1)} %get-tuple-element.45), channel_id=1, source_target_pairs={{0,8},{4,12},{8,0},{12,4},{1,9},{5,13},{9,1},{13,5},{2,10},{6,14},... | collective-permute-start | bytes 208904 | tf_op jit(solution)/shard_map/ppermute | solution.py:753
  24.5 6.9 %collective-permute-start.8 = (s16[272,128]{1,0:T(8,128)(2,1)S(1)}, s16[272,128]{1,0:T(8,128)(2,1)S(1)}, u32[]{:S(2)}, u32[]{:S(2)}) collective-permute-start(s16[272,128]{1,0:T(8,128)(2,1)S(1)} %get-tuple-element.46), channel_id=1, source_target_pairs={{0,12},{4,0},{8,4},{12,8},{1,13},{5,1},{9,5},{13,9},{2,14},{6,2},{... | collective-permute-start | bytes 208904 | tf_op jit(solution)/shard_map/ppermute | solution.py:753
  27.2 4.8 %collective-permute-start.5 = (bf16[128,256]{1,0:T(8,128)(2,1)S(1)}, bf16[128,256]{1,0:T(8,128)(2,1)S(1)}, u32[]{:S(2)}, u32[]{:S(2)}) collective-permute-start(bf16[128,256]{1,0:T(8,128)(2,1)S(1)} %collective-permute-done.4.rest_2_), channel_id=1, source_target_pairs={{0,4},{4,0},{8,12},{12,8},{1,5},{5,1},{9,13},{13,9},{2,6},{6,2},{1... | collective-permute-start | bytes 196616 | tf_op jit(solution)/shard_map/ppermute | solution.py:761
  27.7 9.4 %collective-permute-start.9 = (bf16[128,768]{1,0:T(8,128)(2,1)S(1)}, bf16[128,768]{1,0:T(8,128)(2,1)S(1)}, u32[]{:S(2)}, u32[]{:S(2)}) collective-permute-start(bf16[128,768]{1,0:T(8,128)(2,1)S(1)} %pack.2.refs_0_.first_ref), channel_id=1, source_target_pairs={{0,2},{2,0},{1,3},{3,1},{4,6},{6,4},{5,7},{7,5},{8,10},{10,8},{9,1... | collective-permute-start | bytes 589832 | tf_op jit(solution)/shard_map/ppermute | solution.py:753
  32.0 5.0 %collective-permute-start.10 = (bf16[128,512]{1,0:T(8,128)(2,1)S(1)}, bf16[128,512]{1,0:T(8,128)(2,1)S(1)}, u32[]{:S(2)}, u32[]{:S(2)}) collective-permute-start(bf16[128,512]{1,0:T(8,128)(2,1)S(1)} %pack.3.last_ref), channel_id=1, source_target_pairs={{0,2},{2,0},{1,3},{3,1},{4,6},{6,4},{5,7},{7,5},{8,10},{10,8},{9,1... | collective-permute-start | bytes 393224 | tf_op jit(solution)/shard_map/ppermute | solution.py:753
  33.5 3.8 %collective-permute-start.11 = (bf16[160,1024]{1,0:T(8,128)(2,1)S(1)}, bf16[160,1024]{1,0:T(8,128)(2,1)S(1)}, u32[]{:S(2)}, u32[]{:S(2)}) collective-permute-start(bf16[160,1024]{1,0:T(8,128)(2,1)S(1)} %token_block.2.rest_0_), channel_id=1, source_target_pairs={{0,1},{1,0},{2,3},{3,2},{4,5},{5,4},{6,7},{7,6},{8,9},{9,8},{10,11... | collective-permute-start | bytes 983048 | tf_op jit(solution)/shard_map/ppermute | solution.py:753
  37.1 1.7 %collective-permute-start.12 = (bf16[160,1024]{1,0:T(8,128)(2,1)S(1)}, bf16[160,1024]{1,0:T(8,128)(2,1)S(1)}, u32[]{:S(2)}, u32[]{:S(2)}) collective-permute-start(bf16[160,1024]{1,0:T(8,128)(2,1)S(1)} %token_block.3.rest_1_), channel_id=1, source_target_pairs={{0,1},{1,0},{2,3},{3,2},{4,5},{5,4},{6,7},{7,6},{8,9},{9,8},{10,11... | collective-permute-start | bytes 983048 | tf_op jit(solution)/shard_map/ppermute | solution.py:753
  44.6 6.0 %collective-permute-start.13 = (s16[144,512]{1,0:T(8,128)(2,1)S(1)}, s16[144,512]{1,0:T(8,128)(2,1)S(1)}, u32[]{:S(2)}, u32[]{:S(2)}) collective-permute-start(s16[144,512]{1,0:T(8,128)(2,1)S(1)} %get-tuple-element.51), channel_id=1, source_target_pairs={{0,4},{4,0},{8,12},{12,8},{1,5},{5,1},{9,13},{13,9},{2,6},{6,2},{1... | collective-permute-start | bytes 442376 | tf_op jit(solution)/shard_map/ppermute | solution.py:761
  48.5 7.7 %collective-permute-start.14 = (s16[144,512]{1,0:T(8,128)(2,1)S(1)}, s16[144,512]{1,0:T(8,128)(2,1)S(1)}, u32[]{:S(2)}, u32[]{:S(2)}) collective-permute-start(s16[144,512]{1,0:T(8,128)(2,1)S(1)} %get-tuple-element.53), channel_id=1, source_target_pairs={{0,4},{4,0},{8,12},{12,8},{1,5},{5,1},{9,13},{13,9},{2,6},{6,2},{1... | collective-permute-start | bytes 442376 | tf_op jit(solution)/shard_map/ppermute | solution.py:761
  50.8 9.2 %copy-start.1 = (s32[2048]{0:T(1024)S(1)}, s32[2048]{0:T(1024)}, u32[]{:S(2)}) copy-start(s32[2048]{0:T(1024)} %param.13) | copy-start | bytes 24580
  50.8 9.2 %collective-permute-start.15 = (s16[144,512]{1,0:T(8,128)(2,1)S(1)}, s16[144,512]{1,0:T(8,128)(2,1)S(1)}, u32[]{:S(2)}, u32[]{:S(2)}) collective-permute-start(s16[144,512]{1,0:T(8,128)(2,1)S(1)} %add_scores.1.after_ref), channel_id=1, source_target_pairs={{0,8},{4,12},{8,0},{12,4},{1,9},{5,13},{9,1},{13,5},{2,10},{6,14},... | collective-permute-start | bytes 442376 | tf_op jit(solution)/shard_map/ppermute | solution.py:753
  60.6 11.2 %collective-permute-start.19 = (bf16[144,512]{1,0:T(8,128)(2,1)S(1)}, bf16[144,512]{1,0:T(8,128)(2,1)S(1)}, u32[]{:S(2)}, u32[]{:S(2)}) collective-permute-start(bf16[144,512]{1,0:T(8,128)(2,1)S(1)} %get-tuple-element.60), channel_id=1, source_target_pairs={{0,4},{4,0},{8,12},{12,8},{1,5},{5,1},{9,13},{13,9},{2,6},{6,2},{1... | collective-permute-start | bytes 442376 | tf_op jit(solution)/shard_map/ppermute | solution.py:761
  60.6 9.0 %collective-permute-start.17 = (bf16[80,512]{1,0:T(8,128)(2,1)S(1)}, bf16[80,512]{1,0:T(8,128)(2,1)S(1)}, u32[]{:S(2)}, u32[]{:S(2)}) collective-permute-start(bf16[80,512]{1,0:T(8,128)(2,1)S(1)} %get-tuple-element.57.rest_0_), channel_id=1, source_target_pairs={{0,8},{4,12},{8,0},{12,4},{1,9},{5,13},{9,1},{13,5},{2,10},{6,14},... | collective-permute-start | bytes 245768 | tf_op jit(solution)/shard_map/ppermute | solution.py:753
  63.7 6.8 %collective-permute-start.16 = (bf16[64,512]{1,0:T(8,128)(2,1)S(1)}, bf16[64,512]{1,0:T(8,128)(2,1)S(1)}, u32[]{:S(2)}, u32[]{:S(2)}) collective-permute-start(bf16[64,512]{1,0:T(8,128)(2,1)S(1)} %get-tuple-element.56.rest_1_), channel_id=1, source_target_pairs={{0,8},{4,12},{8,0},{12,4},{1,9},{5,13},{9,1},{13,5},{2,10},{6,14},... | collective-permute-start | bytes 196616 | tf_op jit(solution)/shard_map/ppermute | solution.py:753
  69.7 4.5 %collective-permute-start.20 = (bf16[80,512]{1,0:T(8,128)(2,1)S(1)}, bf16[80,512]{1,0:T(8,128)(2,1)S(1)}, u32[]{:S(2)}, u32[]{:S(2)}) collective-permute-start(bf16[80,512]{1,0:T(8,128)(2,1)S(1)} %relay.2.rest_0_), channel_id=1, source_target_pairs={{0,4},{4,0},{8,12},{12,8},{1,5},{5,1},{9,13},{13,9},{2,6},{6,2},{1... | collective-permute-start | bytes 245768 | tf_op jit(solution)/shard_map/ppermute | solution.py:761
  70.5 5.2 %collective-permute-start.18 = (bf16[64,512]{1,0:T(8,128)(2,1)S(1)}, bf16[64,512]{1,0:T(8,128)(2,1)S(1)}, u32[]{:S(2)}, u32[]{:S(2)}) collective-permute-start(bf16[64,512]{1,0:T(8,128)(2,1)S(1)} %relay.3.rest_6_), channel_id=1, source_target_pairs={{0,4},{4,0},{8,12},{12,8},{1,5},{5,1},{9,13},{13,9},{2,6},{6,2},{1... | collective-permute-start | bytes 196616 | tf_op jit(solution)/shard_map/ppermute | solution.py:761
  75.7 2.1 %collective-permute-start.23 = (bf16[2,16,4224]{2,1,0:T(8,128)(2,1)S(1)}, bf16[2,16,4224]{2,1,0:T(8,128)(2,1)S(1)}, u32[]{:S(2)}, u32[]{:S(2)}) collective-permute-start(bf16[2,16,4224]{2,1,0:T(8,128)(2,1)S(1)} %get-tuple-element.70), channel_id=1, source_target_pairs={{0,1},{1,0},{2,3},{3,2},{4,5},{5,4},{6,7},{7,6},{8,9},{9,8},{10,11... | collective-permute-start | bytes 811016 | tf_op jit(solution)/shard_map/ppermute | solution.py:753
  77.2 1.7 %collective-permute-start.21 = (bf16[2,16,4224]{2,1,0:T(8,128)(2,1)S(1)}, bf16[2,16,4224]{2,1,0:T(8,128)(2,1)S(1)}, u32[]{:S(2)}, u32[]{:S(2)}) collective-permute-start(bf16[2,16,4224]{2,1,0:T(8,128)(2,1)S(1)} %get-tuple-element.66), channel_id=1, source_target_pairs={{0,1},{1,0},{2,3},{3,2},{4,5},{5,4},{6,7},{7,6},{8,9},{9,8},{10,11... | collective-permute-start | bytes 811016 | tf_op jit(solution)/shard_map/ppermute | solution.py:753
  78.4 6.5 %collective-permute-start.24 = (bf16[16,4224]{1,0:T(8,128)(2,1)S(1)}, bf16[16,4224]{1,0:T(8,128)(2,1)S(1)}, u32[]{:S(2)}, u32[]{:S(2)}) collective-permute-start(bf16[16,4224]{1,0:T(8,128)(2,1)S(1)} %get-tuple-element.72), channel_id=1, source_target_pairs={{0,2},{2,0},{1,3},{3,1},{4,6},{6,4},{5,7},{7,5},{8,10},{10,8},{9,1... | collective-permute-start | bytes 405512 | tf_op jit(solution)/shard_map/ppermute | solution.py:753
  79.6 7.3 %collective-permute-start.22 = (bf16[16,4224]{1,0:T(8,128)(2,1)S(1)}, bf16[16,4224]{1,0:T(8,128)(2,1)S(1)}, u32[]{:S(2)}, u32[]{:S(2)}) collective-permute-start(bf16[16,4224]{1,0:T(8,128)(2,1)S(1)} %get-tuple-element.68), channel_id=1, source_target_pairs={{0,2},{2,0},{1,3},{3,1},{4,6},{6,4},{5,7},{7,5},{8,10},{10,8},{9,1... | collective-permute-start | bytes 405512 | tf_op jit(solution)/shard_map/ppermute | solution.py:753

commit v3 on v2

--- a/solution.py
+++ b/solution.py
@@ -347,7 +347,7 @@
         grad[:, pl.ds(first, group), :] = product.reshape(width, group, rank)
         return carry
 
-    lax.fori_loop(0, passages // group, step, 0, unroll=2)
+    lax.fori_loop(0, passages // group, step, 0, unroll=4)
     squares = jnp.zeros((passages, LANES), F32)
     for a in range(width):
         column = grad[a]
@@ -521,7 +521,7 @@
     return jnp.concatenate([value[(2 * n + half) * size:(2 * n + half + 1) * size] for n in range(owners)], axis=0)
 
 
-def weight_body(owners, me_ref, owner_ref, own_ref, sumsq_ref, open_ref, open_sumsq_ref, message_ref, first_ref, second_ref, whole_ref):
+def weight_body(owners, me_ref, owner_ref, own_ref, sumsq_ref, open_ref, open_sumsq_ref, message_ref, first_ref, second_ref):
     passages, rows = own_ref.shape
     opened = open_ref[...], open_sumsq_ref[0:1, :]
     value, _ = add_terms([(own_ref[...], sumsq_ref[0:1, :]), opened, read_scores(message_ref)])
@@ -535,9 +535,6 @@
     first_ref[:passages // 2, :] = half_of(weight, 0, owners).astype(BF16)
     first_ref[passages // 2:, :] = code_rows(split3(turn_back(top)) + split3(turn_back(total)), rows).astype(BF16)
     second_ref[...] = half_of(weight, 1, owners).astype(BF16)
-    size = first_ref.shape[0]
-    whole_ref[:size, :] = first_ref[...]
-    whole_ref[size:, :] = second_ref[...]
 
 
 def weights_of(me, owner, own, sumsq, opened, message, owners):
@@ -545,12 +542,11 @@
     return pl.pallas_call(
         functools.partial(weight_body, owners),
         grid_spec=pltpu.PrefetchScalarGridSpec(
-            num_scalar_prefetch=1, grid=(), in_specs=[VMEM] * 6, out_specs=[VMEM] * 3
+            num_scalar_prefetch=1, grid=(), in_specs=[VMEM] * 6, out_specs=[VMEM] * 2
         ),
         out_shape=[
             jax.ShapeDtypeStruct((passages // 2 + CODES, rows), BF16),
             jax.ShapeDtypeStruct((passages // 2, rows), BF16),
-            jax.ShapeDtypeStruct((passages + CODES, rows), BF16),
         ],
         compiler_params=params(8),
         cost_estimate=pl.CostEstimate(flops=8 * passages * rows, bytes_accessed=16 * passages * rows, transcendentals=passages * rows),
@@ -594,19 +590,13 @@
     return jnp.where(lane == 0, top, total)
 
 
-def sums_body(owners, counts, started, *rest):
-    pieces = []
-    for count in counts:
-        parts, rest = rest[:count], rest[count:]
-        if count == 1:
-            size = (parts[0].shape[0] - CODES) // 2
-            parts = parts[0].at[pl.ds(0, size + CODES), :], parts[0].at[pl.ds(size + CODES, size), :]
-        pieces.append(parts)
-    held_ref, rest = rest[0], rest[1:]
+def sums_body(owners, sources, started, *rest):
+    count = 2 * sources
+    parts, held_ref, rest = rest[:count], rest[count], rest[count + 1:]
     before, acc_ref, stats_ref = rest[:2 * started], *rest[-2:]
-    quarters = [held_ref.at[n] for n in range(len(counts))]
-    codes = [piece[0] for piece in pieces]
-    top, total, factors = running_stats(owners, codes, before[1] if before else None)
+    pieces = [parts[2 * n:2 * n + 2] for n in range(sources)]
+    quarters = [held_ref.at[n] for n in range(sources)]
+    top, total, factors = running_stats(owners, parts[::2], before[1] if before else None)
     weights = [jnp.concatenate([piece[0][:piece[1].shape[0], :], piece[1][...]], axis=0) for piece in pieces]
     add_sums(weights, quarters, factors, before[0] if before else None, acc_ref)
     stats_ref[...] = stats_tile(top, total)
@@ -614,10 +604,10 @@
 
 def weighted_sums(owners, pieces, held, before, after=()):
     parts = [part for piece in pieces for part in piece]
-    passages = 2 * pieces[-1][1].shape[0]
+    passages = 2 * parts[1].shape[0]
     _, quarter, depth = held.shape
     return pl.pallas_call(
-        functools.partial(sums_body, owners, tuple(len(piece) for piece in pieces), len(before) // 2),
+        functools.partial(sums_body, owners, len(pieces), len(before) // 2),
         in_specs=[VMEM] * (len(parts) + 1 + len(before)) + [ANY] * len(after),
         out_specs=[VMEM] * 2,
         out_shape=[jax.ShapeDtypeStruct((passages, depth), F32), jax.ShapeDtypeStruct((passages, LANES), F32)],
@@ -809,8 +799,8 @@
     own, held_far = own_scores(me, low, sumsq, corpus, nfeat, across)
     owners = nrows * nsub
     opened = open_scores(to_pair(beside), own)
-    *pieces, whole_piece = weights_of(me, owner, own, sumsq, opened, shift(across, "feat", 2), owners)
-    across, beside = [shift(p, "feat", 2) for p in pieces], [to_pair(whole_piece)]
+    pieces = weights_of(me, owner, own, sumsq, opened, shift(across, "feat", 2), owners)
+    beside, across = [to_pair(p) for p in pieces], [shift(p, "feat", 2) for p in pieces]
     sums = weighted_sums(owners, [pieces], held_far, ())
     relayed = [relay(across[0], sums[1])]
     relayed.append(relay(across[1], relayed[0]))

time: 88 us -> 86.3 us (0.981)
  waiting for transfers between devices: 24.9 us -> 22.1 us
  starting transfers between devices: 29.4 us -> 30.7 us
    ppermute x7 -> x8, starting transfers between devices: 6.24 us -> 10.5 us  [to_pair(): lax.ppermute(value, 'feat', [(i, i ^ 1) for i in range(lax.axis_size('fea...]
    ppermute x18, starting transfers between devices: 23.1 us -> 20.2 us  [shift(): lax.ppermute(value, axis, [(i, (i + by) % count) for i in range(count)])]
    ppermute x18, waiting for transfers between devices: 22.4 us -> 19.7 us  [shift(): lax.ppermute(value, axis, [(i, (i + by) % count) for i in range(count)])]
    ppermute x7 -> x8, waiting for transfers between devices: 2.46 us -> 2.39 us  [to_pair(): lax.ppermute(value, 'feat', [(i, i ^ 1) for i in range(lax.axis_size('fea...]
  transfers between devices with their start and end apart: 25 -> 26, of which waited for: 12 -> 13; matrix products, arithmetic and copies ran while one was open for 1% -> 1% of each run, Pallas kernels for 19% -> 20%
where the time goes in v3:
time: 86.3 us; the launch traced here: 86.2 us
  Pallas kernels  32.7 us (38%)
  starting transfers between devices  30.7 us (36%)
  waiting for transfers between devices  22.1 us (26%)
    ppermute x18, starting transfers between devices, shift(): lax.ppermute(value, axis, [(i, (i + by) % count) for i in range(count)])  20.2 us
    ppermute x18, waiting for transfers between devices, shift(): lax.ppermute(value, axis, [(i, (i + by) % count) for i in range(count)])  19.7 us
    ppermute x8, starting transfers between devices, to_pair(): lax.ppermute(value, 'feat', [(i, i ^ 1) for i in range(lax.axis_size('fea...  10.5 us
    pallas_call x1, Pallas kernels, project_x(): pl.pallas_call(functools.partial(x_body, nfeat, steps, 3), grid_spec=pltp...  8.5 us
    pallas_call x1, Pallas kernels, first_scores(): pl.pallas_call(functools.partial(first_body, nblk, passages), grid_spec=p...  5.64 us
    pallas_call x1, Pallas kernels, own_scores(): pl.pallas_call(own_body, grid_spec=pltpu.PrefetchScalarGridSpec(num_scala...  3.7 us
    pallas_call x1, Pallas kernels, project_g(): pl.pallas_call(functools.partial(g_body, nfeat, steps), grid_spec=pltpu.P...  3.4 us
    pallas_call x1, Pallas kernels, near_scores(): pl.pallas_call(near_body, in_specs=[VMEM] * 3, out_specs=[VMEM] * 2, out_...  2.89 us
  transfers between devices with their start and end apart: 26, of which 13 were waited for; matrix products, arithmetic and copies ran while one was open for 1% of the time, Pallas kernels for 20%

profile of v3, /device:TPU:0, one launch (start us, length us, event | category | flops | bytes accessed | tf_op | source)
XLA Modules:
  0.0 86.2 jit_solution(16665851871174209286)
XLA Ops:
  0.0 8.5 %project_x.1 = (f32[128,256]{1,0:T(8,128)S(1)}, s16[144,256]{1,0:T(8,128)(2,1)S(1)}, s16[144,256]{1,0:T(8,128)(2,1)S(1)}, s16[144,256]{1,0:T(8,128)(2,1)S(1)}) custom-call(s32[1]{0:T(128)} %bitcast.me_ref, bf16[1024,7168]{1,0:T(8,128)(2,1)} %act_hbm.1, bf16[7168,128]{1,0:T(8,128)(2,1)} %proj_hbm.3), custom_call_target="tpu_custom_call" | custom-call | flops 1879048192 | bytes 16515072 | tf_op jit(solution)/shard_map/project_x/pallas_call | solution.py:109
  8.5 3.1 %collective-permute-start = (s16[144,256]{1,0:T(8,128)(2,1)S(1)}, s16[144,256]{1,0:T(8,128)(2,1)S(1)}, u32[]{:S(2)}, u32[]{:S(2)}) collective-permute-start(s16[144,256]{1,0:T(8,128)(2,1)S(1)} %get-tuple-element.40), channel_id=1, source_target_pairs={{0,4},{4,8},{8,12},{12,0},{1,5},{5,9},{9,13},{13,1},{2,6},{6,10},{... | collective-permute-start | bytes 221192 | tf_op jit(solution)/shard_map/ppermute | solution.py:743
  11.6 2.6 %collective-permute-start.1 = (s16[144,256]{1,0:T(8,128)(2,1)S(1)}, s16[144,256]{1,0:T(8,128)(2,1)S(1)}, u32[]{:S(2)}, u32[]{:S(2)}) collective-permute-start(s16[144,256]{1,0:T(8,128)(2,1)S(1)} %get-tuple-element.41), channel_id=1, source_target_pairs={{0,8},{4,12},{8,0},{12,4},{1,9},{5,13},{9,1},{13,5},{2,10},{6,14},... | collective-permute-start | bytes 221192 | tf_op jit(solution)/shard_map/ppermute | solution.py:743
  14.2 1.3 %collective-permute-start.2 = (s16[144,256]{1,0:T(8,128)(2,1)S(1)}, s16[144,256]{1,0:T(8,128)(2,1)S(1)}, u32[]{:S(2)}, u32[]{:S(2)}) collective-permute-start(s16[144,256]{1,0:T(8,128)(2,1)S(1)} %get-tuple-element.42), channel_id=1, source_target_pairs={{0,12},{4,0},{8,4},{12,8},{1,13},{5,1},{9,5},{13,9},{2,14},{6,2},{... | collective-permute-start | bytes 221192 | tf_op jit(solution)/shard_map/ppermute | solution.py:743
  15.5 0.1 copy.9
  15.6 0.2 reduce-window.9
  15.8 0.1 reduce.ends_ref
  15.9 3.4 %project_g.1 = (f32[32,1024]{1,0:T(8,128)S(1)}, s16[272,128]{1,0:T(8,128)(2,1)S(1)}, s16[272,128]{1,0:T(8,128)(2,1)S(1)}, s16[272,128]{1,0:T(8,128)(2,1)S(1)}) custom-call(s32[1]{0:T(128)} %bitcast.me_ref, bf16[1024,2048]{1,0:T(8,128)(2,1)} %grad_hbm.1, bf16[2048,128]{1,0:T(8,128)(2,1)S(1)} %copy-done, s32[128]{0:T(128)S(1)} %sub.3.starts_ref, ...), custom_call_target="tpu_custom_call" | custom-call | flops 536870912 | bytes 4718592 | tf_op jit(solution)/shard_map/project_g/pallas_call | solution.py:170
  19.3 0.0 collective-permute-done.refs_2_
  19.4 0.0 collective-permute-done.1.refs_3_
  19.4 0.1 join_x_body.1.rest_0_
  19.4 1.6 %collective-permute-start.4 = (bf16[128,256]{1,0:T(8,128)(2,1)S(1)}, bf16[128,256]{1,0:T(8,128)(2,1)S(1)}, u32[]{:S(2)}, u32[]{:S(2)}) collective-permute-start(bf16[128,256]{1,0:T(8,128)(2,1)S(1)} %join_x_body.1.rest_0_), channel_id=1, source_target_pairs={{0,8},{4,12},{8,0},{12,4},{1,9},{5,13},{9,1},{13,5},{2,10},{6,14},... | collective-permute-start | bytes 196616 | tf_op jit(solution)/shard_map/ppermute | solution.py:743
  21.0 2.2 %collective-permute-start.3 = (bf16[128,256]{1,0:T(8,128)(2,1)S(1)}, bf16[128,256]{1,0:T(8,128)(2,1)S(1)}, u32[]{:S(2)}, u32[]{:S(2)}) collective-permute-start(bf16[128,256]{1,0:T(8,128)(2,1)S(1)} %join_x_body.1.rest_0_), channel_id=1, source_target_pairs={{0,4},{4,0},{8,12},{12,8},{1,5},{5,1},{9,13},{13,9},{2,6},{6,2},{1... | collective-permute-start | bytes 196616 | tf_op jit(solution)/shard_map/ppermute | solution.py:751
  23.3 0.0 collective-permute-start.6
  23.3 1.2 %collective-permute-start.7 = (s16[272,128]{1,0:T(8,128)(2,1)S(1)}, s16[272,128]{1,0:T(8,128)(2,1)S(1)}, u32[]{:S(2)}, u32[]{:S(2)}) collective-permute-start(s16[272,128]{1,0:T(8,128)(2,1)S(1)} %get-tuple-element.44), channel_id=1, source_target_pairs={{0,8},{4,12},{8,0},{12,4},{1,9},{5,13},{9,1},{13,5},{2,10},{6,14},... | collective-permute-start | bytes 208904 | tf_op jit(solution)/shard_map/ppermute | solution.py:743
  24.5 2.7 %collective-permute-start.8 = (s16[272,128]{1,0:T(8,128)(2,1)S(1)}, s16[272,128]{1,0:T(8,128)(2,1)S(1)}, u32[]{:S(2)}, u32[]{:S(2)}) collective-permute-start(s16[272,128]{1,0:T(8,128)(2,1)S(1)} %get-tuple-element.45), channel_id=1, source_target_pairs={{0,12},{4,0},{8,4},{12,8},{1,13},{5,1},{9,5},{13,9},{2,14},{6,2},{... | collective-permute-start | bytes 208904 | tf_op jit(solution)/shard_map/ppermute | solution.py:743
  27.2 0.0 collective-permute-done.4.rest_2_
  27.2 0.5 collective-permute-start.5
  27.7 1.6 %collective-permute-start.9 = (bf16[128,768]{1,0:T(8,128)(2,1)S(1)}, bf16[128,768]{1,0:T(8,128)(2,1)S(1)}, u32[]{:S(2)}, u32[]{:S(2)}) collective-permute-start(bf16[128,768]{1,0:T(8,128)(2,1)S(1)} %pack.2.refs_0_.first_ref), channel_id=1, source_target_pairs={{0,2},{2,0},{1,3},{3,1},{4,6},{6,4},{5,7},{7,5},{8,10},{10,8},{9,1... | collective-permute-start | bytes 589832 | tf_op jit(solution)/shard_map/ppermute | solution.py:743
  29.2 0.9 %collective-permute-done.6.refs_2_ = s16[272,128]{1,0:T(8,128)(2,1)S(1)} collective-permute-done((s16[272,128]{1,0:T(8,128)(2,1)S(1)}, s16[272,128]{1,0:T(8,128)(2,1)S(1)}, u32[]{:S(2)}, u32[]{:S(2)}) %collective-permute-start.6) | collective-permute-done | bytes 69664 | tf_op jit(solution)/shard_map/ppermute | solution.py:743
  30.2 1.2 %collective-permute-done.7.refs_3_ = s16[272,128]{1,0:T(8,128)(2,1)S(1)} collective-permute-done((s16[272,128]{1,0:T(8,128)(2,1)S(1)}, s16[272,128]{1,0:T(8,128)(2,1)S(1)}, u32[]{:S(2)}, u32[]{:S(2)}) %collective-permute-start.7) | collective-permute-done | bytes 69664 | tf_op jit(solution)/shard_map/ppermute | solution.py:743
  31.3 0.0 collective-permute-done.8.refs_4_
  31.3 0.1 join_g_body.1.rest_1_
  31.4 0.6 collective-permute-done.5.rest_0_
  32.0 1.5 %collective-permute-start.10 = (bf16[128,512]{1,0:T(8,128)(2,1)S(1)}, bf16[128,512]{1,0:T(8,128)(2,1)S(1)}, u32[]{:S(2)}, u32[]{:S(2)}) collective-permute-start(bf16[128,512]{1,0:T(8,128)(2,1)S(1)} %pack.3.last_ref), channel_id=1, source_target_pairs={{0,2},{2,0},{1,3},{3,1},{4,6},{6,4},{5,7},{7,5},{8,10},{10,8},{9,1... | collective-permute-start | bytes 393224 | tf_op jit(solution)/shard_map/ppermute | solution.py:743
  33.5 0.1 collective-permute-start.11
  33.6 3.5 %collective-permute-done.10.last_ref = bf16[128,512]{1,0:T(8,128)(2,1)S(1)} collective-permute-done((bf16[128,512]{1,0:T(8,128)(2,1)S(1)}, bf16[128,512]{1,0:T(8,128)(2,1)S(1)}, u32[]{:S(2)}, u32[]{:S(2)}) %collective-permute-start.10) | collective-permute-done | bytes 131104 | tf_op jit(solution)/shard_map/ppermute | solution.py:743
  37.1 0.1 collective-permute-start.12
  37.2 0.1 stack.31.place_ref
  37.3 1.5 %collective-permute-done.12.rest_3_ = bf16[160,1024]{1,0:T(8,128)(2,1)S(1)} collective-permute-done((bf16[160,1024]{1,0:T(8,128)(2,1)S(1)}, bf16[160,1024]{1,0:T(8,128)(2,1)S(1)}, u32[]{:S(2)}, u32[]{:S(2)}) %collective-permute-start.12) | collective-permute-done | bytes 327712 | tf_op jit(solution)/shard_map/ppermute | solution.py:743
  38.8 5.6 %first_scores.1 = (s16[144,512]{1,0:T(8,128)(2,1)S(1)}, f32[8,128]{1,0:T(8,128)S(1)}, bf16[128,4096]{1,0:T(8,128)(2,1)S(1)}, bf16[2,512,4096]{2,1,0:T(8,128)(2,1)S(1)}) custom-call(s32[7]{0:T(128)S(1)} %stack.31.place_ref, s32[128]{0:T(128)S(1)} %sub.3.starts_ref, s32[128]{0:T(128)S(1)} %reduce.ends_ref, bf16[160,1024]{1,0:T(8,128)(2,1)S(1)} %token_block.2.rest_0_, ...), custom_call_target="tpu_custom_call" | custom-call | flops 2147483648 | bytes 8388608 | tf_op jit(solution)/shard_map/first_scores/pallas_call | solution.py:372
  44.4 1.0 %collective-permute-start.13 = (s16[144,512]{1,0:T(8,128)(2,1)S(1)}, s16[144,512]{1,0:T(8,128)(2,1)S(1)}, u32[]{:S(2)}, u32[]{:S(2)}) collective-permute-start(s16[144,512]{1,0:T(8,128)(2,1)S(1)} %get-tuple-element.50), channel_id=1, source_target_pairs={{0,4},{4,0},{8,12},{12,8},{1,5},{5,1},{9,13},{13,9},{2,6},{6,2},{1... | collective-permute-start | bytes 442376 | tf_op jit(solution)/shard_map/ppermute | solution.py:751
  45.4 2.9 %near_scores.1 = (f32[128,512]{1,0:T(8,128)S(1)}, s16[144,512]{1,0:T(8,128)(2,1)S(1)}) custom-call(bf16[128,4096]{1,0:T(8,128)(2,1)S(1)} %get-tuple-element.46.low_ref, f32[8,128]{1,0:T(8,128)S(1)} %get-tuple-element.47.sumsq_ref, bf16[2,512,4096]{2,1,0:T(8,128)(2,1)S(1)} %get-tuple-element.48.held_ref.rest_4_), custom_call_target="tpu_custom_call" | custom-call | flops 1073741824 | bytes 8388608 | tf_op jit(solution)/shard_map/near_scores/pallas_call | solution.py:409
  48.3 1.2 %collective-permute-start.14 = (s16[144,512]{1,0:T(8,128)(2,1)S(1)}, s16[144,512]{1,0:T(8,128)(2,1)S(1)}, u32[]{:S(2)}, u32[]{:S(2)}) collective-permute-start(s16[144,512]{1,0:T(8,128)(2,1)S(1)} %get-tuple-element.52), channel_id=1, source_target_pairs={{0,4},{4,0},{8,12},{12,8},{1,5},{5,1},{9,13},{13,9},{2,6},{6,2},{1... | collective-permute-start | bytes 442376 | tf_op jit(solution)/shard_map/ppermute | solution.py:751
  49.5 0.9 %collective-permute-done.13.message_ref = s16[144,512]{1,0:T(8,128)(2,1)S(1)} collective-permute-done((s16[144,512]{1,0:T(8,128)(2,1)S(1)}, s16[144,512]{1,0:T(8,128)(2,1)S(1)}, u32[]{:S(2)}, u32[]{:S(2)}) %collective-permute-start.13) | collective-permute-done | bytes 147488 | tf_op jit(solution)/shard_map/ppermute | solution.py:751
  50.4 0.3 add_scores.1.after_ref
  50.7 0.0 copy-start.1
  50.7 1.6 %collective-permute-start.15 = (s16[144,512]{1,0:T(8,128)(2,1)S(1)}, s16[144,512]{1,0:T(8,128)(2,1)S(1)}, u32[]{:S(2)}, u32[]{:S(2)}) collective-permute-start(s16[144,512]{1,0:T(8,128)(2,1)S(1)} %add_scores.1.after_ref), channel_id=1, source_target_pairs={{0,8},{4,12},{8,0},{12,4},{1,9},{5,13},{9,1},{13,5},{2,10},{6,14},... | collective-permute-start | bytes 442376 | tf_op jit(solution)/shard_map/ppermute | solution.py:743
  52.3 3.7 %own_scores.1 = (f32[128,512]{1,0:T(8,128)S(1)}, bf16[2,512,4096]{2,1,0:T(8,128)(2,1)S(1)}) custom-call(s32[1]{0:T(128)} %bitcast.me_ref, bf16[128,4096]{1,0:T(8,128)(2,1)S(1)} %get-tuple-element.46.low_ref, f32[8,128]{1,0:T(8,128)S(1)} %get-tuple-element.47.sumsq_ref, bf16[2048,4096]{1,0:T(8,128)(2,1)} %corpus_hbm.1, s16[144,512]{1,0:T(8,128)(2,1)S(1)} %add_scores.1.after_ref), custom_call_target="tpu_custom_call" | custom-call | flops 536870912 | bytes 8388608 | tf_op jit(solution)/shard_map/own_scores/pallas_call | solution.py:437
  56.1 3.9 %collective-permute-done.15.message_ref = s16[144,512]{1,0:T(8,128)(2,1)S(1)} collective-permute-done((s16[144,512]{1,0:T(8,128)(2,1)S(1)}, s16[144,512]{1,0:T(8,128)(2,1)S(1)}, u32[]{:S(2)}, u32[]{:S(2)}) %collective-permute-start.15) | collective-permute-done | bytes 147488 | tf_op jit(solution)/shard_map/ppermute | solution.py:743
  59.9 0.5 weights.1
  60.4 0.1 collective-permute-start.17
  60.5 3.1 %collective-permute-start.19 = (bf16[80,512]{1,0:T(8,128)(2,1)S(1)}, bf16[80,512]{1,0:T(8,128)(2,1)S(1)}, u32[]{:S(2)}, u32[]{:S(2)}) collective-permute-start(bf16[80,512]{1,0:T(8,128)(2,1)S(1)} %get-tuple-element.56.rest_0_), channel_id=1, source_target_pairs={{0,4},{4,0},{8,12},{12,8},{1,5},{5,1},{9,13},{13,9},{2,6},{6,2},{1... | collective-permute-start | bytes 245768 | tf_op jit(solution)/shard_map/ppermute | solution.py:751
  63.6 0.1 collective-permute-start.16
  63.7 1.8 %collective-permute-start.20 = (bf16[64,512]{1,0:T(8,128)(2,1)S(1)}, bf16[64,512]{1,0:T(8,128)(2,1)S(1)}, u32[]{:S(2)}, u32[]{:S(2)}) collective-permute-start(bf16[64,512]{1,0:T(8,128)(2,1)S(1)} %get-tuple-element.55.rest_1_), channel_id=1, source_target_pairs={{0,4},{4,0},{8,12},{12,8},{1,5},{5,1},{9,13},{13,9},{2,6},{6,2},{1... | collective-permute-start | bytes 196616 | tf_op jit(solution)/shard_map/ppermute | solution.py:751
  65.4 0.7 weighted_sums.2
  66.2 2.0 %collective-permute-done.17.piece_ref.rest_2_ = bf16[80,512]{1,0:T(8,128)(2,1)S(1)} collective-permute-done((bf16[80,512]{1,0:T(8,128)(2,1)S(1)}, bf16[80,512]{1,0:T(8,128)(2,1)S(1)}, u32[]{:S(2)}, u32[]{:S(2)}) %collective-permute-start.17) | collective-permute-done | bytes 81952 | tf_op jit(solution)/shard_map/ppermute | solution.py:743
  68.1 1.3 %collective-permute-done.16.piece_ref.rest_3_ = bf16[64,512]{1,0:T(8,128)(2,1)S(1)} collective-permute-done((bf16[64,512]{1,0:T(8,128)(2,1)S(1)}, bf16[64,512]{1,0:T(8,128)(2,1)S(1)}, u32[]{:S(2)}, u32[]{:S(2)}) %collective-permute-start.16) | collective-permute-done | bytes 65568 | tf_op jit(solution)/shard_map/ppermute | solution.py:743
  69.4 0.8 collective-permute-start.18
  70.2 0.1 collective-permute-done.20.rest_1_
  70.4 1.4 %weighted_sums.3 = (f32[128,4096]{1,0:T(8,128)S(1)}, f32[128,128]{1,0:T(8,128)S(1)}) custom-call(bf16[80,512]{1,0:T(8,128)(2,1)S(1)} %collective-permute-done.19.rest_0_, bf16[64,512]{1,0:T(8,128)(2,1)S(1)} %collective-permute-done.20.rest_1_, bf16[80,512]{1,0:T(8,128)(2,1)S(1)} %collective-permute-done.17.piece_ref.rest_2_, ...), custom_call_target="tpu_custom_call" | custom-call | flops 1073741824 | bytes 4194304 | tf_op jit(solution)/shard_map/weighted_sums/pallas_call | solution.py:609
  71.8 0.8 collective-permute-done.21.piece_ref
  72.6 1.4 %last_sums.2 = (bf16[2,16,4224]{2,1,0:T(8,128)(2,1)S(1)}, f32[2,16,4224]{2,1,0:T(8,128)S(1)}, f32[64,128]{1,0:T(8,128)S(1)}) custom-call(s32[7]{0:T(128)S(1)} %stack.31.place_ref, bf16[80,512]{1,0:T(8,128)(2,1)S(1)} %collective-permute-done.21.piece_ref, bf16[2,512,4096]{2,1,0:T(8,128)(2,1)S(1)} %get-tuple-element.57.rest_2_.held_ref, ...), custom_call_target="tpu_custom_call" | custom-call | tf_op jit(solution)/shard_map/last_sums/pallas_call | solution.py:662
  74.0 0.1 collective-permute-start.24
  74.1 1.4 %last_sums.3 = (bf16[2,16,4224]{2,1,0:T(8,128)(2,1)S(1)}, f32[2,16,4224]{2,1,0:T(8,128)S(1)}) custom-call(s32[7]{0:T(128)S(1)} %stack.31.place_ref, bf16[64,512]{1,0:T(8,128)(2,1)S(1)} %collective-permute-done.18.piece_ref, bf16[2,512,4096]{2,1,0:T(8,128)(2,1)S(1)} %get-tuple-element.57.rest_2_.held_ref, f32[128,4096]{1,0:T(8,128)S(1)} %get-tuple-element.60.old_ref, ...), custom_call_target="tpu_custom_call" | custom-call | tf_op jit(solution)/shard_map/last_sums/pallas_call | solution.py:662
  75.5 0.6 collective-permute-start.22
  76.1 0.7 merge_core.3
  76.8 1.1 %collective-permute-start.25 = (bf16[16,4224]{1,0:T(8,128)(2,1)S(1)}, bf16[16,4224]{1,0:T(8,128)(2,1)S(1)}, u32[]{:S(2)}, u32[]{:S(2)}) collective-permute-start(bf16[16,4224]{1,0:T(8,128)(2,1)S(1)} %get-tuple-element.70), channel_id=1, source_target_pairs={{0,2},{2,0},{1,3},{3,1},{4,6},{6,4},{5,7},{7,5},{8,10},{10,8},{9,1... | collective-permute-start | bytes 405512 | tf_op jit(solution)/shard_map/ppermute | solution.py:743
  77.9 0.7 merge_core.2
  78.7 1.0 %collective-permute-start.23 = (bf16[16,4224]{1,0:T(8,128)(2,1)S(1)}, bf16[16,4224]{1,0:T(8,128)(2,1)S(1)}, u32[]{:S(2)}, u32[]{:S(2)}) collective-permute-start(bf16[16,4224]{1,0:T(8,128)(2,1)S(1)} %get-tuple-element.66), channel_id=1, source_target_pairs={{0,2},{2,0},{1,3},{3,1},{4,6},{6,4},{5,7},{7,5},{8,10},{10,8},{9,1... | collective-permute-start | bytes 405512 | tf_op jit(solution)/shard_map/ppermute | solution.py:743
  79.7 3.6 %collective-permute-done.25.other_ref = bf16[16,4224]{1,0:T(8,128)(2,1)S(1)} collective-permute-done((bf16[16,4224]{1,0:T(8,128)(2,1)S(1)}, bf16[16,4224]{1,0:T(8,128)(2,1)S(1)}, u32[]{:S(2)}, u32[]{:S(2)}) %collective-permute-start.25) | collective-permute-done | bytes 135200 | tf_op jit(solution)/shard_map/ppermute | solution.py:743
  83.3 0.1 merge_last.2.rest_0_
  83.5 1.8 %collective-permute-done.23.other_ref = bf16[16,4224]{1,0:T(8,128)(2,1)S(1)} collective-permute-done((bf16[16,4224]{1,0:T(8,128)(2,1)S(1)}, bf16[16,4224]{1,0:T(8,128)(2,1)S(1)}, u32[]{:S(2)}, u32[]{:S(2)}) %collective-permute-start.23) | collective-permute-done | bytes 135200 | tf_op jit(solution)/shard_map/ppermute | solution.py:743
  85.3 0.9 %merge_last.3 = f32[32,4096]{1,0:T(8,128)} custom-call(f32[16,4224]{1,0:T(8,128)S(1)} %get-tuple-element.65.keep_ref, bf16[16,4224]{1,0:T(8,128)(2,1)S(1)} %collective-permute-done.23.other_ref, f32[16,4096]{1,0:T(8,128)S(1)} %merge_last.2.rest_0_), custom_call_target="tpu_custom_call" | custom-call | tf_op jit(solution)/shard_map/merge_last/pallas_call | solution.py:731
  (23 shorter events, 0.2 us)
Async XLA Ops:
  0.0 15.5 %copy-start.2 = (s32[128]{0:T(128)S(1)}, s32[128]{0:T(128)}, u32[]{:S(2)}) copy-start(s32[128]{0:T(128)} %param.11) | copy-start | bytes 1540
  0.0 15.9 %copy-start = (bf16[2048,128]{1,0:T(8,128)(2,1)S(1)}, bf16[2048,128]{1,0:T(8,128)(2,1)}, u32[]{:S(2)}) copy-start(bf16[2048,128]{1,0:T(8,128)(2,1)} %proj_hbm.2) | copy-start | bytes 1572868
  8.5 10.8 %collective-permute-start = (s16[144,256]{1,0:T(8,128)(2,1)S(1)}, s16[144,256]{1,0:T(8,128)(2,1)S(1)}, u32[]{:S(2)}, u32[]{:S(2)}) collective-permute-start(s16[144,256]{1,0:T(8,128)(2,1)S(1)} %get-tuple-element.40), channel_id=1, source_target_pairs={{0,4},{4,8},{8,12},{12,0},{1,5},{5,9},{9,13},{13,1},{2,6},{6,10},{... | collective-permute-start | bytes 221192 | tf_op jit(solution)/shard_map/ppermute | solution.py:743
  11.6 7.8 %collective-permute-start.1 = (s16[144,256]{1,0:T(8,128)(2,1)S(1)}, s16[144,256]{1,0:T(8,128)(2,1)S(1)}, u32[]{:S(2)}, u32[]{:S(2)}) collective-permute-start(s16[144,256]{1,0:T(8,128)(2,1)S(1)} %get-tuple-element.41), channel_id=1, source_target_pairs={{0,8},{4,12},{8,0},{12,4},{1,9},{5,13},{9,1},{13,5},{2,10},{6,14},... | collective-permute-start | bytes 221192 | tf_op jit(solution)/shard_map/ppermute | solution.py:743
  14.2 5.2 %collective-permute-start.2 = (s16[144,256]{1,0:T(8,128)(2,1)S(1)}, s16[144,256]{1,0:T(8,128)(2,1)S(1)}, u32[]{:S(2)}, u32[]{:S(2)}) collective-permute-start(s16[144,256]{1,0:T(8,128)(2,1)S(1)} %get-tuple-element.42), channel_id=1, source_target_pairs={{0,12},{4,0},{8,4},{12,8},{1,13},{5,1},{9,5},{13,9},{2,14},{6,2},{... | collective-permute-start | bytes 221192 | tf_op jit(solution)/shard_map/ppermute | solution.py:743
  19.4 7.7 %collective-permute-start.4 = (bf16[128,256]{1,0:T(8,128)(2,1)S(1)}, bf16[128,256]{1,0:T(8,128)(2,1)S(1)}, u32[]{:S(2)}, u32[]{:S(2)}) collective-permute-start(bf16[128,256]{1,0:T(8,128)(2,1)S(1)} %join_x_body.1.rest_0_), channel_id=1, source_target_pairs={{0,8},{4,12},{8,0},{12,4},{1,9},{5,13},{9,1},{13,5},{2,10},{6,14},... | collective-permute-start | bytes 196616 | tf_op jit(solution)/shard_map/ppermute | solution.py:743
  21.0 6.6 %collective-permute-start.3 = (bf16[128,256]{1,0:T(8,128)(2,1)S(1)}, bf16[128,256]{1,0:T(8,128)(2,1)S(1)}, u32[]{:S(2)}, u32[]{:S(2)}) collective-permute-start(bf16[128,256]{1,0:T(8,128)(2,1)S(1)} %join_x_body.1.rest_0_), channel_id=1, source_target_pairs={{0,4},{4,0},{8,12},{12,8},{1,5},{5,1},{9,13},{13,9},{2,6},{6,2},{1... | collective-permute-start | bytes 196616 | tf_op jit(solution)/shard_map/ppermute | solution.py:751
  23.3 6.9 %collective-permute-start.6 = (s16[272,128]{1,0:T(8,128)(2,1)S(1)}, s16[272,128]{1,0:T(8,128)(2,1)S(1)}, u32[]{:S(2)}, u32[]{:S(2)}) collective-permute-start(s16[272,128]{1,0:T(8,128)(2,1)S(1)} %get-tuple-element.43), channel_id=1, source_target_pairs={{0,4},{4,8},{8,12},{12,0},{1,5},{5,9},{9,13},{13,1},{2,6},{6,10},{... | collective-permute-start | bytes 208904 | tf_op jit(solution)/shard_map/ppermute | solution.py:743
  23.3 8.0 %collective-permute-start.7 = (s16[272,128]{1,0:T(8,128)(2,1)S(1)}, s16[272,128]{1,0:T(8,128)(2,1)S(1)}, u32[]{:S(2)}, u32[]{:S(2)}) collective-permute-start(s16[272,128]{1,0:T(8,128)(2,1)S(1)} %get-tuple-element.44), channel_id=1, source_target_pairs={{0,8},{4,12},{8,0},{12,4},{1,9},{5,13},{9,1},{13,5},{2,10},{6,14},... | collective-permute-start | bytes 208904 | tf_op jit(solution)/shard_map/ppermute | solution.py:743
  24.5 6.9 %collective-permute-start.8 = (s16[272,128]{1,0:T(8,128)(2,1)S(1)}, s16[272,128]{1,0:T(8,128)(2,1)S(1)}, u32[]{:S(2)}, u32[]{:S(2)}) collective-permute-start(s16[272,128]{1,0:T(8,128)(2,1)S(1)} %get-tuple-element.45), channel_id=1, source_target_pairs={{0,12},{4,0},{8,4},{12,8},{1,13},{5,1},{9,5},{13,9},{2,14},{6,2},{... | collective-permute-start | bytes 208904 | tf_op jit(solution)/shard_map/ppermute | solution.py:743
  27.2 4.8 %collective-permute-start.5 = (bf16[128,256]{1,0:T(8,128)(2,1)S(1)}, bf16[128,256]{1,0:T(8,128)(2,1)S(1)}, u32[]{:S(2)}, u32[]{:S(2)}) collective-permute-start(bf16[128,256]{1,0:T(8,128)(2,1)S(1)} %collective-permute-done.4.rest_2_), channel_id=1, source_target_pairs={{0,4},{4,0},{8,12},{12,8},{1,5},{5,1},{9,13},{13,9},{2,6},{6,2},{1... | collective-permute-start | bytes 196616 | tf_op jit(solution)/shard_map/ppermute | solution.py:751
  27.7 9.4 %collective-permute-start.9 = (bf16[128,768]{1,0:T(8,128)(2,1)S(1)}, bf16[128,768]{1,0:T(8,128)(2,1)S(1)}, u32[]{:S(2)}, u32[]{:S(2)}) collective-permute-start(bf16[128,768]{1,0:T(8,128)(2,1)S(1)} %pack.2.refs_0_.first_ref), channel_id=1, source_target_pairs={{0,2},{2,0},{1,3},{3,1},{4,6},{6,4},{5,7},{7,5},{8,10},{10,8},{9,1... | collective-permute-start | bytes 589832 | tf_op jit(solution)/shard_map/ppermute | solution.py:743
  32.0 5.0 %collective-permute-start.10 = (bf16[128,512]{1,0:T(8,128)(2,1)S(1)}, bf16[128,512]{1,0:T(8,128)(2,1)S(1)}, u32[]{:S(2)}, u32[]{:S(2)}) collective-permute-start(bf16[128,512]{1,0:T(8,128)(2,1)S(1)} %pack.3.last_ref), channel_id=1, source_target_pairs={{0,2},{2,0},{1,3},{3,1},{4,6},{6,4},{5,7},{7,5},{8,10},{10,8},{9,1... | collective-permute-start | bytes 393224 | tf_op jit(solution)/shard_map/ppermute | solution.py:743
  33.5 3.8 %collective-permute-start.11 = (bf16[160,1024]{1,0:T(8,128)(2,1)S(1)}, bf16[160,1024]{1,0:T(8,128)(2,1)S(1)}, u32[]{:S(2)}, u32[]{:S(2)}) collective-permute-start(bf16[160,1024]{1,0:T(8,128)(2,1)S(1)} %token_block.2.rest_0_), channel_id=1, source_target_pairs={{0,1},{1,0},{2,3},{3,2},{4,5},{5,4},{6,7},{7,6},{8,9},{9,8},{10,11... | collective-permute-start | bytes 983048 | tf_op jit(solution)/shard_map/ppermute | solution.py:743
  37.1 1.7 %collective-permute-start.12 = (bf16[160,1024]{1,0:T(8,128)(2,1)S(1)}, bf16[160,1024]{1,0:T(8,128)(2,1)S(1)}, u32[]{:S(2)}, u32[]{:S(2)}) collective-permute-start(bf16[160,1024]{1,0:T(8,128)(2,1)S(1)} %token_block.3.rest_1_), channel_id=1, source_target_pairs={{0,1},{1,0},{2,3},{3,2},{4,5},{5,4},{6,7},{7,6},{8,9},{9,8},{10,11... | collective-permute-start | bytes 983048 | tf_op jit(solution)/shard_map/ppermute | solution.py:743
  44.4 6.0 %collective-permute-start.13 = (s16[144,512]{1,0:T(8,128)(2,1)S(1)}, s16[144,512]{1,0:T(8,128)(2,1)S(1)}, u32[]{:S(2)}, u32[]{:S(2)}) collective-permute-start(s16[144,512]{1,0:T(8,128)(2,1)S(1)} %get-tuple-element.50), channel_id=1, source_target_pairs={{0,4},{4,0},{8,12},{12,8},{1,5},{5,1},{9,13},{13,9},{2,6},{6,2},{1... | collective-permute-start | bytes 442376 | tf_op jit(solution)/shard_map/ppermute | solution.py:751
  48.3 7.7 %collective-permute-start.14 = (s16[144,512]{1,0:T(8,128)(2,1)S(1)}, s16[144,512]{1,0:T(8,128)(2,1)S(1)}, u32[]{:S(2)}, u32[]{:S(2)}) collective-permute-start(s16[144,512]{1,0:T(8,128)(2,1)S(1)} %get-tuple-element.52), channel_id=1, source_target_pairs={{0,4},{4,0},{8,12},{12,8},{1,5},{5,1},{9,13},{13,9},{2,6},{6,2},{1... | collective-permute-start | bytes 442376 | tf_op jit(solution)/shard_map/ppermute | solution.py:751
  50.7 9.2 %copy-start.1 = (s32[2048]{0:T(1024)S(1)}, s32[2048]{0:T(1024)}, u32[]{:S(2)}) copy-start(s32[2048]{0:T(1024)} %param.13) | copy-start | bytes 24580
  50.7 9.2 %collective-permute-start.15 = (s16[144,512]{1,0:T(8,128)(2,1)S(1)}, s16[144,512]{1,0:T(8,128)(2,1)S(1)}, u32[]{:S(2)}, u32[]{:S(2)}) collective-permute-start(s16[144,512]{1,0:T(8,128)(2,1)S(1)} %add_scores.1.after_ref), channel_id=1, source_target_pairs={{0,8},{4,12},{8,0},{12,4},{1,9},{5,13},{9,1},{13,5},{2,10},{6,14},... | collective-permute-start | bytes 442376 | tf_op jit(solution)/shard_map/ppermute | solution.py:743
  60.4 7.7 %collective-permute-start.17 = (bf16[80,512]{1,0:T(8,128)(2,1)S(1)}, bf16[80,512]{1,0:T(8,128)(2,1)S(1)}, u32[]{:S(2)}, u32[]{:S(2)}) collective-permute-start(bf16[80,512]{1,0:T(8,128)(2,1)S(1)} %get-tuple-element.56.rest_0_), channel_id=1, source_target_pairs={{0,8},{4,12},{8,0},{12,4},{1,9},{5,13},{9,1},{13,5},{2,10},{6,14},... | collective-permute-start | bytes 245768 | tf_op jit(solution)/shard_map/ppermute | solution.py:743
  60.5 9.9 %collective-permute-start.19 = (bf16[80,512]{1,0:T(8,128)(2,1)S(1)}, bf16[80,512]{1,0:T(8,128)(2,1)S(1)}, u32[]{:S(2)}, u32[]{:S(2)}) collective-permute-start(bf16[80,512]{1,0:T(8,128)(2,1)S(1)} %get-tuple-element.56.rest_0_), channel_id=1, source_target_pairs={{0,4},{4,0},{8,12},{12,8},{1,5},{5,1},{9,13},{13,9},{2,6},{6,2},{1... | collective-permute-start | bytes 245768 | tf_op jit(solution)/shard_map/ppermute | solution.py:751
  63.6 5.8 %collective-permute-start.16 = (bf16[64,512]{1,0:T(8,128)(2,1)S(1)}, bf16[64,512]{1,0:T(8,128)(2,1)S(1)}, u32[]{:S(2)}, u32[]{:S(2)}) collective-permute-start(bf16[64,512]{1,0:T(8,128)(2,1)S(1)} %get-tuple-element.55.rest_1_), channel_id=1, source_target_pairs={{0,8},{4,12},{8,0},{12,4},{1,9},{5,13},{9,1},{13,5},{2,10},{6,14},... | collective-permute-start | bytes 196616 | tf_op jit(solution)/shard_map/ppermute | solution.py:743
  63.7 6.7 %collective-permute-start.20 = (bf16[64,512]{1,0:T(8,128)(2,1)S(1)}, bf16[64,512]{1,0:T(8,128)(2,1)S(1)}, u32[]{:S(2)}, u32[]{:S(2)}) collective-permute-start(bf16[64,512]{1,0:T(8,128)(2,1)S(1)} %get-tuple-element.55.rest_1_), channel_id=1, source_target_pairs={{0,4},{4,0},{8,12},{12,8},{1,5},{5,1},{9,13},{13,9},{2,6},{6,2},{1... | collective-permute-start | bytes 196616 | tf_op jit(solution)/shard_map/ppermute | solution.py:751
  68.1 4.4 %collective-permute-start.21 = (bf16[80,512]{1,0:T(8,128)(2,1)S(1)}, bf16[80,512]{1,0:T(8,128)(2,1)S(1)}, u32[]{:S(2)}, u32[]{:S(2)}) collective-permute-start(bf16[80,512]{1,0:T(8,128)(2,1)S(1)} %relay.2.rest_0_), channel_id=1, source_target_pairs={{0,4},{4,0},{8,12},{12,8},{1,5},{5,1},{9,13},{13,9},{2,6},{6,2},{1... | collective-permute-start | bytes 245768 | tf_op jit(solution)/shard_map/ppermute | solution.py:751
  69.4 4.7 %collective-permute-start.18 = (bf16[64,512]{1,0:T(8,128)(2,1)S(1)}, bf16[64,512]{1,0:T(8,128)(2,1)S(1)}, u32[]{:S(2)}, u32[]{:S(2)}) collective-permute-start(bf16[64,512]{1,0:T(8,128)(2,1)S(1)} %relay.3.rest_7_), channel_id=1, source_target_pairs={{0,4},{4,0},{8,12},{12,8},{1,5},{5,1},{9,13},{13,9},{2,6},{6,2},{1... | collective-permute-start | bytes 196616 | tf_op jit(solution)/shard_map/ppermute | solution.py:751
  74.0 2.1 %collective-permute-start.24 = (bf16[2,16,4224]{2,1,0:T(8,128)(2,1)S(1)}, bf16[2,16,4224]{2,1,0:T(8,128)(2,1)S(1)}, u32[]{:S(2)}, u32[]{:S(2)}) collective-permute-start(bf16[2,16,4224]{2,1,0:T(8,128)(2,1)S(1)} %get-tuple-element.68), channel_id=1, source_target_pairs={{0,1},{1,0},{2,3},{3,2},{4,5},{5,4},{6,7},{7,6},{8,9},{9,8},{10,11... | collective-permute-start | bytes 811016 | tf_op jit(solution)/shard_map/ppermute | solution.py:743
  75.5 2.4 %collective-permute-start.22 = (bf16[2,16,4224]{2,1,0:T(8,128)(2,1)S(1)}, bf16[2,16,4224]{2,1,0:T(8,128)(2,1)S(1)}, u32[]{:S(2)}, u32[]{:S(2)}) collective-permute-start(bf16[2,16,4224]{2,1,0:T(8,128)(2,1)S(1)} %get-tuple-element.64), channel_id=1, source_target_pairs={{0,1},{1,0},{2,3},{3,2},{4,5},{5,4},{6,7},{7,6},{8,9},{9,8},{10,11... | collective-permute-start | bytes 811016 | tf_op jit(solution)/shard_map/ppermute | solution.py:743
  76.8 6.5 %collective-permute-start.25 = (bf16[16,4224]{1,0:T(8,128)(2,1)S(1)}, bf16[16,4224]{1,0:T(8,128)(2,1)S(1)}, u32[]{:S(2)}, u32[]{:S(2)}) collective-permute-start(bf16[16,4224]{1,0:T(8,128)(2,1)S(1)} %get-tuple-element.70), channel_id=1, source_target_pairs={{0,2},{2,0},{1,3},{3,1},{4,6},{6,4},{5,7},{7,5},{8,10},{10,8},{9,1... | collective-permute-start | bytes 405512 | tf_op jit(solution)/shard_map/ppermute | solution.py:743
  78.7 6.6 %collective-permute-start.23 = (bf16[16,4224]{1,0:T(8,128)(2,1)S(1)}, bf16[16,4224]{1,0:T(8,128)(2,1)S(1)}, u32[]{:S(2)}, u32[]{:S(2)}) collective-permute-start(bf16[16,4224]{1,0:T(8,128)(2,1)S(1)} %get-tuple-element.66), channel_id=1, source_target_pairs={{0,2},{2,0},{1,3},{3,1},{4,6},{6,4},{5,7},{7,5},{8,10},{10,8},{9,1... | collective-permute-start | bytes 405512 | tf_op jit(solution)/shard_map/ppermute | solution.py:743
